TPU v7x, 32 devices: a whole 2x2x4 slice. The times are simulated.
32 devices in a mesh: ctx: 16 (over z, y, core), fsdp: 2 (over x).
Axes of the slice: x: 2, y: 2, z: 4, core: 2. Of those that a mesh axis runs over, the one named last changes fastest.
Arguments:
- tokens: bfloat16 [2, 2048, 768], P('fsdp', 'ctx'), may hold values from -6 to 6
- prev_logits: float32 [2, 2048, 12], P('fsdp', 'ctx'), may hold values from -3 to 3
- routes: int32 [2, 2048, 2], P('fsdp', 'ctx'), may hold values from 0 to 11, all different within a row
- order: int32 [2, 4096], P('fsdp', 'ctx'), may hold values from 0 to 255, as said below
- deal: int32 [32], replicated, may hold values from 0 to 31, each once
- w_qkv: bfloat16 [2, 768, 2304], P(None, ('ctx', 'fsdp')), may hold values from -0.21875 to 0.21875
- w_out: bfloat16 [2, 768, 768], P(None, ('ctx', 'fsdp')), may hold values from -0.625 to 0.625
- w_gate: bfloat16 [2, 8, 768, 2048], P(None, None, ('ctx', 'fsdp')), may hold values from -0.21875 to 0.21875
- w_up: bfloat16 [2, 8, 768, 2048], P(None, None, ('ctx', 'fsdp')), may hold values from -0.21875 to 0.21875
- w_down: bfloat16 [2, 8, 2048, 768], P(None, None, ('ctx', 'fsdp')), may hold values from -0.25 to 0.25
- norm_attn: bfloat16 [2, 768], P(None, ('ctx', 'fsdp')), may hold values from 0.5 to 1.5
- norm_moe: bfloat16 [2, 768], P(None, ('ctx', 'fsdp')), may hold values from 0.5 to 1.5
- w_router: bfloat16 [2, 768, 12], P(None, ('ctx', 'fsdp')), may hold values from -0.125 to 0.125
- w_const: bfloat16 [2, 768, 4], P(None, ('ctx', 'fsdp')), may hold values from -0.21875 to 0.21875
- const_vec: bfloat16 [2, 768, 2], P(None, ('ctx', 'fsdp')), may hold values from -5 to 5
- grad_out: bfloat16 [2, 2048, 768], P('fsdp', 'ctx'), may hold values from -6 to 6
Outputs:
- output_rows: bfloat16 [2, 2048, 768], P('fsdp', 'ctx')
- input_grad: float32 [2, 2048, 768], P('fsdp', 'ctx')
- qkv_grad: float32 [2, 768, 2304], P(None, ('ctx', 'fsdp'))
- out_grad: float32 [2, 768, 768], P(None, ('ctx', 'fsdp'))
- gate_grad: float32 [2, 8, 768, 2048], P(None, None, ('ctx', 'fsdp'))
- up_grad: float32 [2, 8, 768, 2048], P(None, None, ('ctx', 'fsdp'))
- down_grad: float32 [2, 8, 2048, 768], P(None, None, ('ctx', 'fsdp'))
- norm_attn_grad: float32 [2, 768], P(None, ('ctx', 'fsdp'))
- norm_moe_grad: float32 [2, 768], P(None, ('ctx', 'fsdp'))
- router_grad: float32 [2, 768, 12], P(None, ('ctx', 'fsdp'))
- const_gate_grad: float32 [2, 768, 4], P(None, ('ctx', 'fsdp'))
- const_vec_grad: float32 [2, 768, 2], P(None, ('ctx', 'fsdp'))
Inputs may be any that keep to these rules, and one draw needn't show every extreme that they name: Each token names 2 different routes: 0 to 7 feed-forward experts, 8 the zero expert, 9 the copy expert, 10 and 11 the constant experts. `order`: each aligned block of 256 entries (one device's pairs) is a permutation of 0 to 255. `deal`: a permutation, the same for every group.
All inputs are finite; a program needn't handle non-finite values.
Results may differ from a plain program's by a relative error of at most 0.023.
Values may be sent and summed in bfloat16 or wider, within the bound.
No kernel may reach another device: no remote copies, remote signals or barrier semaphores. Data moves between devices by JAX's collectives and lax.ppermute only.
A program may use at most 576 MiB of HBM per device.

v0:
```python
import jax
import jax.numpy as jnp
from jax import lax
from jax.sharding import PartitionSpec as P

HEADS = 12
HEAD_DIM = 64
EXPERTS = 8
TOP = 2
LAYERS = 2
ROUTED = 12
CAP = 26


norm_eps = 1e-06
masked_score = -1e30
highest = lax.Precision.HIGHEST


def rms_rows(values, gain):
    scale = lax.rsqrt(jnp.mean(values * values, axis=-1, keepdims=True) + norm_eps)
    return values * scale * gain


def rotate(heads_in, cosine_table, sine_table):
    half_dim = heads_in.shape[-1] // 2
    former = heads_in[..., :half_dim]
    latter = heads_in[..., half_dim:]
    return jnp.concatenate(
        [former * cosine_table - latter * sine_table, latter * cosine_table + former * sine_table],
        axis=-1,
    )


def place_rows(rows, deal, block_rows):
    owners = rows // block_rows
    numbers = jnp.arange(deal.shape[0], dtype=jnp.int32)
    looked = jnp.sum(
        jnp.where(owners[:, None] == numbers[None, :], deal[None, :], 0), axis=1, dtype=jnp.int32
    )
    return looked * block_rows + rows % block_rows


def visible(query_places, key_places, prompt, cont_len):
    query_segment = jnp.where(query_places >= prompt, (query_places - prompt) // cont_len, -1)
    key_segment = jnp.where(key_places >= prompt, (key_places - prompt) // cont_len, -1)
    earlier = key_places[None, :] <= query_places[:, None]
    shared = (key_places[None, :] < prompt) | (key_segment[None, :] == query_segment[:, None])
    return earlier & shared


def keep_pairs(route_rows, rank_rows):
    flat_routes = route_rows.reshape(-1)
    onehot = (flat_routes[:, None] == jnp.arange(EXPERTS, dtype=jnp.int32)[None, :]).astype(
        jnp.int32
    )
    ranked = jnp.zeros_like(onehot).at[rank_rows].set(onehot)
    before = jnp.cumsum(ranked, axis=0, dtype=jnp.int32) - ranked
    slot_rank = jnp.sum(before[rank_rows] * onehot, axis=1, dtype=jnp.int32)
    return (slot_rank, (flat_routes >= EXPERTS) | (slot_rank < CAP))


def block_scan(block_fn, running, arrays):
    row_count = arrays[0].shape[0]
    span = row_count
    while span > 512 and span % 2 == 0:
        span //= 2
    block_count = row_count // span
    stacked = tuple((member.reshape((block_count, span) + member.shape[1:]) for member in arrays))

    def advance(carried, inputs):
        return (block_fn(carried, inputs[1:], inputs[0] * span), None)

    result, _ = lax.scan(advance, running, (jnp.arange(block_count, dtype=jnp.int32),) + stacked)
    return result


def side_experts(mixed_rows, mixing, cvec, route_rows):
    total = (route_rows == EXPERTS + 1).astype(jnp.float32)[..., None] * mixed_rows[:, None, :]
    for number in range(2):
        const_out = (
            mixing[:, number, 0:1] * mixed_rows + mixing[:, number, 1:2] * cvec[:, number][None, :]
        )
        total = (
            total
            + (route_rows == EXPERTS + 2 + number).astype(jnp.float32)[..., None]
            * const_out[:, None, :]
        )
    return total


def mix_gates(const_logits):
    return jax.nn.softmax(const_logits.reshape(const_logits.shape[0], 2, 2), axis=-1)


def softmax_last(logits):
    return jax.nn.softmax(logits, axis=-1)


def shards(
    tokens,
    prev_logits,
    routes,
    order,
    deal,
    w_qkv,
    w_out,
    w_gate,
    w_up,
    w_down,
    norm_attn,
    norm_moe,
    w_router,
    w_const,
    const_vec,
    grad_out,
):
    tok_rows = tokens.shape[1]
    model_width = tokens.shape[2]
    group_len = tok_rows * lax.axis_size("ctx")
    prompt = group_len // 2
    cont_len = prompt // (lax.axis_size("ctx") // 8)
    block_rows = tok_rows // 2
    scale = HEAD_DIM ** (-0.5)
    first_row = lax.axis_index("ctx") * tok_rows
    own_places = place_rows(first_row + jnp.arange(tok_rows, dtype=jnp.int32), deal, block_rows)
    within = jnp.where(own_places < prompt, own_places, prompt + (own_places - prompt) % cont_len)
    frequency = 10000.0 ** (-jnp.arange(HEAD_DIM // 2, dtype=jnp.float32) / (HEAD_DIM // 2))
    angles = within.astype(jnp.float32)[:, None] * frequency[None, :]
    cosine_table = jnp.cos(angles)[:, None, :]
    sine_table = jnp.sin(angles)[:, None, :]
    route_rows = routes[0]
    slot_rank, retained = keep_pairs(route_rows, order[0])
    route_flat = route_rows.reshape(-1)
    to_slot = route_flat * CAP + slot_rank
    in_slot = (route_flat < EXPERTS) & retained
    slot_index = jnp.where(in_slot, to_slot, EXPERTS * CAP)
    pair_ids = jnp.arange(tok_rows * TOP, dtype=jnp.int32)
    slot_pair = (
        jnp.full((EXPERTS * CAP,), tok_rows * TOP, jnp.int32)
        .at[slot_index]
        .set(pair_ids, mode="drop")
    )
    slot_token = slot_pair // TOP
    route_onehot = (route_rows[..., None] == jnp.arange(ROUTED, dtype=jnp.int32)).astype(
        jnp.float32
    )

    def turn(heads_in):
        return rotate(heads_in, cosine_table, sine_table)

    def fetch(layer_at):
        return (
            lax.all_gather(w_qkv[layer_at], ("ctx", "fsdp"), axis=0, tiled=True),
            lax.all_gather(w_out[layer_at], ("ctx", "fsdp"), axis=0, tiled=True),
            lax.all_gather(w_gate[layer_at], ("ctx", "fsdp"), axis=1, tiled=True),
            lax.all_gather(w_up[layer_at], ("ctx", "fsdp"), axis=1, tiled=True),
            lax.all_gather(w_down[layer_at], ("ctx", "fsdp"), axis=1, tiled=True),
            lax.all_gather(norm_attn[layer_at], ("ctx", "fsdp"), axis=0, tiled=True),
            lax.all_gather(norm_moe[layer_at], ("ctx", "fsdp"), axis=0, tiled=True),
            lax.all_gather(w_router[layer_at], ("ctx", "fsdp"), axis=0, tiled=True),
            lax.all_gather(w_const[layer_at], ("ctx", "fsdp"), axis=0, tiled=True),
            lax.all_gather(const_vec[layer_at], ("ctx", "fsdp"), axis=0, tiled=True),
        )

    def layer_back(grad_next, logit_next, saved, weights_now):
        (
            hidden,
            normed_low,
            query_heads,
            key_rows,
            value_rows,
            attended,
            log_total,
            att_low,
            midway,
            mixed_rows,
            mixed_low,
            logits,
            const_logits,
            mixing,
            slot_in,
            gate_act,
            upward,
            hidden_act,
            ffn_pairs,
            side_terms,
            picked,
        ) = saved
        wqkv, wout, wgate, wup, wdown, gain_attn, gain_moe, wrouter, wconst, cvec = weights_now
        pair_grad = picked[..., None] * grad_next[:, None, :]
        picked_grad = jnp.sum(grad_next[:, None, :] * (ffn_pairs + side_terms), axis=-1)
        flat_grad = jnp.concatenate(
            [
                pair_grad.reshape(tok_rows * TOP, model_width),
                jnp.zeros((1, model_width), jnp.float32),
            ],
            axis=0,
        )
        slot_grad_out = (
            jnp.take(flat_grad, slot_pair, axis=0)
            .astype(jnp.bfloat16)
            .reshape(EXPERTS, CAP, model_width)
        )
        inner_grad = jnp.einsum(
            "ecd,efd->ecf", slot_grad_out, wdown, preferred_element_type=jnp.float32
        )
        down_grad = jnp.einsum(
            "ecf,ecd->efd", hidden_act, slot_grad_out, preferred_element_type=jnp.float32
        )

        def swiglu(gate_in, up_in):
            return jax.nn.silu(gate_in) * up_in

        _, swiglu_back = jax.vjp(swiglu, gate_act, upward)
        gate_grad, up_grad = swiglu_back(inner_grad)
        gate_low = gate_grad.astype(jnp.bfloat16)
        up_low = up_grad.astype(jnp.bfloat16)
        slot_grad_in = jnp.einsum(
            "ecf,edf->ecd", gate_low, wgate, preferred_element_type=jnp.float32
        ) + jnp.einsum("ecf,edf->ecd", up_low, wup, preferred_element_type=jnp.float32)
        gate_w_grad = jnp.einsum(
            "ecd,ecf->edf", slot_in, gate_low, preferred_element_type=jnp.float32
        )
        up_w_grad = jnp.einsum("ecd,ecf->edf", slot_in, up_low, preferred_element_type=jnp.float32)
        low_grad = (
            jnp.zeros((tok_rows + 1, model_width), jnp.float32)
            .at[slot_token]
            .add(slot_grad_in.reshape(EXPERTS * CAP, model_width))[:tok_rows]
        )

        def side_only(mixed_in, mixing_in, cvec_in):
            return side_experts(mixed_in, mixing_in, cvec_in, route_rows)

        _, side_back = jax.vjp(side_only, mixed_rows, mixing, cvec.astype(jnp.float32))
        mixed_grad, mixing_grad, cvec_grad = side_back(pair_grad)
        chance_grad = jnp.sum(route_onehot * picked_grad[..., None], axis=1)
        _, soft_back = jax.vjp(softmax_last, logits)
        logit_grad = soft_back(chance_grad)[0] + logit_next
        _, mix_back = jax.vjp(mix_gates, const_logits)
        const_logit_grad = mix_back(mixing_grad)[0]
        router_f = wrouter.astype(jnp.float32)
        const_f = wconst.astype(jnp.float32)
        mixed_f = mixed_low.astype(jnp.float32)
        low_grad = (
            low_grad
            + jnp.dot(logit_grad, router_f.T, precision=highest)
            + jnp.dot(const_logit_grad, const_f.T, precision=highest)
        )
        router_grad = jnp.dot(mixed_f.T, logit_grad, precision=highest)
        const_grad = jnp.dot(mixed_f.T, const_logit_grad, precision=highest)
        _, norm_back_moe = jax.vjp(rms_rows, midway, gain_moe.astype(jnp.float32))
        mid_part, gain_moe_grad = norm_back_moe(mixed_grad + low_grad)
        mid_grad = grad_next + mid_part
        mid_low = mid_grad.astype(jnp.bfloat16)
        att_grad = jnp.einsum("tj,dj->td", mid_low, wout, preferred_element_type=jnp.float32)
        out_w_grad = jnp.einsum("td,tj->dj", att_low, mid_low, preferred_element_type=jnp.float32)
        att_grad_low = att_grad.astype(jnp.bfloat16)
        grad_heads = att_grad_low.reshape(tok_rows, HEADS, HEAD_DIM)
        delta = jnp.sum(
            (att_grad_low.astype(jnp.float32) * attended).reshape(tok_rows, HEADS, HEAD_DIM),
            axis=-1,
        )
        stats_all = (
            lax.all_gather(log_total, "ctx", axis=0, tiled=True),
            lax.all_gather(delta, "ctx", axis=0, tiled=True),
        )
        total_hq = log_total.T
        delta_hq = delta.T
        own_keys = key_rows.reshape(tok_rows, HEADS, HEAD_DIM)
        own_values = value_rows.reshape(tok_rows, HEADS, HEAD_DIM)

        def query_block(running, portion, offset):
            key_blk, value_blk = portion
            row_count = key_blk.shape[0]
            key_places = place_rows(
                offset + jnp.arange(row_count, dtype=jnp.int32), deal, block_rows
            )
            allowed = visible(own_places, key_places, prompt, cont_len)
            key_heads = key_blk.reshape(row_count, HEADS, HEAD_DIM)
            scores = (
                jnp.einsum(
                    "qhd,khd->hqk", query_heads, key_heads, preferred_element_type=jnp.float32
                )
                * scale
            )
            probs = jnp.where(allowed[None], jnp.exp(scores - total_hq[..., None]), 0.0)
            prob_grad = jnp.einsum(
                "qhd,khd->hqk",
                grad_heads,
                value_blk.reshape(row_count, HEADS, HEAD_DIM),
                preferred_element_type=jnp.float32,
            )
            score_grad = (probs * (prob_grad - delta_hq[..., None])).astype(jnp.bfloat16)
            return (
                running
                + jnp.einsum(
                    "hqk,khd->hqd", score_grad, key_heads, preferred_element_type=jnp.float32
                )
                * scale
            )

        def key_block(running, portion, offset):
            query_blk, grad_blk = portion
            row_count = query_blk.shape[0]
            query_places = place_rows(
                offset + jnp.arange(row_count, dtype=jnp.int32), deal, block_rows
            )
            total_blk = lax.dynamic_slice_in_dim(stats_all[0], offset, row_count, 0).T
            delta_blk = lax.dynamic_slice_in_dim(stats_all[1], offset, row_count, 0).T
            allowed = visible(query_places, own_places, prompt, cont_len)
            query_part = query_blk.reshape(row_count, HEADS, HEAD_DIM)
            grad_part = grad_blk.reshape(row_count, HEADS, HEAD_DIM)
            scores = (
                jnp.einsum("qhd,khd->hqk", query_part, own_keys, preferred_element_type=jnp.float32)
                * scale
            )
            probs = jnp.where(allowed[None], jnp.exp(scores - total_blk[..., None]), 0.0)
            value_acc = running[1] + jnp.einsum(
                "hqk,qhd->hkd",
                probs.astype(jnp.bfloat16),
                grad_part,
                preferred_element_type=jnp.float32,
            )
            prob_grad = jnp.einsum(
                "qhd,khd->hqk", grad_part, own_values, preferred_element_type=jnp.float32
            )
            score_grad = (probs * (prob_grad - delta_blk[..., None])).astype(jnp.bfloat16)
            key_acc = (
                running[0]
                + jnp.einsum(
                    "hqk,qhd->hkd", score_grad, query_part, preferred_element_type=jnp.float32
                )
                * scale
            )
            return (key_acc, value_acc)

        zero_heads = jnp.zeros((HEADS, tok_rows, HEAD_DIM), jnp.float32)
        query_flat = query_heads.reshape(tok_rows, model_width)
        query_grad = block_scan(
            query_block,
            zero_heads,
            (
                lax.all_gather(key_rows, "ctx", axis=0, tiled=True),
                lax.all_gather(value_rows, "ctx", axis=0, tiled=True),
            ),
        )
        key_grad, value_grad = block_scan(
            key_block,
            (zero_heads, zero_heads),
            (
                lax.all_gather(query_flat, "ctx", axis=0, tiled=True),
                lax.all_gather(att_grad_low, "ctx", axis=0, tiled=True),
            ),
        )
        _, turn_back = jax.vjp(turn, jnp.zeros((tok_rows, HEADS, HEAD_DIM), jnp.float32))
        query_raw = turn_back(query_grad.transpose(1, 0, 2))[0].reshape(tok_rows, model_width)
        key_raw = turn_back(key_grad.transpose(1, 0, 2))[0].reshape(tok_rows, model_width)
        value_raw = value_grad.transpose(1, 0, 2).reshape(tok_rows, model_width)
        proj_grad = jnp.concatenate([query_raw, key_raw, value_raw], axis=1).astype(jnp.bfloat16)
        normed_grad = jnp.einsum("tj,dj->td", proj_grad, wqkv, preferred_element_type=jnp.float32)
        qkv_w_grad = jnp.einsum(
            "td,tj->dj", normed_low, proj_grad, preferred_element_type=jnp.float32
        )
        _, norm_back_attn = jax.vjp(rms_rows, hidden, gain_attn.astype(jnp.float32))
        hidden_part, gain_attn_grad = norm_back_attn(normed_grad)
        grads = (
            qkv_w_grad,
            out_w_grad,
            gate_w_grad,
            up_w_grad,
            down_grad,
            gain_attn_grad,
            gain_moe_grad,
            router_grad,
            const_grad,
            cvec_grad,
        )
        return (mid_grad + hidden_part, logit_grad, grads)

    hidden = tokens[0].astype(jnp.float32)
    previous = prev_logits[0]
    saved_all = []
    for layer_at in range(LAYERS):
        weights_now = fetch(layer_at)
        (
            layer_wqkv,
            layer_wout,
            layer_wgate,
            layer_wup,
            layer_wdown,
            layer_gain_attn,
            layer_gain_moe,
            layer_wrouter,
            layer_wconst,
            layer_cvec,
        ) = weights_now
        layer_normed_low = rms_rows(hidden, layer_gain_attn.astype(jnp.float32)).astype(
            jnp.bfloat16
        )
        projected = jnp.dot(layer_normed_low, layer_wqkv, preferred_element_type=jnp.float32)
        layer_query_heads = turn(
            projected[:, :model_width].reshape(tok_rows, HEADS, HEAD_DIM)
        ).astype(jnp.bfloat16)
        layer_key_rows = (
            turn(projected[:, model_width : 2 * model_width].reshape(tok_rows, HEADS, HEAD_DIM))
            .astype(jnp.bfloat16)
            .reshape(tok_rows, model_width)
        )
        layer_value_rows = projected[:, 2 * model_width :].astype(jnp.bfloat16)

        def ahead_block(running, portion, offset):
            run_max, run_sum, weighted = running
            key_blk, value_blk = portion
            row_count = key_blk.shape[0]
            key_places = place_rows(
                offset + jnp.arange(row_count, dtype=jnp.int32), deal, block_rows
            )
            allowed = visible(own_places, key_places, prompt, cont_len)
            scores = (
                jnp.einsum(
                    "qhd,khd->hqk",
                    layer_query_heads,
                    key_blk.reshape(row_count, HEADS, HEAD_DIM),
                    preferred_element_type=jnp.float32,
                )
                * scale
            )
            scores = jnp.where(allowed[None], scores, masked_score)
            new_max = jnp.maximum(run_max, jnp.max(scores, axis=-1))
            factor = jnp.exp(run_max - new_max)
            expo = jnp.where(allowed[None], jnp.exp(scores - new_max[..., None]), 0.0)
            run_sum = run_sum * factor + jnp.sum(expo, axis=-1)
            weighted = weighted * factor[..., None] + jnp.einsum(
                "hqk,khd->hqd",
                expo.astype(jnp.bfloat16),
                value_blk.reshape(row_count, HEADS, HEAD_DIM),
                preferred_element_type=jnp.float32,
            )
            return (new_max, run_sum, weighted)

        start = (
            jnp.full((HEADS, tok_rows), masked_score, jnp.float32),
            jnp.zeros((HEADS, tok_rows), jnp.float32),
            jnp.zeros((HEADS, tok_rows, HEAD_DIM), jnp.float32),
        )
        run_max, run_sum, weighted = block_scan(
            ahead_block,
            start,
            (
                lax.all_gather(layer_key_rows, "ctx", axis=0, tiled=True),
                lax.all_gather(layer_value_rows, "ctx", axis=0, tiled=True),
            ),
        )
        layer_attended = (
            (weighted / run_sum[..., None]).transpose(1, 0, 2).reshape(tok_rows, model_width)
        )
        layer_log_total = (run_max + jnp.log(run_sum)).T
        layer_att_low = layer_attended.astype(jnp.bfloat16)
        layer_midway = hidden + jnp.dot(
            layer_att_low, layer_wout, preferred_element_type=jnp.float32
        )
        layer_mixed_rows = rms_rows(layer_midway, layer_gain_moe.astype(jnp.float32))
        layer_mixed_low = layer_mixed_rows.astype(jnp.bfloat16)
        layer_logits = (
            jnp.dot(layer_mixed_low, layer_wrouter, preferred_element_type=jnp.float32) + previous
        )
        chances = softmax_last(layer_logits)
        layer_const_logits = jnp.dot(
            layer_mixed_low, layer_wconst, preferred_element_type=jnp.float32
        )
        layer_mixing = mix_gates(layer_const_logits)
        padded_in = jnp.concatenate(
            [layer_mixed_low, jnp.zeros((1, model_width), jnp.bfloat16)], axis=0
        )
        layer_slot_in = jnp.take(padded_in, slot_token, axis=0).reshape(EXPERTS, CAP, model_width)
        layer_gate_act = jnp.einsum(
            "ecd,edf->ecf", layer_slot_in, layer_wgate, preferred_element_type=jnp.float32
        )
        layer_upward = jnp.einsum(
            "ecd,edf->ecf", layer_slot_in, layer_wup, preferred_element_type=jnp.float32
        )
        layer_hidden_act = (jax.nn.silu(layer_gate_act) * layer_upward).astype(jnp.bfloat16)
        slot_out = jnp.einsum(
            "ecf,efd->ecd", layer_hidden_act, layer_wdown, preferred_element_type=jnp.float32
        ).reshape(EXPERTS * CAP, model_width)
        padded_out = jnp.concatenate([slot_out, jnp.zeros((1, model_width), jnp.float32)], axis=0)
        layer_ffn_pairs = jnp.take(padded_out, slot_index, axis=0).reshape(
            tok_rows, TOP, model_width
        )
        layer_side_terms = side_experts(
            layer_mixed_rows, layer_mixing, layer_cvec.astype(jnp.float32), route_rows
        )
        layer_picked = jnp.sum(route_onehot * chances[:, None, :], axis=-1)
        output = layer_midway + jnp.sum(
            layer_picked[..., None] * (layer_ffn_pairs + layer_side_terms), axis=1
        )
        layer_saved = (
            hidden,
            layer_normed_low,
            layer_query_heads,
            layer_key_rows,
            layer_value_rows,
            layer_attended,
            layer_log_total,
            layer_att_low,
            layer_midway,
            layer_mixed_rows,
            layer_mixed_low,
            layer_logits,
            layer_const_logits,
            layer_mixing,
            layer_slot_in,
            layer_gate_act,
            layer_upward,
            layer_hidden_act,
            layer_ffn_pairs,
            layer_side_terms,
            layer_picked,
        )
        hidden = output
        previous = layer_logits
        saved = layer_saved
        saved_all.append(saved)
    output_rows = hidden.astype(jnp.bfloat16)[None]
    grad_now = grad_out[0].astype(jnp.float32)
    logit_now = jnp.zeros_like(previous)
    parts_all = [None] * LAYERS
    for layer_at in reversed(range(LAYERS)):
        weights_now = fetch(layer_at)
        grad_now, logit_now, grads = layer_back(
            grad_now, logit_now, saved_all[layer_at], weights_now
        )
        parts_all[layer_at] = (
            lax.psum_scatter(grads[0], ("ctx", "fsdp"), scatter_dimension=0, tiled=True),
            lax.psum_scatter(grads[1], ("ctx", "fsdp"), scatter_dimension=0, tiled=True),
            lax.psum_scatter(grads[2], ("ctx", "fsdp"), scatter_dimension=1, tiled=True),
            lax.psum_scatter(grads[3], ("ctx", "fsdp"), scatter_dimension=1, tiled=True),
            lax.psum_scatter(grads[4], ("ctx", "fsdp"), scatter_dimension=1, tiled=True),
            lax.psum_scatter(grads[5], ("ctx", "fsdp"), scatter_dimension=0, tiled=True),
            lax.psum_scatter(grads[6], ("ctx", "fsdp"), scatter_dimension=0, tiled=True),
            lax.psum_scatter(grads[7], ("ctx", "fsdp"), scatter_dimension=0, tiled=True),
            lax.psum_scatter(grads[8], ("ctx", "fsdp"), scatter_dimension=0, tiled=True),
            lax.psum_scatter(grads[9], ("ctx", "fsdp"), scatter_dimension=0, tiled=True),
        )
    stacked = tuple(
        (
            jnp.stack([parts_all[layer_at][member] for layer_at in range(LAYERS)])
            for member in range(10)
        )
    )
    return (
        output_rows,
        grad_now[None],
        stacked[0],
        stacked[1],
        stacked[2],
        stacked[3],
        stacked[4],
        stacked[5],
        stacked[6],
        stacked[7],
        stacked[8],
        stacked[9],
    )


def solution(mesh):
    placed = (
        P("fsdp", "ctx", None),
        P("fsdp", "ctx", None),
        P("fsdp", "ctx", None),
        P("fsdp", "ctx"),
        P(),
        P(None, ("ctx", "fsdp"), None),
        P(None, ("ctx", "fsdp"), None),
        P(None, None, ("ctx", "fsdp"), None),
        P(None, None, ("ctx", "fsdp"), None),
        P(None, None, ("ctx", "fsdp"), None),
        P(None, ("ctx", "fsdp")),
        P(None, ("ctx", "fsdp")),
        P(None, ("ctx", "fsdp"), None),
        P(None, ("ctx", "fsdp"), None),
        P(None, ("ctx", "fsdp"), None),
        P("fsdp", "ctx", None),
    )
    return jax.shard_map(
        shards,
        mesh=mesh,
        in_specs=placed,
        out_specs=(
            P("fsdp", "ctx", None),
            P("fsdp", "ctx", None),
            P(None, ("ctx", "fsdp"), None),
            P(None, ("ctx", "fsdp"), None),
            P(None, None, ("ctx", "fsdp"), None),
            P(None, None, ("ctx", "fsdp"), None),
            P(None, None, ("ctx", "fsdp"), None),
            P(None, ("ctx", "fsdp")),
            P(None, ("ctx", "fsdp")),
            P(None, ("ctx", "fsdp"), None),
            P(None, ("ctx", "fsdp"), None),
            P(None, ("ctx", "fsdp"), None),
        ),
        check_vma=False,
    )
```

profile of v0, /device:TPU:0, one launch (start us, length us, event | category | flops | bytes accessed | tf_op | source)
XLA Modules:
  0.0 4983.8 jit_solution(2935750164702925309)
XLA Ops:
  11.3 42.1 all-reduce.41
  56.0 18.4 all-gather.55.cloned.1.call-done
  102.2 69.7 %all-gather.9 = bf16[1,768,2]{2,0,1:T(2,128)(2,1)S(1)} all-gather(bf16[1,24,2]{2,0,1:T(2,128)(2,1)S(1)} %copy.294), channel_id=11, replica_groups=mesh['ctx'=16,'fsdp'=2] {'ctx','fsdp'}, dimensions={1}, use_global_device_ids=true | all-gather | bytes 3168 | tf_op jit(solution)/shard_map/all_gather | solution.py:163
  174.0 65.8 %all-gather.8 = bf16[1,768,4]{2,0,1:T(2,128)(2,1)S(1)} all-gather(bf16[1,24,4]{2,0,1:T(2,128)(2,1)S(1)} %copy.293), channel_id=10, replica_groups=mesh['ctx'=16,'fsdp'=2] {'ctx','fsdp'}, dimensions={1}, use_global_device_ids=true | all-gather | bytes 6336 | tf_op jit(solution)/shard_map/all_gather | solution.py:162
  242.4 71.5 %all-gather.4 = bf16[1,768,12]{2,0,1:T(2,128)(2,1)S(1)} all-gather(bf16[1,24,12]{2,0,1:T(2,128)(2,1)S(1)} %copy.292), channel_id=6, replica_groups=mesh['ctx'=16,'fsdp'=2] {'ctx','fsdp'}, dimensions={1}, use_global_device_ids=true | all-gather | bytes 19008 | tf_op jit(solution)/shard_map/all_gather | solution.py:161
  325.7 36.9 while.96
  370.3 22.4 all-gather.59.cloned.1.call-done
  403.6 144.7 %all-gather.61.cloned.1.call-done = bf16[1,8,768,2048]{3,2,1,0:T(8,128)(2,1)} async-done(((bf16[1,8,24,2048]{3,2,1,0:T(8,128)(2,1)}), bf16[1,8,768,2048]{3,2,1,0:T(8,128)(2,1)}) %all-gather.61.cloned.1.call-update) | async-done | bytes 25165840 | tf_op jit(solution)/shard_map/all_gather | solution.py:157
  548.3 14.2 multiply_convert_fusion.5
  562.5 141.5 %all-gather.63.cloned.1.call-done = bf16[1,8,2048,768]{3,2,1,0:T(8,128)(2,1)} async-done(((bf16[1,8,64,768]{3,2,1,0:T(8,128)(2,1)}), bf16[1,8,2048,768]{3,2,1,0:T(8,128)(2,1)}) %all-gather.63.cloned.1.call-update) | async-done | bytes 25165840 | tf_op jit(solution)/shard_map/all_gather | solution.py:158
  704.1 12.4 fusion.130
  724.4 41.5 all-gather.65.cloned.1.call-done
  776.1 69.5 %all-gather.19 = bf16[1,768,2]{2,0,1:T(2,128)(2,1)S(1)} all-gather(bf16[1,24,2]{2,0,1:T(2,128)(2,1)S(1)} %copy.297), channel_id=21, replica_groups=mesh['ctx'=16,'fsdp'=2] {'ctx','fsdp'}, dimensions={1}, use_global_device_ids=true | all-gather | bytes 3168 | tf_op jit(solution)/shard_map/all_gather | solution.py:163
  846.1 66.2 %all-gather.18 = bf16[1,768,4]{2,0,1:T(2,128)(2,1)S(1)} all-gather(bf16[1,24,4]{2,0,1:T(2,128)(2,1)S(1)} %copy.295), channel_id=20, replica_groups=mesh['ctx'=16,'fsdp'=2] {'ctx','fsdp'}, dimensions={1}, use_global_device_ids=true | all-gather | bytes 6336 | tf_op jit(solution)/shard_map/all_gather | solution.py:162
  913.3 70.0 %all-gather.14 = bf16[1,768,12]{2,0,1:T(2,128)(2,1)S(1)} all-gather(bf16[1,24,12]{2,0,1:T(2,128)(2,1)S(1)} %copy.296), channel_id=16, replica_groups=mesh['ctx'=16,'fsdp'=2] {'ctx','fsdp'}, dimensions={1}, use_global_device_ids=true | all-gather | bytes 19008 | tf_op jit(solution)/shard_map/all_gather | solution.py:161
  996.6 39.9 while.97
  1048.5 28.6 all-gather.69.cloned.1.call-done
  1087.7 145.1 %all-gather.71.cloned.1.call-done = bf16[1,8,768,2048]{3,2,1,0:T(8,128)(2,1)} async-done(((bf16[1,8,24,2048]{3,2,1,0:T(8,128)(2,1)}), bf16[1,8,768,2048]{3,2,1,0:T(8,128)(2,1)}) %all-gather.71.cloned.1.call-update) | async-done | bytes 25165840 | tf_op jit(solution)/shard_map/all_gather | solution.py:157
  1232.8 14.3 multiply_convert_fusion.4
  1247.1 141.3 %all-gather.73.cloned.1.call-done = bf16[1,8,2048,768]{3,2,1,0:T(8,128)(2,1)} async-done(((bf16[1,8,64,768]{3,2,1,0:T(8,128)(2,1)}), bf16[1,8,2048,768]{3,2,1,0:T(8,128)(2,1)}) %all-gather.73.cloned.1.call-update) | async-done | bytes 25165840 | tf_op jit(solution)/shard_map/all_gather | solution.py:158
  1388.4 13.4 fusion.118
  1416.1 13.7 fusion.150
  1429.8 13.2 fusion.120
  1483.2 21.7 all_gather.145
  1505.2 19.4 all_gather.147
  1524.6 43.1 while.98
  1567.8 73.8 %while.99 = (s32[]{:T(128)}, f32[12,128,64]{1,2,0:T(8,128)}, f32[12,128,64]{1,2,0:T(8,128)}, s32[128]{0:T(128)S(1)}, s32[4]{0:T(128)S(1)}, /*index=5*/s32[32]{0:...) while((s32[]{:T(128)}, f32[12,128,64]{1,2,0:T(8,128)}, ...), condition=%wide.region_51.55_spmd.clone, body=%wide.region_49.54_spmd.clone.sunk | while | flops 411346816 | bytes 22015116 | solution.py:74
  1653.6 13.7 fusion.153
  1671.0 12.3 fusion.132
  1708.3 20.7 all_gather.149
  1734.8 42.9 while.100
  1779.1 19.4 all_gather.151
  1805.2 73.7 %while.101 = (s32[]{:T(128)}, f32[12,128,64]{1,2,0:T(8,128)}, f32[12,128,64]{1,2,0:T(8,128)}, s32[128]{0:T(128)S(1)}, s32[4]{0:T(128)S(1)}, /*index=5*/s32[32]{0...) while((s32[]{:T(128)}, f32[12,128,64]{1,2,0:T(8,128)}, ...), condition=%wide.region_72.76_spmd.clone, body=%wide.region_70.75_spmd.clone.sunk | while | flops 411346816 | bytes 21228656 | solution.py:74
  1896.0 19.7 fusion.278
  1917.0 19.8 fusion.277
  1938.1 19.5 fusion.280
  1958.9 19.5 fusion.279
  1979.6 19.6 fusion.282
  2000.6 19.8 fusion.281
  2023.1 68.7 %all-reduce.44.cloned.1.call-done = (f32[768]{0:T(1024)}, f32[768]{0:T(1024)}, f32[768]{0:T(1024)}, f32[768]{0:T(1024)}, f32[768,12]{0,1:T(8,128)}, /*index=5*/f...) async-done(((f32[768]{0:T(1024)}, f32[768]{0:T(1024)}, f32[768]{0:T(1024)}, f32[768]{0:T(1024)}, f32[768,12]{0,1:T(8,128)}, ...) | async-done | bytes 122896
  2102.3 117.7 %reduce-scatter.19.cloned.1.call-done = f32[24,2304]{1,0:T(8,128)} async-done(((f32[768,2304]{1,0:T(8,128)}), f32[24,2304]{1,0:T(8,128)}) %reduce-scatter.19.cloned.1.call-update) | async-done | bytes 221200 | tf_op jit(solution)/shard_map/reduce_scatter | solution.py:535
  2220.1 124.0 %reduce-scatter.17.cloned.1.call-done = f32[24,2304]{1,0:T(8,128)} async-done(((f32[768,2304]{1,0:T(8,128)}), f32[24,2304]{1,0:T(8,128)}) %reduce-scatter.17.cloned.1.call-update) | async-done | bytes 221200 | tf_op jit(solution)/shard_map/reduce_scatter | solution.py:535
  2345.9 436.6 %reduce-scatter.27.cloned.1.call-done = f32[8,24,2048]{2,1,0:T(8,128)} async-done(((f32[8,768,2048]{2,1,0:T(8,128)}), f32[8,24,2048]{2,1,0:T(8,128)}) %reduce-scatter.27.cloned.1.call-update) | async-done | bytes 1572880 | tf_op jit(solution)/shard_map/reduce_scatter | solution.py:537
  2782.5 438.0 %reduce-scatter.25.cloned.1.call-done = f32[8,24,2048]{2,1,0:T(8,128)} async-done(((f32[8,768,2048]{2,1,0:T(8,128)}), f32[8,24,2048]{2,1,0:T(8,128)}) %reduce-scatter.25.cloned.1.call-update) | async-done | bytes 1572880 | tf_op jit(solution)/shard_map/reduce_scatter | solution.py:537
  3224.5 434.0 %reduce-scatter.31.cloned.1.call-done = f32[8,24,2048]{2,1,0:T(8,128)} async-done(((f32[8,768,2048]{2,1,0:T(8,128)}), f32[8,24,2048]{2,1,0:T(8,128)}) %reduce-scatter.31.cloned.1.call-update) | async-done | bytes 1572880 | tf_op jit(solution)/shard_map/reduce_scatter | solution.py:538
  3658.5 438.0 %reduce-scatter.29.cloned.1.call-done = f32[8,24,2048]{2,1,0:T(8,128)} async-done(((f32[8,768,2048]{2,1,0:T(8,128)}), f32[8,24,2048]{2,1,0:T(8,128)}) %reduce-scatter.29.cloned.1.call-update) | async-done | bytes 1572880 | tf_op jit(solution)/shard_map/reduce_scatter | solution.py:538
  4100.5 434.3 %reduce-scatter.35.cloned.1.call-done = f32[8,64,768]{2,1,0:T(8,128)} async-done(((f32[8,2048,768]{2,1,0:T(8,128)}), f32[8,64,768]{2,1,0:T(8,128)}) %reduce-scatter.35.cloned.1.call-update) | async-done | bytes 1572880 | tf_op jit(solution)/shard_map/reduce_scatter | solution.py:539
  4534.8 438.2 %reduce-scatter.33.cloned.1.call-done = f32[8,64,768]{2,1,0:T(8,128)} async-done(((f32[8,2048,768]{2,1,0:T(8,128)}), f32[8,64,768]{2,1,0:T(8,128)}) %reduce-scatter.33.cloned.1.call-update) | async-done | bytes 1572880 | tf_op jit(solution)/shard_map/reduce_scatter | solution.py:539
  (1327 shorter events, 573.5 us)
Async XLA Ops:
  7.2 67.2 %all-gather.55.cloned.1.call-start = ((), (), s32[]{:S(2)}) async-start(), calls=%async_computation.28 | async-start | bytes 3649536 | tf_op jit(solution)/shard_map/all_gather | solution.py:154
  8.9 306.5 %all-gather.39.cloned.1.call-start = ((), (), s32[]{:S(2)}) async-start(), calls=%async_computation.10 | async-start | bytes 3342336 | tf_op jit(solution)/shard_map/all_gather | solution.py:451
  83.9 236.6 %all-gather.41.cloned.1.call-start = ((), (), s32[]{:S(2)}) async-start(), calls=%async_computation.11 | async-start | bytes 3342336 | tf_op jit(solution)/shard_map/all_gather | solution.py:452
  84.7 279.1 %all-gather.57.cloned.1.call-start = ((), (), s32[]{:S(2)}) async-start(), calls=%async_computation.29 | async-start | bytes 1216512 | tf_op jit(solution)/shard_map/all_gather | solution.py:155
  86.2 306.5 %all-gather.59.cloned.1.call-start = ((), (), s32[]{:S(2)}) async-start(), calls=%async_computation.30 | async-start | bytes 25952256 | tf_op jit(solution)/shard_map/all_gather | solution.py:156
  87.5 460.8 %all-gather.61.cloned.1.call-start = ((), (), s32[]{:S(2)}) async-start(), calls=%async_computation.31 | async-start | bytes 25952256 | tf_op jit(solution)/shard_map/all_gather | solution.py:157
  90.5 613.5 %all-gather.63.cloned.1.call-start = ((), (), s32[]{:S(2)}) async-start(), calls=%async_computation.32 | async-start | bytes 25952256 | tf_op jit(solution)/shard_map/all_gather | solution.py:158
  91.8 81.5 %copy-start.238 = (bf16[2,24,4]{1,2,0:T(4,128)(2,1)S(1)}, bf16[2,24,4]{1,2,0:T(4,128)(2,1)}, u32[]{:S(2)}) copy-start(bf16[2,24,4]{1,2,0:T(4,128)(2,1)} %param.47) | copy-start | bytes 1156
  91.8 149.8 %copy-start.165 = (bf16[2,24,12]{1,0,2:T(2,128)(2,1)S(1)}, bf16[2,24,12]{1,0,2:T(2,128)(2,1)}, u32[]{:S(2)}) copy-start(bf16[2,24,12]{1,0,2:T(2,128)(2,1)} %param.46) | copy-start | bytes 3460
  91.9 674.0 %all-gather.65.cloned.1.call-start = ((), (), s32[]{:S(2)}) async-start(), calls=%async_computation.33 | async-start | bytes 3649536 | tf_op jit(solution)/shard_map/all_gather | solution.py:154
  92.6 894.1 %all-gather.43.cloned.1.call-start = ((), (), s32[]{:S(2)}) async-start(), calls=%async_computation.12 | async-start | bytes 3342336 | tf_op jit(solution)/shard_map/all_gather | solution.py:451
  93.7 221.7 %copy-start.124 = (bf16[128,12,32]{0,2,1:T(8,128)(2,1)S(1)}, bf16[128,12,32]{0,2,1:T(8,128)(2,1)}, u32[]{:S(2)}) copy-start(bf16[128,12,32]{0,2,1:T(8,128)(2,1)} %get-tuple-element.1998) | copy-start | bytes 294916
  93.7 221.6 %copy-start.125 = (bf16[128,12,32]{0,2,1:T(8,128)(2,1)S(1)}, bf16[128,12,32]{0,2,1:T(8,128)(2,1)}, u32[]{:S(2)}) copy-start(bf16[128,12,32]{0,2,1:T(8,128)(2,1)} %get-tuple-element.1999) | copy-start | bytes 294916
  100.5 220.1 %copy-start.230 = (s32[208]{0:T(256)}, s32[208]{0:T(256)S(1)}, u32[]{:S(2)}) copy-start(s32[208]{0:T(256)S(1)} %get-tuple-element.1947) | copy-start | bytes 2500
  240.8 480.6 %copy-start.82 = (f32[128,2]{1,0:T(8,128)}, f32[128,2]{1,0:T(8,128)S(1)}, u32[]{:S(2)}) copy-start(f32[128,2]{1,0:T(8,128)S(1)} %copy.236) | copy-start | bytes 3076
  240.9 480.5 %copy-start.85 = (f32[128,2]{1,0:T(8,128)}, f32[128,2]{1,0:T(8,128)S(1)}, u32[]{:S(2)}) copy-start(f32[128,2]{1,0:T(8,128)S(1)} %copy.232) | copy-start | bytes 3076
  366.9 354.5 %copy-start.24 = (f32[128,768]{1,0:T(8,128)}, f32[128,768]{1,0:T(8,128)S(1)}, u32[]{:S(2)}) copy-start(f32[128,768]{1,0:T(8,128)S(1)} %get-tuple-element.1949) | copy-start | bytes 1179652
  369.0 179.4 %copy-start.15 = (bf16[8,26,768]{2,1,0:T(8,128)(2,1)}, bf16[8,26,768]{2,1,0:T(8,128)(2,1)S(1)}, u32[]{:S(2)}) copy-start(bf16[8,26,768]{2,1,0:T(8,128)(2,1)S(1)} %reshape.1741) | copy-start | bytes 958468
  369.1 352.4 %copy-start.90 = (f32[128,2]{1,0:T(8,128)}, f32[128,2]{1,0:T(8,128)S(1)}, u32[]{:S(2)}) copy-start(f32[128,2]{1,0:T(8,128)S(1)} %copy.224) | copy-start | bytes 3076
  403.6 159.0 %copy-start.2 = (f32[8,26,2048]{2,1,0:T(8,128)}, f32[8,26,2048]{2,1,0:T(8,128)S(1)}, u32[]{:S(2)}) copy-start(f32[8,26,2048]{2,1,0:T(8,128)S(1)} %fusion.138) | copy-start | bytes 5111812
  770.1 221.3 %all-gather.45.cloned.1.call-start = ((), (), s32[]{:S(2)}) async-start(), calls=%async_computation.13 | async-start | bytes 3342336 | tf_op jit(solution)/shard_map/all_gather | solution.py:452
  770.9 266.8 %all-gather.67.cloned.1.call-start = ((), (), s32[]{:S(2)}) async-start(), calls=%async_computation.34 | async-start | bytes 1216512 | tf_op jit(solution)/shard_map/all_gather | solution.py:155
  771.6 305.5 %all-gather.69.cloned.1.call-start = ((), (), s32[]{:S(2)}) async-start(), calls=%async_computation.35 | async-start | bytes 25952256 | tf_op jit(solution)/shard_map/all_gather | solution.py:156
  772.2 460.6 %all-gather.71.cloned.1.call-start = ((), (), s32[]{:S(2)}) async-start(), calls=%async_computation.36 | async-start | bytes 25952256 | tf_op jit(solution)/shard_map/all_gather | solution.py:157
  772.9 140.3 %copy-start.166 = (bf16[1,24,12]{1,0,2:T(2,128)(2,1)S(1)}, bf16[1,24,12]{1,0,2:T(2,128)(2,1)}, u32[]{:S(2)}) copy-start(bf16[1,24,12]{1,0,2:T(2,128)(2,1)} %get-tuple-element.2020) | copy-start | bytes 1732
  773.0 615.4 %all-gather.73.cloned.1.call-start = ((), (), s32[]{:S(2)}) async-start(), calls=%async_computation.37 | async-start | bytes 25952256 | tf_op jit(solution)/shard_map/all_gather | solution.py:158
  773.5 210.7 %copy-start.232 = (s32[208]{0:T(256)S(1)}, s32[208]{0:T(256)}, u32[]{:S(2)}) copy-start(s32[208]{0:T(256)} %copy-done.231) | copy-start | bytes 2500
  773.5 794.2 %all-gather.47.cloned.1.call-start = ((), (), s32[]{:S(2)}) async-start(), calls=%async_computation.14 | async-start | bytes 3342336 | tf_op jit(solution)/shard_map/all_gather | solution.py:352
  774.3 211.5 %copy-start.66 = (f32[128,768]{1,0:T(8,128)}, f32[128,768]{1,0:T(8,128)S(1)}, u32[]{:S(2)}) copy-start(f32[128,768]{1,0:T(8,128)S(1)} %bitcast_convert_fusion) | copy-start | bytes 1179652
  986.6 581.1 %all-gather.49.cloned.1.call-start = ((), (), s32[]{:S(2)}) async-start(), calls=%async_computation.15 | async-start | bytes 3342336 | tf_op jit(solution)/shard_map/all_gather | solution.py:353
  1040.0 370.8 %copy-start.134 = (f32[128,12]{0,1:T(8,128)}, f32[128,12]{0,1:T(8,128)S(1)}, u32[]{:S(2)}) copy-start(f32[128,12]{0,1:T(8,128)S(1)} %get-tuple-element.2066) | copy-start | bytes 18436
  1040.1 370.8 %copy-start.179 = (f32[128]{0:T(128)}, f32[128]{0:T(128)S(1)}, u32[]{:S(2)}) copy-start(f32[128]{0:T(128)S(1)} %get-tuple-element.2065) | copy-start | bytes 1540
  1048.5 184.3 %copy-start.17 = (bf16[8,26,768]{2,1,0:T(8,128)(2,1)}, bf16[8,26,768]{2,1,0:T(8,128)(2,1)S(1)}, u32[]{:S(2)}) copy-start(bf16[8,26,768]{2,1,0:T(8,128)(2,1)S(1)} %reshape.1750) | copy-start | bytes 958468
  1471.9 333.2 %all-gather.51.cloned.1.call-start = ((), (), s32[]{:S(2)}) async-start(), calls=%async_computation.16 | async-start | bytes 3342336 | tf_op jit(solution)/shard_map/all_gather | solution.py:352
  1472.9 332.3 %all-gather.53.cloned.1.call-start = ((), (), s32[]{:S(2)}) async-start(), calls=%async_computation.17 | async-start | bytes 3342336 | tf_op jit(solution)/shard_map/all_gather | solution.py:353
  1707.4 313.0 %reduce-scatter.23.cloned.1.call-start = ((), (), s32[]{:S(2)}) async-start(), calls=%async_computation.21 | async-start | bytes 2433024 | tf_op jit(solution)/shard_map/reduce_scatter | solution.py:536
  1732.5 287.9 %reduce-scatter.21.cloned.1.call-start = ((), (), s32[]{:S(2)}) async-start(), calls=%async_computation.20 | async-start | bytes 2433024 | tf_op jit(solution)/shard_map/reduce_scatter | solution.py:536
  1804.5 287.3 %all-reduce.44.cloned.1.call-start = ((), (), s32[]{:S(2)}) async-start(), calls=%async_computation.38 | async-start | bytes 303104
  1805.2 74.8 %copy-start.110 = (f32[128,32]{0,1:T(8,128)S(1)}, f32[128,32]{0,1:T(8,128)}, u32[]{:S(2)}) copy-start(f32[128,32]{0,1:T(8,128)} %copy-done.108) | copy-start | bytes 49156
  1805.2 74.8 %copy-start.113 = (f32[128,32]{0,1:T(8,128)S(1)}, f32[128,32]{0,1:T(8,128)}, u32[]{:S(2)}) copy-start(f32[128,32]{0,1:T(8,128)} %copy-done.111) | copy-start | bytes 49156
  1886.4 333.7 %reduce-scatter.19.cloned.1.call-start = ((), (), s32[]{:S(2)}) async-start(), calls=%async_computation.19 | async-start | bytes 7299072 | tf_op jit(solution)/shard_map/reduce_scatter | solution.py:535
  1890.6 453.5 %reduce-scatter.17.cloned.1.call-start = ((), (), s32[]{:S(2)}) async-start(), calls=%async_computation.18 | async-start | bytes 7299072 | tf_op jit(solution)/shard_map/reduce_scatter | solution.py:535
  1894.7 887.9 %reduce-scatter.27.cloned.1.call-start = ((), (), s32[]{:S(2)}) async-start(), calls=%async_computation.23 | async-start | bytes 51904512 | tf_op jit(solution)/shard_map/reduce_scatter | solution.py:537
  1915.7 1304.8 %reduce-scatter.25.cloned.1.call-start = ((), (), s32[]{:S(2)}) async-start(), calls=%async_computation.22 | async-start | bytes 51904512 | tf_op jit(solution)/shard_map/reduce_scatter | solution.py:537
  1936.9 1721.6 %reduce-scatter.31.cloned.1.call-start = ((), (), s32[]{:S(2)}) async-start(), calls=%async_computation.25 | async-start | bytes 51904512 | tf_op jit(solution)/shard_map/reduce_scatter | solution.py:538
  1957.7 2138.9 %reduce-scatter.29.cloned.1.call-start = ((), (), s32[]{:S(2)}) async-start(), calls=%async_computation.24 | async-start | bytes 51904512 | tf_op jit(solution)/shard_map/reduce_scatter | solution.py:538
  1978.4 2556.4 %reduce-scatter.35.cloned.1.call-start = ((), (), s32[]{:S(2)}) async-start(), calls=%async_computation.27 | async-start | bytes 51904512 | tf_op jit(solution)/shard_map/reduce_scatter | solution.py:539
  1999.3 2973.7 %reduce-scatter.33.cloned.1.call-start = ((), (), s32[]{:S(2)}) async-start(), calls=%async_computation.26 | async-start | bytes 51904512 | tf_op jit(solution)/shard_map/reduce_scatter | solution.py:539
  (306 other events, 2144.2 us)
Sparse Core Ops, SparseCore 0:
  11.5 62.8 all-gather.54
  84.0 44.3 all-gather.38
  130.8 44.7 all-gather.40
  178.3 53.0 all-gather.56
  234.7 157.9 all-gather.58
  395.4 152.8 all-gather.60
  551.2 152.8 all-gather.62
  707.5 58.3 all-gather.64
  770.2 44.5 all-gather.42
  816.9 44.4 all-gather.44
  864.3 53.5 all-gather.66
  920.6 156.4 all-gather.68
  1079.9 152.8 all-gather.70
  1235.5 152.8 all-gather.72
  1390.5 43.3 all-gather.46
  1472.1 44.3 all-gather.48
  1518.6 43.6 all-gather.50
  1707.5 42.5 all-gather.52
  1755.9 97.9 reduce-scatter.22
  1860.4 98.0 reduce-scatter.20
  1966.1 125.7 all-reduce.43
  2098.4 121.5 reduce-scatter.18
  2225.7 118.2 reduce-scatter.16
  2351.5 430.9 reduce-scatter.26
  2790.1 430.4 reduce-scatter.24
  3228.0 430.4 reduce-scatter.30
  3665.9 430.5 reduce-scatter.28
  4104.1 430.5 reduce-scatter.34
  4542.3 430.5 reduce-scatter.32
where the time goes:
time: 5000 us; the launch traced here: 4980 us
  waiting for transfers between devices  3620 us (72%)
  blocking collectives  536 us (11%)
  matrix products  439 us (9%)
  local copies, waits for them, and re-layouts  238 us (5%)
  other arithmetic  116 us (2%)
    reduce_scatter x2, waiting for transfers between devices, shards(): lax.psum_scatter(grads[2], ('ctx', 'fsdp'), scatter_dimension=1, tiled=True)  875 us
    reduce_scatter x2, waiting for transfers between devices, shards(): lax.psum_scatter(grads[4], ('ctx', 'fsdp'), scatter_dimension=1, tiled=True)  873 us
    reduce_scatter x2, waiting for transfers between devices, shards(): lax.psum_scatter(grads[3], ('ctx', 'fsdp'), scatter_dimension=1, tiled=True)  872 us
    all_gather x2, waiting for transfers between devices, fetch(): lax.all_gather(w_up[layer_at], ('ctx', 'fsdp'), axis=1, tiled=True)  290 us
    all_gather x2, waiting for transfers between devices, fetch(): lax.all_gather(w_down[layer_at], ('ctx', 'fsdp'), axis=1, tiled=True)  283 us
    reduce_scatter x2, waiting for transfers between devices, shards(): lax.psum_scatter(grads[0], ('ctx', 'fsdp'), scatter_dimension=0, tiled=True)  242 us
    all_gather x2, blocking collectives, fetch(): lax.all_gather(w_router[layer_at], ('ctx', 'fsdp'), axis=0, tiled=True)  142 us
    all_gather x2, blocking collectives, fetch(): lax.all_gather(const_vec[layer_at], ('ctx', 'fsdp'), axis=0, tiled=True)  139 us
  transfers between devices with their start and end apart: 29, of which 17 were waited for; matrix products, arithmetic and copies ran while one was open for 15% of the time, Pallas kernels for 0%

commit v1 on v0

v1 whole, which is shorter than its diff:
```python
import functools

import jax
import jax.numpy as jnp
from jax import lax
from jax.experimental import pallas as pl
from jax.experimental.pallas import tpu as pltpu
from jax.sharding import Mesh
from jax.sharding import PartitionSpec as P

HEADS = 12
HEAD_DIM = 64
EXPERTS = 8
TOP = 2
LAYERS = 2
ROUTED = 12
CAP = 26
SLOTS = 32
LANES = 128
PAIRS = HEADS // 2

EX = "ex"
SUB = "sub"
FS = "fsdp"
CTX = (EX, SUB)
ALL = (EX, SUB, FS)

norm_eps = 1e-06
masked_score = -1e30
highest = lax.Precision.HIGHEST
f32 = jnp.float32
bf16 = jnp.bfloat16
VMEM_LIMIT = 56 * 1024 * 1024

SMALL_ROUTER = 2
SMALL_CONST = SMALL_ROUTER + ROUTED
SMALL_CVEC = SMALL_CONST + 4
SMALL_USED = SMALL_CVEC + 2


def dot_nn(a, b):
    return lax.dot_general(a, b, (((1,), (0,)), ((), ())), preferred_element_type=f32)


def dot_nt(a, b):
    return lax.dot_general(a, b, (((1,), (1,)), ((), ())), preferred_element_type=f32)


def dot_tn(a, b):
    return lax.dot_general(a, b, (((0,), (0,)), ((), ())), preferred_element_type=f32)


def kernel_params(steps):
    return pltpu.CompilerParams(
        dimension_semantics=("arbitrary",) * steps, vmem_limit_bytes=VMEM_LIMIT
    )


def turn_lanes(x, cosine, sine):
    lane = lax.broadcasted_iota(jnp.int32, x.shape, 1)
    ahead = pltpu.roll(x, LANES - HEAD_DIM // 2, 1)
    behind = pltpu.roll(x, HEAD_DIM // 2, 1)
    partner = jnp.where(lane % HEAD_DIM < HEAD_DIM // 2, ahead, behind)
    return x * cosine + partner * sine


def project_kernel(turned, a_ref, *refs):
    count = len(turned)
    w_refs = refs[:count]
    cos_ref, sin_ref = refs[count : count + 2]
    out_refs = refs[count + 2 :]
    a = a_ref[...]
    for w_ref, out_ref, turn in zip(w_refs, out_refs, turned):
        acc = dot_nn(a, w_ref[...])
        if not turn:
            out_ref[...] = acc.astype(bf16)
            continue
        for at in range(0, acc.shape[1], LANES):
            part = turn_lanes(acc[:, at : at + LANES], cos_ref[...], sin_ref[...])
            out_ref[:, at : at + LANES] = part.astype(bf16)


def project(rows, packed, columns, turned, cosine, sine):
    count, width = rows.shape
    tile = min(count, 256)
    w_specs = [
        pl.BlockSpec((width, width), functools.partial(lambda at, i: (0, at), at))
        for at in columns
    ]
    row_spec = pl.BlockSpec((tile, width), lambda i: (i, 0))
    table = pl.BlockSpec((tile, LANES), lambda i: (i, 0))
    return pl.pallas_call(
        functools.partial(project_kernel, turned),
        grid=(count // tile,),
        in_specs=[row_spec] + w_specs + [table, table],
        out_specs=[row_spec] * len(columns),
        out_shape=[jax.ShapeDtypeStruct((count, width), bf16)] * len(columns),
        compiler_params=kernel_params(1),
        cost_estimate=pl.CostEstimate(
            flops=2 * count * width * width * len(columns),
            bytes_accessed=2 * width * (count * (1 + len(columns)) + width * len(columns)),
            transcendentals=0,
        ),
    )(rows, *([packed] * len(columns)), cosine, sine)


def split_heads(x):
    wide = x.astype(f32)
    left = lax.broadcasted_iota(jnp.int32, wide.shape, 1) < HEAD_DIM
    zero = jnp.zeros_like(wide)
    return jnp.concatenate(
        [jnp.where(left, wide, zero), jnp.where(left, zero, wide)], axis=0
    ).astype(bf16)


def join_heads(x, rows):
    left = lax.broadcasted_iota(jnp.int32, (rows, LANES), 1) < HEAD_DIM
    return jnp.where(left, x[:rows], x[rows:])


def attend_kernel(
    prompt, q_ref, k_ref, v_ref, at_ref, start_ref, key_ref, o_ref, total_ref, bias_ref
):
    pair = pl.program_id(0)
    rows = q_ref.shape[0]

    @pl.when(pair == 0)
    def _():
        places, keys = at_ref[...], key_ref[...]
        seen = (keys <= places) & ((keys < prompt) | (keys >= start_ref[...]))
        bias_ref[...] = jnp.where(seen, 0.0, masked_score)
        total_ref[...] = jnp.zeros_like(total_ref)

    queries = split_heads(q_ref[...] * HEAD_DIM ** (-0.5))
    keys, values = k_ref[...], v_ref[...]
    lane = lax.broadcasted_iota(jnp.int32, (rows, LANES), 1)
    outs = []
    totals = total_ref[...]
    for side in range(2):
        scores = dot_nt(queries[side * rows : (side + 1) * rows], keys) + bias_ref[...]
        top = jnp.max(scores, axis=1, keepdims=True)
        expo = jnp.exp(scores - top)
        total = jnp.sum(expo, axis=1, keepdims=True)
        outs.append(dot_nn(expo.astype(bf16), values) / total)
        totals = jnp.where(lane == 2 * pair + side, top + jnp.log(total), totals)
    o_ref[...] = jnp.where(lane < HEAD_DIM, outs[0], outs[1])
    total_ref[...] = totals


def attend(queries, keys, values, places, starts, key_places, prompt):
    rows, width = queries.shape
    length = keys.shape[0]
    own = pl.BlockSpec((rows, LANES), lambda j: (0, j))
    every = pl.BlockSpec((length, LANES), lambda j: (0, j))
    column = pl.BlockSpec((rows, 1), lambda j: (0, 0))
    line = pl.BlockSpec((1, length), lambda j: (0, 0))
    return pl.pallas_call(
        functools.partial(attend_kernel, prompt),
        grid=(PAIRS,),
        in_specs=[own, every, every, column, column, line],
        out_specs=[own, pl.BlockSpec((rows, LANES), lambda j: (0, 0))],
        out_shape=[
            jax.ShapeDtypeStruct((rows, width), f32),
            jax.ShapeDtypeStruct((rows, LANES), f32),
        ],
        scratch_shapes=[pltpu.VMEM((rows, length), f32)],
        compiler_params=kernel_params(1),
        cost_estimate=pl.CostEstimate(
            flops=8 * rows * length * width,
            bytes_accessed=4 * length * width,
            transcendentals=rows * length * HEADS,
        ),
    )(queries, keys, values, places, starts, key_places)


def pick_column(table, at):
    lane = lax.broadcasted_iota(jnp.int32, table.shape, 1)
    return jnp.sum(jnp.where(lane == at, table, 0.0), axis=1, keepdims=True)


def query_kernel(
    prompt,
    q_ref,
    g_ref,
    k_ref,
    v_ref,
    total_ref,
    delta_ref,
    at_ref,
    start_ref,
    key_ref,
    cos_ref,
    sin_ref,
    out_ref,
    bias_ref,
):
    pair = pl.program_id(0)
    rows = q_ref.shape[0]

    @pl.when(pair == 0)
    def _():
        places, keys = at_ref[...], key_ref[...]
        seen = (keys <= places) & ((keys < prompt) | (keys >= start_ref[...]))
        bias_ref[...] = jnp.where(seen, 0.0, masked_score)

    scale = HEAD_DIM ** (-0.5)
    queries = split_heads(q_ref[...] * scale)
    grads = split_heads(g_ref[...])
    keys, values = k_ref[...], v_ref[...]
    lane = lax.broadcasted_iota(jnp.int32, (rows, LANES), 1)
    outs = []
    for side in range(2):
        part = slice(side * rows, (side + 1) * rows)
        total = pick_column(total_ref[...], 2 * pair + side)
        delta = pick_column(delta_ref[...], 2 * pair + side)
        scores = dot_nt(queries[part], keys) + bias_ref[...]
        probs = jnp.exp(scores - total)
        prob_grad = dot_nt(grads[part], values)
        score_grad = (probs * (prob_grad - delta)).astype(bf16)
        outs.append(dot_nn(score_grad, keys))
    out = jnp.where(lane < HEAD_DIM, outs[0], outs[1]) * scale
    out_ref[...] = turn_lanes(out, cos_ref[...], -sin_ref[...]).astype(bf16)


def query_back(queries, grads, keys, values, totals, delta, places, starts, key_places, cosine, sine, prompt):
    rows, width = queries.shape
    length = keys.shape[0]
    own = pl.BlockSpec((rows, LANES), lambda j: (0, j))
    every = pl.BlockSpec((length, LANES), lambda j: (0, j))
    same = pl.BlockSpec((rows, LANES), lambda j: (0, 0))
    column = pl.BlockSpec((rows, 1), lambda j: (0, 0))
    line = pl.BlockSpec((1, length), lambda j: (0, 0))
    return pl.pallas_call(
        functools.partial(query_kernel, prompt),
        grid=(PAIRS,),
        in_specs=[own, own, every, every, same, same, column, column, line, same, same],
        out_specs=own,
        out_shape=jax.ShapeDtypeStruct((rows, width), bf16),
        scratch_shapes=[pltpu.VMEM((rows, length), f32)],
        compiler_params=kernel_params(1),
        cost_estimate=pl.CostEstimate(
            flops=12 * rows * length * width,
            bytes_accessed=4 * length * width,
            transcendentals=rows * length * HEADS,
        ),
    )(queries, grads, keys, values, totals, delta, places, starts, key_places, cosine, sine)


def key_kernel(
    prompt,
    k_ref,
    v_ref,
    q_ref,
    g_ref,
    stat_ref,
    own_ref,
    at_ref,
    start_ref,
    cos_ref,
    sin_ref,
    dk_ref,
    dv_ref,
    bias_ref,
    lines_ref,
):
    pair = pl.program_id(0)
    rows = k_ref.shape[0]

    @pl.when(pair == 0)
    def _():
        keys, places = own_ref[...], at_ref[...]
        seen = (keys <= places) & ((keys < prompt) | (keys >= start_ref[...]))
        bias_ref[...] = jnp.where(seen, 0.0, masked_score)
        flat = stat_ref[...].astype(f32).T
        for head in range(HEADS):
            lines_ref[head] = flat[head : head + 1] + flat[16 + head : 17 + head]
            lines_ref[16 + head] = flat[32 + head : 33 + head] + flat[48 + head : 49 + head]

    scale = HEAD_DIM ** (-0.5)
    own_keys = split_heads(k_ref[...] * scale)
    own_values = split_heads(v_ref[...])
    queries, grads = q_ref[...], g_ref[...]
    lane = lax.broadcasted_iota(jnp.int32, (rows, LANES), 1)
    key_outs, value_outs = [], []
    for side in range(2):
        part = slice(side * rows, (side + 1) * rows)
        total = lines_ref[2 * pair + side]
        delta = lines_ref[16 + 2 * pair + side]
        scores = dot_nt(own_keys[part], queries) + bias_ref[...]
        probs = jnp.exp(scores - total)
        value_outs.append(dot_nn(probs.astype(bf16), grads))
        prob_grad = dot_nt(own_values[part], grads)
        score_grad = (probs * (prob_grad - delta)).astype(bf16)
        key_outs.append(dot_nn(score_grad, queries))
    left = lane < HEAD_DIM
    dk = jnp.where(left, key_outs[0], key_outs[1]) * scale
    dk_ref[...] = turn_lanes(dk, cos_ref[...], -sin_ref[...]).astype(bf16)
    dv_ref[...] = jnp.where(left, value_outs[0], value_outs[1]).astype(bf16)


def key_back(own_keys, own_values, queries, sent, own_places, places, starts, cosine, sine, prompt):
    rows, width = own_keys.shape
    length = queries.shape[0]
    own = pl.BlockSpec((rows, LANES), lambda j: (0, j))
    every = pl.BlockSpec((length, LANES), lambda j: (0, j))
    stats = pl.BlockSpec((length, LANES), lambda j: (0, PAIRS))
    same = pl.BlockSpec((rows, LANES), lambda j: (0, 0))
    column = pl.BlockSpec((rows, 1), lambda j: (0, 0))
    line = pl.BlockSpec((1, length), lambda j: (0, 0))
    return pl.pallas_call(
        functools.partial(key_kernel, prompt),
        grid=(PAIRS,),
        in_specs=[own, own, every, every, stats, column, line, line, same, same],
        out_specs=[own, own],
        out_shape=[jax.ShapeDtypeStruct((rows, width), bf16)] * 2,
        scratch_shapes=[
            pltpu.VMEM((rows, length), f32),
            pltpu.VMEM((32, 1, length), f32),
        ],
        compiler_params=kernel_params(1),
        cost_estimate=pl.CostEstimate(
            flops=16 * rows * length * width,
            bytes_accessed=4 * length * width,
            transcendentals=rows * length * HEADS,
        ),
    )(own_keys, own_values, queries, sent, sent, own_places, places, starts, cosine, sine)


def rms_rows(values, gain):
    scale = lax.rsqrt(jnp.mean(values * values, axis=-1, keepdims=True) + norm_eps)
    return values * scale * gain


def rms_back(values, gain, grad):
    mean = jnp.mean(values * values, axis=-1, keepdims=True) + norm_eps
    scale = lax.rsqrt(mean)
    inner = grad * gain
    along = jnp.mean(inner * values, axis=-1, keepdims=True)
    gain_grad = jnp.sum(grad * values * scale, axis=0)
    return scale * inner - values * (scale / mean * along), gain_grad


def high_low(x):
    top = x.astype(bf16)
    return top, (x - top.astype(f32)).astype(bf16)


def dispatch(x):
    return lax.all_to_all(x, EX, 0, 0, tiled=True)


def shards(
    tokens,
    prev_logits,
    routes,
    order,
    deal,
    w_qkv,
    w_out,
    w_gate,
    w_up,
    w_down,
    norm_attn,
    norm_moe,
    w_router,
    w_const,
    const_vec,
    grad_out,
):
    rows, width = tokens.shape[1], tokens.shape[2]
    subs = lax.axis_size(SUB)
    ctx_size = lax.axis_size(EX) * subs
    length = rows * ctx_size
    prompt = length // 2
    cont_len = prompt // (ctx_size // 8)
    block_rows = rows // 2
    own_rows = w_qkv.shape[1]
    me = lax.axis_index(CTX)

    pad = jnp.zeros((own_rows, LANES - SMALL_USED), bf16)

    def fetch(layer):
        mine = jnp.concatenate(
            [
                w_qkv[layer],
                w_out[layer],
                norm_attn[layer][:, None],
                norm_moe[layer][:, None],
                w_router[layer],
                w_const[layer],
                const_vec[layer],
                pad,
            ],
            axis=1,
        )
        packed = lax.all_gather(mine, ALL, axis=0, tiled=True)
        experts = []
        for member in (w_gate, w_up, w_down):
            moved = dispatch(member[layer])
            whole = lax.all_gather(moved, (SUB, FS), axis=1, tiled=True)
            experts.append(whole.reshape(-1, whole.shape[2]))
        return packed, experts

    fetched = [fetch(layer) for layer in range(LAYERS)]

    all_places = (
        deal[:, None] * block_rows + jnp.arange(block_rows, dtype=jnp.int32)[None, :]
    ).reshape(length)
    within = jnp.where(all_places < prompt, all_places, prompt + (all_places - prompt) % cont_len)
    all_starts = jnp.where(all_places < prompt, 0, all_places - (all_places - prompt) % cont_len)
    lane = jnp.arange(LANES, dtype=jnp.int32)
    half = HEAD_DIM // 2
    frequency = 10000.0 ** (-(lane % half).astype(f32) / half)
    angles = within.astype(f32)[:, None] * frequency[None, :]
    cosine = jnp.cos(angles)
    sine = jnp.sin(angles) * jnp.where(lane % HEAD_DIM < half, -1.0, 1.0)[None, :]

    def own_part(table):
        return lax.dynamic_slice_in_dim(table, me * rows, rows, 0)

    own_cos, own_sin = own_part(cosine), own_part(sine)
    own_places = own_part(all_places)[:, None]
    own_starts = own_part(all_starts)[:, None]
    place_line, start_line = all_places[None, :], all_starts[None, :]

    route_rows = routes[0]
    flat_routes = jnp.concatenate([route_rows[:, k] for k in range(TOP)])
    flat_order = jnp.concatenate([order[0].reshape(rows, TOP)[:, k] for k in range(TOP)])
    earlier = (flat_routes[None, :] == flat_routes[:, None]) & (
        flat_order[None, :] < flat_order[:, None]
    )
    slot = jnp.sum(earlier.astype(jnp.int32), axis=1)
    in_slot = (flat_routes < EXPERTS) & (slot < CAP)
    target = jnp.where(in_slot, flat_routes * SLOTS + slot, -1)
    slot_ids = jnp.arange(EXPERTS * SLOTS, dtype=jnp.int32)
    pair_slots = (target[:, None] == slot_ids[None, :]).astype(bf16)
    slot_pairs = (slot_ids[:, None] == target[None, :]).astype(bf16)
    slot_tokens = slot_pairs[:, :rows] + slot_pairs[:, rows:]
    token_slots = pair_slots[:rows] + pair_slots[rows:]
    route_ids = jnp.arange(ROUTED, dtype=jnp.int32)
    picks = [(route_rows[:, k : k + 1] == route_ids[None, :]).astype(f32) for k in range(TOP)]
    chosen = picks[0] + picks[1]
    head_of = (
        jnp.arange(width, dtype=jnp.int32)[:, None] // HEAD_DIM == lane[None, :]
    ).astype(f32)

    def unpack(packed):
        small = packed[:, 4 * width :]
        return small, small[:, 0].astype(f32), small[:, 1].astype(f32)

    hidden = tokens[0].astype(f32)
    previous = prev_logits[0]
    saved_all = []
    for layer in range(LAYERS):
        packed, (wgate, wup, wdown) = fetched[layer]
        small, gain_attn, gain_moe = unpack(packed)
        normed = rms_rows(hidden, gain_attn).astype(bf16)
        normed_all = lax.all_gather(normed, CTX, axis=0, tiled=True)
        (queries,) = project(normed, packed, (0,), (True,), own_cos, own_sin)
        keys, values = project(normed_all, packed, (1, 2), (True, False), cosine, sine)
        attended, totals = attend(
            queries, keys, values, own_places, own_starts, place_line, prompt
        )
        att_low = attended.astype(bf16)
        wout = packed[:, 3 * width : 4 * width]
        midway = hidden + dot_nn(att_low, wout)
        mixed = rms_rows(midway, gain_moe)
        mixed_low = mixed.astype(bf16)
        slot_in = dot_nn(slot_tokens, mixed_low).astype(bf16)
        expert_in = dispatch(slot_in.reshape(EXPERTS, SLOTS, width)).reshape(-1, width)
        thin = dot_nn(mixed_low, small)
        logits = thin[:, SMALL_ROUTER:SMALL_CONST] + previous
        chances = jax.nn.softmax(logits, axis=-1)
        mixing = jax.nn.softmax(thin[:, SMALL_CONST:SMALL_CVEC].reshape(rows, 2, 2), axis=-1)
        gate_act = dot_nn(expert_in, wgate)
        upward = dot_nn(expert_in, wup)
        inner = (jax.nn.silu(gate_act) * upward).astype(bf16)
        expert_out = dot_nn(inner, wdown).astype(bf16)
        back = dispatch(expert_out.reshape(EXPERTS, SLOTS, width)).reshape(-1, width)
        pair_out = dot_nn(pair_slots, back)
        weight = chances * chosen
        picked = [jnp.sum(chances * picks[k], axis=1, keepdims=True) for k in range(TOP)]
        alpha = (
            weight[:, 9:10]
            + weight[:, 10:11] * mixing[:, 0, 0:1]
            + weight[:, 11:12] * mixing[:, 1, 0:1]
        )
        betas = [weight[:, 10 + c : 11 + c] * mixing[:, c, 1:2] for c in range(2)]
        cvecs = [small[:, SMALL_CVEC + c].astype(f32) for c in range(2)]
        output = (
            midway
            + picked[0] * pair_out[:rows]
            + picked[1] * pair_out[rows:]
            + alpha * mixed
            + betas[0] * cvecs[0][None, :]
            + betas[1] * cvecs[1][None, :]
        )
        saved_all.append(
            (
                hidden,
                normed,
                normed_all,
                queries,
                keys,
                values,
                attended,
                totals,
                att_low,
                midway,
                mixed,
                mixed_low,
                chances,
                mixing,
                expert_in,
                gate_act,
                upward,
                inner,
                pair_out,
                weight,
                picked,
                alpha,
                betas,
                cvecs,
            )
        )
        hidden = output
        previous = logits
    output_rows = hidden.astype(bf16)[None]

    grad = grad_out[0].astype(f32)
    logit_next = jnp.zeros((rows, ROUTED), f32)
    results = [None] * LAYERS
    for layer in reversed(range(LAYERS)):
        (
            hidden,
            normed,
            normed_all,
            queries,
            keys,
            values,
            attended,
            totals,
            att_low,
            midway,
            mixed,
            mixed_low,
            chances,
            mixing,
            expert_in,
            gate_act,
            upward,
            inner,
            pair_out,
            weight,
            picked,
            alpha,
            betas,
            cvecs,
        ) = saved_all[layer]
        packed, (wgate, wup, wdown) = fetched[layer]
        small, gain_attn, gain_moe = unpack(packed)
        pair_grad = jnp.concatenate([picked[k] * grad for k in range(TOP)], axis=0).astype(bf16)
        slot_grad = dot_nn(slot_pairs, pair_grad).astype(bf16)
        out_grad = dispatch(slot_grad.reshape(EXPERTS, SLOTS, width)).reshape(-1, width)
        inner_grad = dot_nt(out_grad, wdown)
        sigma = jax.nn.sigmoid(gate_act)
        gated = gate_act * sigma
        up_grad = (inner_grad * gated).astype(bf16)
        gate_grad = (inner_grad * upward * (sigma + gated * (1.0 - sigma))).astype(bf16)
        in_grad = (dot_nt(gate_grad, wgate) + dot_nt(up_grad, wup)).astype(bf16)
        in_back = dispatch(in_grad.reshape(EXPERTS, SLOTS, width)).reshape(-1, width)
        expert_grads = (
            dot_tn(expert_in, gate_grad),
            dot_tn(expert_in, up_grad),
            dot_tn(inner, out_grad),
        )
        returned = []
        for member in expert_grads:
            cut = member.astype(bf16).reshape(EXPERTS, subs * 2, -1, member.shape[1])
            part = lax.psum_scatter(cut, (SUB, FS), scatter_dimension=1, tiled=True)
            returned.append(dispatch(part.reshape(EXPERTS, -1, member.shape[1])).astype(f32))

        picked_grad = [
            jnp.sum(grad * pair_out[k * rows : (k + 1) * rows], axis=1, keepdims=True)
            for k in range(TOP)
        ]
        along = jnp.sum(grad * mixed, axis=1, keepdims=True)
        across = [jnp.sum(grad * cvecs[c][None, :], axis=1, keepdims=True) for c in range(2)]
        chance_grad = picks[0] * picked_grad[0] + picks[1] * picked_grad[1]
        side = jnp.concatenate(
            [
                jnp.zeros((rows, EXPERTS + 1), f32),
                along,
                mixing[:, 0, 0:1] * along + mixing[:, 0, 1:2] * across[0],
                mixing[:, 1, 0:1] * along + mixing[:, 1, 1:2] * across[1],
            ],
            axis=1,
        )
        chance_grad = chance_grad + side * chosen
        logit_grad = (
            chances * (chance_grad - jnp.sum(chances * chance_grad, axis=1, keepdims=True))
            + logit_next
        )
        mix_cols = []
        for c in range(2):
            first = weight[:, 10 + c : 11 + c] * along
            second = weight[:, 10 + c : 11 + c] * across[c]
            m0, m1 = mixing[:, c, 0:1], mixing[:, c, 1:2]
            mean = m0 * first + m1 * second
            mix_cols += [m0 * (first - mean), m1 * (second - mean)]
        thin_grad = jnp.concatenate(
            [jnp.zeros((rows, SMALL_ROUTER), f32), logit_grad]
            + mix_cols
            + [jnp.zeros((rows, LANES - SMALL_CVEC), f32)],
            axis=1,
        )
        low_grad = (
            alpha * grad
            + lax.dot_general(
                thin_grad,
                small.astype(f32),
                (((1,), (1,)), ((), ())),
                precision=highest,
                preferred_element_type=f32,
            )
            + dot_nn(token_slots, in_back)
        )
        mid_part, gain_moe_grad = rms_back(midway, gain_moe, low_grad)
        mid_grad = grad + mid_part
        mid_low = mid_grad.astype(bf16)
        wout = packed[:, 3 * width : 4 * width]
        att_grad = dot_nt(mid_low, wout).astype(bf16)
        delta = jnp.dot(att_grad.astype(f32) * attended, head_of, precision=highest)
        pieces = []
        for stat in (totals, delta):
            pieces += [part[:, :16] for part in high_low(stat)]
        sent = jnp.concatenate(
            [att_grad] + pieces + [jnp.zeros((rows, LANES - 64), bf16)], axis=1
        )
        sent_all = lax.all_gather(sent, CTX, axis=0, tiled=True)
        (all_queries,) = project(normed_all, packed, (0,), (True,), cosine, sine)
        query_grad = query_back(
            queries,
            att_grad,
            keys,
            values,
            totals,
            delta,
            own_places,
            own_starts,
            place_line,
            own_cos,
            own_sin,
            prompt,
        )
        key_grad, value_grad = key_back(
            own_part(keys),
            own_part(values),
            all_queries,
            sent_all,
            own_places,
            place_line,
            start_line,
            own_cos,
            own_sin,
            prompt,
        )
        proj_grad = jnp.concatenate([query_grad, key_grad, value_grad], axis=1)
        normed_grad = dot_nt(proj_grad, packed[:, : 3 * width])
        hidden_part, gain_attn_grad = rms_back(hidden, gain_attn, normed_grad)
        thin_w = jnp.dot(mixed_low.astype(f32).T, thin_grad, precision=highest)
        cvec_grads = [jnp.sum(betas[c] * grad, axis=0)[:, None] for c in range(2)]
        packed_grad = jnp.concatenate(
            [
                dot_tn(normed, proj_grad),
                dot_tn(att_low, mid_low),
                gain_attn_grad[:, None],
                gain_moe_grad[:, None],
                thin_w[:, SMALL_ROUTER:SMALL_CVEC],
                cvec_grads[0],
                cvec_grads[1],
                jnp.zeros((width, LANES - SMALL_USED), f32),
            ],
            axis=1,
        ).astype(bf16)
        owned = lax.psum_scatter(packed_grad, ALL, scatter_dimension=0, tiled=True).astype(f32)
        results[layer] = (
            owned[:, : 3 * width],
            owned[:, 3 * width : 4 * width],
            returned[0],
            returned[1],
            returned[2],
            owned[:, 4 * width],
            owned[:, 4 * width + 1],
            owned[:, 4 * width + SMALL_ROUTER : 4 * width + SMALL_CONST],
            owned[:, 4 * width + SMALL_CONST : 4 * width + SMALL_CVEC],
            owned[:, 4 * width + SMALL_CVEC : 4 * width + SMALL_USED],
        )
        grad = mid_grad + hidden_part
        logit_next = logit_grad
    stacked = tuple(
        jnp.stack([results[layer][member] for layer in range(LAYERS)]) for member in range(10)
    )
    return (output_rows, grad[None]) + stacked


def solution(mesh):
    devices = mesh.devices
    finer = Mesh(devices.reshape(EXPERTS, devices.shape[0] // EXPERTS, devices.shape[1]), ALL)
    token_spec = P(FS, CTX, None)
    row_spec = P(None, ALL, None)
    expert_spec = P(None, None, ALL, None)
    gain_spec = P(None, ALL)
    return jax.shard_map(
        shards,
        mesh=finer,
        in_specs=(
            token_spec,
            token_spec,
            token_spec,
            P(FS, CTX),
            P(),
            row_spec,
            row_spec,
            expert_spec,
            expert_spec,
            expert_spec,
            gain_spec,
            gain_spec,
            row_spec,
            row_spec,
            row_spec,
            token_spec,
        ),
        out_specs=(
            token_spec,
            token_spec,
            row_spec,
            row_spec,
            expert_spec,
            expert_spec,
            expert_spec,
            gain_spec,
            gain_spec,
            row_spec,
            row_spec,
            row_spec,
        ),
        check_vma=False,
    )
```

time: 5000 us -> 1180 us (0.24)
  waiting for transfers between devices: 3620 us -> 557 us
  blocking collectives: 536 us -> 173 us
  matrix products: 439 us -> 91.3 us
  local copies, waits for them, and re-layouts: 238 us -> 96.9 us
  Pallas kernels: 0 us -> 109 us
  starting transfers between devices: 1.36 us -> 65.4 us
  other arithmetic: 116 us -> 54.5 us
    reduce_scatter x10 -> x6, waiting for transfers between devices: 2860 us -> 107 us  [shards(): part = lax.psum_scatter(cut, (SUB, FS), scatter_dimension=1, tiled=True)]
    all_gather x18 -> x12, waiting for transfers between devices: 684 us -> 173 us  [the longest x6 87.2 us: fetch(): whole = lax.all_gather(moved, (SUB, FS), axis=1, tiled=True)]
    all_gather x10 -> x0, blocking collectives: 494 us -> none  [the longest x2 142 us: fetch(): lax.all_gather(w_router[layer_at], ('ctx', 'fsdp'), axis=0, tiled=True)]
    dot_general x98 -> x44, matrix products: 439 us -> 91.3 us  [the longest x18 43.6 us: dot_nn(): lax.dot_general(a, b, (((1,), (0,)), ((), ())), preferred_element_type=f32)]
    all_to_all x0 -> x6, blocking collectives: none -> 173 us  [dispatch(): return lax.all_to_all(x, EX, 0, 0, tiled=True)]
    unnamed x30 -> x22, waiting for transfers between devices: 72.2 us -> 187 us
    pallas_call x0 -> x12, Pallas kernels: none -> 109 us  [the longest x6 47 us: project(): pl.pallas_call(functools.partial(project_kernel, turned), grid=(count //...]
    dynamic_slice x64 -> x6, local copies, waits for them, and re-layouts: 105 us -> 7.81 us  [own_part(): return lax.dynamic_slice_in_dim(table, me * rows, rows, 0)]
  transfers between devices with their start and end apart: 29 -> 34, of which waited for: 17 -> 22; matrix products, arithmetic and copies ran while one was open for 15% -> 15% of each run, Pallas kernels for 0% -> 9%
where the time goes in v1:
time: 1180 us; the launch traced here: 1160 us
  waiting for transfers between devices  557 us (47%)
  blocking collectives  173 us (15%)
  Pallas kernels  109 us (9%)
  local copies, waits for them, and re-layouts  96.9 us (8%)
  matrix products  91.3 us (8%)
  starting transfers between devices  65.4 us (6%)
  other arithmetic  54.5 us (5%)
  between operations  16.5 us (1%)
    unnamed x22, waiting for transfers between devices  187 us
    all_to_all x6, blocking collectives, dispatch(): return lax.all_to_all(x, EX, 0, 0, tiled=True)  173 us
    reduce_scatter x6, waiting for transfers between devices, shards(): part = lax.psum_scatter(cut, (SUB, FS), scatter_dimension=1, tiled=True)  107 us
    all_to_all x14, waiting for transfers between devices, dispatch(): return lax.all_to_all(x, EX, 0, 0, tiled=True)  90 us
    all_gather x6, waiting for transfers between devices, fetch(): whole = lax.all_gather(moved, (SUB, FS), axis=1, tiled=True)  87.2 us
    all_gather x2, waiting for transfers between devices, fetch(): packed = lax.all_gather(mine, ALL, axis=0, tiled=True)  66 us
    all_to_all x14, starting transfers between devices, dispatch(): return lax.all_to_all(x, EX, 0, 0, tiled=True)  64.2 us
    pallas_call x6, Pallas kernels, project(): pl.pallas_call(functools.partial(project_kernel, turned), grid=(count //...  47 us
  transfers between devices with their start and end apart: 34, of which 22 were waited for; matrix products, arithmetic and copies ran while one was open for 15% of the time, Pallas kernels for 9%

profile of v1, /device:TPU:0, one launch (start us, length us, event | category | flops | bytes accessed | tf_op | source)
XLA Modules:
  0.0 1162.9 jit_solution(10005889943136803896)
XLA Ops:
  15.7 65.5 %all-gather.13.cloned.1.call-done.refs_0_.refs_1_ = bf16[768,3200]{1,0:T(8,128)(2,1)} async-done(((bf16[24,3200]{1,0:T(8,128)(2,1)}), bf16[768,3200]{1,0:T(8,128)(2,1)}) %all-gather.13.cloned.1.call-update) | async-done | bytes 4915216 | tf_op jit(solution)/shard_map/all_gather | solution.py:396
  87.9 31.1 %all_to_all.100 = bf16[8,24,2048]{2,1,0:T(8,128)(2,1)} all-to-all(bf16[8,24,2048]{2,1,0:T(8,128)(2,1)S(1)} %get-tuple-element.156), channel_id=1, replica_groups=mesh['ex'=8,'sub'=2,'fsdp'=2] {'ex'}, dimensions={0} | all-to-all | bytes 1572864 | tf_op jit(solution)/shard_map/all_to_all | solution.py:349
  120.0 30.0 %all_to_all.101 = bf16[8,24,2048]{2,1,0:T(8,128)(2,1)} all-to-all(bf16[8,24,2048]{2,1,0:T(8,128)(2,1)S(1)} %get-tuple-element.158), channel_id=1, replica_groups=mesh['ex'=8,'sub'=2,'fsdp'=2] {'ex'}, dimensions={0} | all-to-all | bytes 1572864 | tf_op jit(solution)/shard_map/all_to_all | solution.py:349
  156.7 21.4 %all-to-all-done.3 = bf16[8,64,768]{2,1,0:T(8,128)(2,1)S(1)} async-done(((bf16[8,64,768]{2,1,0:T(8,128)(2,1)}), bf16[8,64,768]{2,1,0:T(8,128)(2,1)S(1)}, u32[]{:S(2)}, u32[]{:S(2)}) %all-to-all-start.3) | async-done | bytes 786464 | tf_op jit(solution)/shard_map/all_to_all | solution.py:349
  189.9 11.1 shard_map.248
  201.0 10.2 shard_map.249
  221.9 25.2 %all-gather.17.cloned.1.call-done = bf16[8,96,2048]{2,1,0:T(8,128)(2,1)} async-done(((bf16[8,24,2048]{2,1,0:T(8,128)(2,1)}), bf16[8,96,2048]{2,1,0:T(8,128)(2,1)}) %all-gather.17.cloned.1.call-update) | async-done | bytes 3145744 | tf_op jit(solution)/shard_map/all_gather | solution.py:400
  251.5 25.6 %all-gather.19.cloned.1.call-done = bf16[8,96,2048]{2,1,0:T(8,128)(2,1)} async-done(((bf16[8,24,2048]{2,1,0:T(8,128)(2,1)}), bf16[8,96,2048]{2,1,0:T(8,128)(2,1)}) %all-gather.19.cloned.1.call-update) | async-done | bytes 3145744 | tf_op jit(solution)/shard_map/all_gather | solution.py:400
  277.1 5.1 multiply_convert_fusion.5
  282.2 24.9 %all-gather.21.cloned.1.call-done = bf16[8,256,768]{2,1,0:T(8,128)(2,1)} async-done(((bf16[8,64,768]{2,1,0:T(8,128)(2,1)}), bf16[8,256,768]{2,1,0:T(8,128)(2,1)}) %all-gather.21.cloned.1.call-update) | async-done | bytes 3145744 | tf_op jit(solution)/shard_map/all_gather | solution.py:400
  310.7 5.6 all-to-all-start.4
  317.7 10.8 all-to-all-done.4
  333.1 30.1 %all_to_all.102 = bf16[8,24,2048]{2,1,0:T(8,128)(2,1)} all-to-all(bf16[8,24,2048]{2,1,0:T(8,128)(2,1)S(1)} %copy-done.26), channel_id=1, replica_groups=mesh['ex'=8,'sub'=2,'fsdp'=2] {'ex'}, dimensions={0} | all-to-all | bytes 1572864 | tf_op jit(solution)/shard_map/all_to_all | solution.py:349
  363.3 32.2 %all_to_all.103 = bf16[8,24,2048]{2,1,0:T(8,128)(2,1)} all-to-all(bf16[8,24,2048]{2,1,0:T(8,128)(2,1)S(1)} %copy-done.27), channel_id=1, replica_groups=mesh['ex'=8,'sub'=2,'fsdp'=2] {'ex'}, dimensions={0} | all-to-all | bytes 1572864 | tf_op jit(solution)/shard_map/all_to_all | solution.py:349
  395.6 23.7 %all_to_all.104 = bf16[8,64,768]{2,1,0:T(8,128)(2,1)} all-to-all(bf16[8,64,768]{2,1,0:T(8,128)(2,1)S(1)} %copy-done.28), channel_id=1, replica_groups=mesh['ex'=8,'sub'=2,'fsdp'=2] {'ex'}, dimensions={0} | all-to-all | bytes 1572864 | tf_op jit(solution)/shard_map/all_to_all | solution.py:349
  421.8 11.0 shard_map.251
  432.9 10.2 shard_map.252
  451.6 9.5 all-to-all-done.5
  465.7 5.5 multiply_convert_fusion.4
  471.2 11.5 all-gather.31.cloned.1.call-done
  486.6 5.9 all-to-all-start.9
  493.9 10.8 all-to-all-done.9
  520.3 9.5 all-to-all-done.10
  529.8 4.7 multiply_convert_fusion.2
  572.3 10.0 shard_map.254.q_ref
  586.5 9.5 shard_map.253
  596.0 19.5 %all-gather.33.cloned.1.call-done.g_ref.stat_ref = bf16[2048,896]{1,0:T(8,128)(2,1)} async-done(((bf16[128,896]{1,0:T(8,128)(2,1)}), bf16[2048,896]{1,0:T(8,128)(2,1)}) %all-gather.33.cloned.1.call-update) | async-done | bytes 3670032 | tf_op jit(solution)/shard_map/all_gather | solution.py:640
  615.5 11.1 shard_map.255
  639.5 9.8 all-to-all-done.12
  666.2 7.9 all-to-all-done.13
  707.4 8.0 concatenate.84
  727.1 9.9 shard_map.257.q_ref
  740.8 9.7 shard_map.256
  752.1 11.0 shard_map.258
  766.4 5.5 all-to-all-start.17
  772.1 4.9 fusion.27
  779.0 7.9 concatenate.83
  786.9 19.9 %reduce-scatter.15.cloned.1.call-done = bf16[8,1,24,2048]{3,2,0,1:T(8,128)(2,1)} async-done(((bf16[8,4,24,2048]{3,2,0,1:T(8,128)(2,1)}), bf16[8,1,24,2048]{3,2,0,1:T(8,128)(2,1)}) %reduce-scatter.15.cloned.1.call-update) | async-done | bytes 786448 | tf_op jit(solution)/shard_map/reduce_scatter | solution.py:580
  806.8 25.7 %all_to_all.105 = bf16[8,24,2048]{2,1,0:T(8,128)(2,1)S(1)} all-to-all(bf16[8,24,2048]{2,1,0:T(8,128)(2,1)} %bitcast.367), channel_id=1, replica_groups=mesh['ex'=8,'sub'=2,'fsdp'=2] {'ex'}, dimensions={0} | all-to-all | bytes 1572864 | tf_op jit(solution)/shard_map/all_to_all | solution.py:349
  832.5 14.9 %reduce-scatter.21.cloned.1.call-done = bf16[8,1,64,768]{3,2,0,1:T(8,128)(2,1)} async-done(((bf16[8,4,64,768]{3,2,0,1:T(8,128)(2,1)}), bf16[8,1,64,768]{3,2,0,1:T(8,128)(2,1)}) %reduce-scatter.21.cloned.1.call-update) | async-done | bytes 786448 | tf_op jit(solution)/shard_map/reduce_scatter | solution.py:580
  847.4 5.5 all-to-all-start.18
  852.9 34.9 %reduce-scatter.17.cloned.1.call-done = bf16[8,1,24,2048]{3,2,0,1:T(8,128)(2,1)} async-done(((bf16[8,4,24,2048]{3,2,0,1:T(8,128)(2,1)}), bf16[8,1,24,2048]{3,2,0,1:T(8,128)(2,1)}) %reduce-scatter.17.cloned.1.call-update) | async-done | bytes 786448 | tf_op jit(solution)/shard_map/reduce_scatter | solution.py:580
  887.7 5.5 all-to-all-start.16
  893.2 105.0 %reduce-scatter.27.cloned.1.call-done = bf16[24,3200]{1,0:T(8,128)(2,1)} async-done(((bf16[768,3200]{1,0:T(8,128)(2,1)}), bf16[24,3200]{1,0:T(8,128)(2,1)}) %reduce-scatter.27.cloned.1.call-update) | async-done | bytes 153616
  1003.4 34.3 %reduce-scatter.13.cloned.1.call-done = bf16[8,1,24,2048]{3,2,0,1:T(8,128)(2,1)} async-done(((bf16[8,4,24,2048]{3,2,0,1:T(8,128)(2,1)}), bf16[8,1,24,2048]{3,2,0,1:T(8,128)(2,1)}) %reduce-scatter.13.cloned.1.call-update) | async-done | bytes 786448 | tf_op jit(solution)/shard_map/reduce_scatter | solution.py:580
  1037.7 5.5 all-to-all-start.14
  1053.1 10.4 all-to-all-done.14
  1066.6 81.6 %reduce-scatter.25.cloned.1.call-done = bf16[24,3200]{1,0:T(8,128)(2,1)} async-done(((bf16[768,3200]{1,0:T(8,128)(2,1)}), bf16[24,3200]{1,0:T(8,128)(2,1)}) %reduce-scatter.25.cloned.1.call-update) | async-done | bytes 153616
  (549 shorter events, 247.5 us)
Async XLA Ops:
  7.2 79.7 %copy-start.33 = (bf16[2,8,24,2048]{3,2,1,0:T(8,128)(2,1)S(1)}, bf16[2,8,24,2048]{3,2,1,0:T(8,128)(2,1)}, u32[]{:S(2)}) copy-start(bf16[2,8,24,2048]{3,2,1,0:T(8,128)(2,1)} %param.23) | copy-start | bytes 4718596
  7.2 74.0 %all-gather.13.cloned.1.call-start = ((), (), s32[]{:S(2)}) async-start(), calls=%async_computation.28 | async-start | bytes 5068800 | tf_op jit(solution)/shard_map/all_gather | solution.py:396
  14.0 175.9 %all-gather.15.cloned.1.call-start = ((), (), s32[]{:S(2)}) async-start(), calls=%async_computation.29 | async-start | bytes 3342336 | tf_op jit(solution)/shard_map/all_gather | solution.py:458
  15.7 69.9 %copy-start.123 = (f32[128]{0:T(128)}, f32[128]{0:T(128)S(1)}, u32[]{:S(2)}) copy-start(f32[128]{0:T(128)S(1)} %fusion.107) | copy-start | bytes 1540
  85.5 132.8 %all-gather.23.cloned.1.call-start = ((), (), s32[]{:S(2)}) async-start(), calls=%async_computation.33 | async-start | bytes 5068800 | tf_op jit(solution)/shard_map/all_gather | solution.py:396
  86.8 160.3 %all-gather.17.cloned.1.call-start = ((), (), s32[]{:S(2)}) async-start(), calls=%async_computation.30 | async-start | bytes 3932160 | tf_op jit(solution)/shard_map/all_gather | solution.py:400
  119.0 158.1 %all-gather.19.cloned.1.call-start = ((), (), s32[]{:S(2)}) async-start(), calls=%async_computation.31 | async-start | bytes 3932160 | tf_op jit(solution)/shard_map/all_gather | solution.py:400
  151.3 26.8 %all-to-all-start.3 = ((bf16[8,64,768]{2,1,0:T(8,128)(2,1)}), bf16[8,64,768]{2,1,0:T(8,128)(2,1)S(1)}, u32[]{:S(2)}, u32[]{:S(2)}) async-start(bf16[8,64,768]{2,1,0:T(8,128)(2,1)} %get-tuple-element.154), calls=%async_computation.3 | async-start | bytes 1572864 | tf_op jit(solution)/shard_map/all_to_all | solution.py:349
  154.9 152.3 %all-gather.21.cloned.1.call-start = ((), (), s32[]{:S(2)}) async-start(), calls=%async_computation.32 | async-start | bytes 3932160 | tf_op jit(solution)/shard_map/all_gather | solution.py:400
  213.1 38.4 %copy-start.22 = (bf16[128,768]{1,0:T(8,128)(2,1)}, bf16[128,768]{1,0:T(8,128)(2,1)S(1)}, u32[]{:S(2)}) copy-start(bf16[128,768]{1,0:T(8,128)(2,1)S(1)} %fusion.50) | copy-start | bytes 589828
  214.2 33.0 %all-to-all-start = ((bf16[8,32,768]{2,1,0:T(8,128)(2,1)}), bf16[8,32,768]{2,1,0:T(8,128)(2,1)S(1)}, u32[]{:S(2)}, u32[]{:S(2)}) async-start(bf16[8,32,768]{2,1,0:T(8,128)(2,1)} %bitcast.14), calls=%async_computation | async-start | bytes 786432 | tf_op jit(solution)/shard_map/all_to_all | solution.py:349
  221.9 94.6 %copy-start.88 = (f32[128]{0:T(128)}, f32[128]{0:T(128)S(1)}, u32[]{:S(2)}) copy-start(f32[128]{0:T(128)S(1)} %get-tuple-element.147) | copy-start | bytes 1540
  247.1 445.9 %copy-start = (bf16[8,32,768]{2,1,0:T(8,128)(2,1)}, bf16[8,32,768]{2,1,0:T(8,128)(2,1)S(1)}, u32[]{:S(2)}) copy-start(bf16[8,32,768]{2,1,0:T(8,128)(2,1)S(1)} %all-to-all-done) | copy-start | bytes 1179652
  310.7 17.7 %all-to-all-start.4 = ((bf16[8,32,768]{2,1,0:T(8,128)(2,1)}), bf16[8,32,768]{2,1,0:T(8,128)(2,1)S(1)}, u32[]{:S(2)}, u32[]{:S(2)}) async-start(bf16[8,32,768]{2,1,0:T(8,128)(2,1)} %bitcast.22), calls=%async_computation.4 | async-start | bytes 786432 | tf_op jit(solution)/shard_map/all_to_all | solution.py:349
  316.4 46.9 %copy-start.27 = (bf16[8,24,2048]{2,1,0:T(8,128)(2,1)S(1)}, bf16[8,24,2048]{2,1,0:T(8,128)(2,1)}, u32[]{:S(2)}) copy-start(bf16[8,24,2048]{2,1,0:T(8,128)(2,1)} %get-tuple-element.157) | copy-start | bytes 2359300
  316.4 105.5 %all-gather.25.cloned.1.call-start = ((), (), s32[]{:S(2)}) async-start(), calls=%async_computation.34 | async-start | bytes 3342336 | tf_op jit(solution)/shard_map/all_gather | solution.py:458
  333.0 118.6 %all-gather.27.cloned.1.call-start = ((), (), s32[]{:S(2)}) async-start(), calls=%async_computation.35 | async-start | bytes 3932160 | tf_op jit(solution)/shard_map/all_gather | solution.py:400
  363.3 102.5 %all-gather.29.cloned.1.call-start = ((), (), s32[]{:S(2)}) async-start(), calls=%async_computation.36 | async-start | bytes 3932160 | tf_op jit(solution)/shard_map/all_gather | solution.py:400
  395.6 87.1 %all-gather.31.cloned.1.call-start = ((), (), s32[]{:S(2)}) async-start(), calls=%async_computation.37 | async-start | bytes 3932160 | tf_op jit(solution)/shard_map/all_gather | solution.py:400
  446.0 15.1 %all-to-all-start.5 = ((bf16[8,32,768]{2,1,0:T(8,128)(2,1)}), bf16[8,32,768]{2,1,0:T(8,128)(2,1)S(1)}, u32[]{:S(2)}, u32[]{:S(2)}) async-start(bf16[8,32,768]{2,1,0:T(8,128)(2,1)} %bitcast.39), calls=%async_computation.5 | async-start | bytes 786432 | tf_op jit(solution)/shard_map/all_to_all | solution.py:349
  486.6 18.0 %all-to-all-start.9 = ((bf16[8,32,768]{2,1,0:T(8,128)(2,1)}), bf16[8,32,768]{2,1,0:T(8,128)(2,1)S(1)}, u32[]{:S(2)}, u32[]{:S(2)}) async-start(bf16[8,32,768]{2,1,0:T(8,128)(2,1)} %bitcast.47), calls=%async_computation.9 | async-start | bytes 786432 | tf_op jit(solution)/shard_map/all_to_all | solution.py:349
  514.1 15.7 %all-to-all-start.10 = ((bf16[8,32,768]{2,1,0:T(8,128)(2,1)}), bf16[8,32,768]{2,1,0:T(8,128)(2,1)}, u32[]{:S(2)}, u32[]{:S(2)}) async-start(bf16[8,32,768]{2,1,0:T(8,128)(2,1)} %bitcast.371), calls=%async_computation.10 | async-start | bytes 786432 | tf_op jit(solution)/shard_map/all_to_all | solution.py:349
  538.9 19.1 %all-to-all-start.11 = ((bf16[8,32,768]{2,1,0:T(8,128)(2,1)}), bf16[8,32,768]{2,1,0:T(8,128)(2,1)}, u32[]{:S(2)}, u32[]{:S(2)}) async-start(bf16[8,32,768]{2,1,0:T(8,128)(2,1)} %bitcast.370), calls=%async_computation.11 | async-start | bytes 786432 | tf_op jit(solution)/shard_map/all_to_all | solution.py:349
  543.0 72.5 %all-gather.33.cloned.1.call-start = ((), (), s32[]{:S(2)}) async-start(), calls=%async_computation.38 | async-start | bytes 3899392 | tf_op jit(solution)/shard_map/all_gather | solution.py:640
  567.5 154.0 %reduce-scatter.23.cloned.1.call-start = ((), (), s32[]{:S(2)}) async-start(), calls=%async_computation.45 | async-start | bytes 3932160 | tf_op jit(solution)/shard_map/reduce_scatter | solution.py:580
  633.2 16.1 %all-to-all-start.12 = ((bf16[8,32,768]{2,1,0:T(8,128)(2,1)}), bf16[8,32,768]{2,1,0:T(8,128)(2,1)S(1)}, u32[]{:S(2)}, u32[]{:S(2)}) async-start(bf16[8,32,768]{2,1,0:T(8,128)(2,1)} %bitcast.70), calls=%async_computation.12 | async-start | bytes 786432 | tf_op jit(solution)/shard_map/all_to_all | solution.py:349
  658.6 15.4 %all-to-all-start.13 = ((bf16[8,32,768]{2,1,0:T(8,128)(2,1)}), bf16[8,32,768]{2,1,0:T(8,128)(2,1)S(1)}, u32[]{:S(2)}, u32[]{:S(2)}) async-start(bf16[8,32,768]{2,1,0:T(8,128)(2,1)} %bitcast.72), calls=%async_computation.13 | async-start | bytes 786432 | tf_op jit(solution)/shard_map/all_to_all | solution.py:349
  662.2 89.9 %all-gather.35.cloned.1.call-start = ((), (), s32[]{:S(2)}) async-start(), calls=%async_computation.39 | async-start | bytes 3899392 | tf_op jit(solution)/shard_map/all_gather | solution.py:640
  680.1 86.3 %reduce-scatter.19.cloned.1.call-start = ((), (), s32[]{:S(2)}) async-start(), calls=%async_computation.43 | async-start | bytes 3932160 | tf_op jit(solution)/shard_map/reduce_scatter | solution.py:580
  684.5 122.4 %reduce-scatter.15.cloned.1.call-start = ((), (), s32[]{:S(2)}) async-start(), calls=%async_computation.41 | async-start | bytes 3932160 | tf_op jit(solution)/shard_map/reduce_scatter | solution.py:580
  688.7 158.6 %reduce-scatter.21.cloned.1.call-start = ((), (), s32[]{:S(2)}) async-start(), calls=%async_computation.44 | async-start | bytes 3932160 | tf_op jit(solution)/shard_map/reduce_scatter | solution.py:580
  693.0 194.7 %reduce-scatter.17.cloned.1.call-start = ((), (), s32[]{:S(2)}) async-start(), calls=%async_computation.42 | async-start | bytes 3932160 | tf_op jit(solution)/shard_map/reduce_scatter | solution.py:580
  697.4 300.8 %reduce-scatter.27.cloned.1.call-start = ((), (), s32[]{:S(2)}) async-start(), calls=%async_computation.47 | async-start | bytes 5068800
  715.4 322.3 %reduce-scatter.13.cloned.1.call-start = ((), (), s32[]{:S(2)}) async-start(), calls=%async_computation.40 | async-start | bytes 3932160 | tf_op jit(solution)/shard_map/reduce_scatter | solution.py:580
  721.5 44.9 %all-to-all-start.19 = ((bf16[8,64,768]{2,1,0:T(8,128)(2,1)}), bf16[8,64,768]{2,1,0:T(8,128)(2,1)S(1)}, u32[]{:S(2)}, u32[]{:S(2)}) async-start(bf16[8,64,768]{2,1,0:T(8,128)(2,1)} %bitcast.364), calls=%async_computation.25 | async-start | bytes 1572864 | tf_op jit(solution)/shard_map/all_to_all | solution.py:349
  766.4 40.4 %all-to-all-start.17 = ((bf16[8,24,2048]{2,1,0:T(8,128)(2,1)}), bf16[8,24,2048]{2,1,0:T(8,128)(2,1)}, u32[]{:S(2)}, u32[]{:S(2)}) async-start(bf16[8,24,2048]{2,1,0:T(8,128)(2,1)} %bitcast.366), calls=%async_computation.21 | async-start | bytes 1572864 | tf_op jit(solution)/shard_map/all_to_all | solution.py:349
  771.9 376.3 %reduce-scatter.25.cloned.1.call-start = ((), (), s32[]{:S(2)}) async-start(), calls=%async_computation.46 | async-start | bytes 5068800
  832.5 213.8 %copy-start.6 = (f32[128,768]{1,0:T(8,128)S(1)}, f32[128,768]{1,0:T(8,128)}, u32[]{:S(2)}) copy-start(f32[128,768]{1,0:T(8,128)} %copy-done.4) | copy-start | bytes 1179652
  847.4 40.4 %all-to-all-start.18 = ((bf16[8,64,768]{2,1,0:T(8,128)(2,1)}), bf16[8,64,768]{2,1,0:T(8,128)(2,1)S(1)}, u32[]{:S(2)}, u32[]{:S(2)}) async-start(bf16[8,64,768]{2,1,0:T(8,128)(2,1)} %bitcast.368), calls=%async_computation.23 | async-start | bytes 1572864 | tf_op jit(solution)/shard_map/all_to_all | solution.py:349
  852.9 195.4 %copy-start.18 = (bf16[8,64,768]{2,1,0:T(8,128)(2,1)S(1)}, bf16[8,64,768]{2,1,0:T(8,128)(2,1)}, u32[]{:S(2)}) copy-start(bf16[8,64,768]{2,1,0:T(8,128)(2,1)} %copy-done.17) | copy-start | bytes 2359300
  887.7 150.0 %all-to-all-start.16 = ((bf16[8,24,2048]{2,1,0:T(8,128)(2,1)}), bf16[8,24,2048]{2,1,0:T(8,128)(2,1)S(1)}, u32[]{:S(2)}, u32[]{:S(2)}) async-start(bf16[8,24,2048]{2,1,0:T(8,128)(2,1)} %bitcast.365), calls=%async_computation.19 | async-start | bytes 1572864 | tf_op jit(solution)/shard_map/all_to_all | solution.py:349
  1037.7 25.8 %all-to-all-start.14 = ((bf16[8,24,2048]{2,1,0:T(8,128)(2,1)}), bf16[8,24,2048]{2,1,0:T(8,128)(2,1)}, u32[]{:S(2)}, u32[]{:S(2)}) async-start(bf16[8,24,2048]{2,1,0:T(8,128)(2,1)} %bitcast.369), calls=%async_computation.15 | async-start | bytes 1572864 | tf_op jit(solution)/shard_map/all_to_all | solution.py:349
  1053.1 98.7 %copy-start.121 = (f32[24,2]{0,1:T(2,128)S(1)}, f32[24,2]{0,1:T(2,128)}, u32[]{:S(2)}) copy-start(f32[24,2]{0,1:T(2,128)} %copy.315) | copy-start | bytes 580
  1053.1 99.3 %copy-start.109 = (f32[24,4]{0,1:T(4,128)S(1)}, f32[24,4]{0,1:T(4,128)}, u32[]{:S(2)}) copy-start(f32[24,4]{0,1:T(4,128)} %copy.313) | copy-start | bytes 1156
  1053.1 99.9 %copy-start.126 = (f32[24]{0:T(128)S(1)}, f32[24]{0:T(128)}, u32[]{:S(2)}) copy-start(f32[24]{0:T(128)} %get-tuple-element.125) | copy-start | bytes 292
  1053.1 100.5 %copy-start.125 = (f32[24]{0:T(128)S(1)}, f32[24]{0:T(128)}, u32[]{:S(2)}) copy-start(f32[24]{0:T(128)} %get-tuple-element.126) | copy-start | bytes 292
  1053.1 101.0 %copy-start.45 = (f32[1,24,2304]{2,1,0:T(8,128)S(1)}, f32[1,24,2304]{2,1,0:T(8,128)}, u32[]{:S(2)}) copy-start(f32[1,24,2304]{2,1,0:T(8,128)} %slice_bitcast_fusion.6) | copy-start | bytes 663556
  1063.5 91.5 %copy-start.56 = (f32[1,24,768]{2,1,0:T(8,128)S(1)}, f32[1,24,768]{2,1,0:T(8,128)}, u32[]{:S(2)}) copy-start(f32[1,24,768]{2,1,0:T(8,128)} %slice_bitcast_fusion.10) | copy-start | bytes 221188
  (126 other events, 1131.0 us)
Sparse Core Ops, SparseCore 0:
  14.1 67.0 all-gather.12
  85.6 59.4 all-gather.14
  148.7 69.5 all-gather.22
  219.7 27.3 all-gather.16
  248.5 28.5 all-gather.18
  278.5 28.5 all-gather.20
  333.2 60.8 all-gather.24
  395.6 26.9 all-gather.26
  424.1 28.5 all-gather.28
  454.1 28.5 all-gather.30
  567.6 47.8 all-gather.32
  617.9 36.9 reduce-scatter.22
  680.2 46.6 all-gather.34
  729.4 36.9 reduce-scatter.18
  768.8 37.9 reduce-scatter.14
  809.4 37.9 reduce-scatter.20
  849.7 37.9 reduce-scatter.16
  894.3 103.9 reduce-scatter.26
  1000.8 36.8 reduce-scatter.12
  1044.2 103.9 reduce-scatter.24

commit v2 on v1

v2 whole, which is shorter than its diff:
```python
import functools

import jax
import jax.numpy as jnp
from jax import lax
from jax.experimental import pallas as pl
from jax.experimental.pallas import tpu as pltpu
from jax.sharding import Mesh
from jax.sharding import PartitionSpec as P

HEADS = 12
HEAD_DIM = 64
EXPERTS = 8
TOP = 2
LAYERS = 2
ROUTED = 12
CAP = 26
SLOTS = 32
LANES = 128
PAIRS = HEADS // 2

FS = "fsdp"


def ctx_axes(size):
    return tuple(f"ctx{at}" for at in range(size.bit_length() - 1))


norm_eps = 1e-06
masked_score = -1e30
highest = lax.Precision.HIGHEST
f32 = jnp.float32
bf16 = jnp.bfloat16
VMEM_LIMIT = 56 * 1024 * 1024

AT_CONST = 16
AT_CVEC = 24
AT_ATTN = 32
AT_MOE = 33


def dot_nn(a, b):
    return lax.dot_general(a, b, (((1,), (0,)), ((), ())), preferred_element_type=f32)


def dot_nt(a, b):
    return lax.dot_general(a, b, (((1,), (1,)), ((), ())), preferred_element_type=f32)


def dot_tn(a, b):
    return lax.dot_general(a, b, (((0,), (0,)), ((), ())), preferred_element_type=f32)


def kernel_params(steps):
    return pltpu.CompilerParams(
        dimension_semantics=("arbitrary",) * steps, vmem_limit_bytes=VMEM_LIMIT
    )


def turn_lanes(x, cosine, sine):
    lane = lax.broadcasted_iota(jnp.int32, x.shape, 1)
    ahead = pltpu.roll(x, LANES - HEAD_DIM // 2, 1)
    behind = pltpu.roll(x, HEAD_DIM // 2, 1)
    partner = jnp.where(lane % HEAD_DIM < HEAD_DIM // 2, ahead, behind)
    return x * cosine + partner * sine


def project_kernel(turned, a_ref, *refs):
    count = len(turned)
    w_refs = refs[:count]
    cos_ref, sin_ref = refs[count : count + 2]
    out_refs = refs[count + 2 :]
    a = a_ref[...]
    for w_ref, out_ref, turn in zip(w_refs, out_refs, turned):
        acc = dot_nn(a, w_ref[...])
        if not turn:
            out_ref[...] = acc.astype(bf16)
            continue
        for at in range(0, acc.shape[1], LANES):
            part = turn_lanes(acc[:, at : at + LANES], cos_ref[...], sin_ref[...])
            out_ref[:, at : at + LANES] = part.astype(bf16)


def project(rows, packed, columns, turned, cosine, sine):
    count, width = rows.shape
    tile = min(count, 512)
    w_specs = [
        pl.BlockSpec((width, width), functools.partial(lambda at, i: (0, at), at))
        for at in columns
    ]
    row_spec = pl.BlockSpec((tile, width), lambda i: (i, 0))
    table = pl.BlockSpec((tile, LANES), lambda i: (i, 0))
    return pl.pallas_call(
        functools.partial(project_kernel, turned),
        grid=(count // tile,),
        in_specs=[row_spec] + w_specs + [table, table],
        out_specs=[row_spec] * len(columns),
        out_shape=[jax.ShapeDtypeStruct((count, width), bf16)] * len(columns),
        compiler_params=kernel_params(1),
        cost_estimate=pl.CostEstimate(
            flops=2 * count * width * width * len(columns),
            bytes_accessed=2 * width * (count * (1 + len(columns)) + width * len(columns)),
            transcendentals=0,
        ),
    )(rows, *([packed] * len(columns)), cosine, sine)


def split_heads(x):
    wide = x.astype(f32)
    left = lax.broadcasted_iota(jnp.int32, wide.shape, 1) < HEAD_DIM
    zero = jnp.zeros_like(wide)
    return jnp.concatenate(
        [jnp.where(left, wide, zero), jnp.where(left, zero, wide)], axis=0
    ).astype(bf16)


def join_heads(x, rows):
    left = lax.broadcasted_iota(jnp.int32, (rows, LANES), 1) < HEAD_DIM
    return jnp.where(left, x[:rows], x[rows:])


def attend_kernel(
    prompt, q_ref, k_ref, v_ref, at_ref, start_ref, key_ref, o_ref, total_ref, bias_ref
):
    pair = pl.program_id(0)
    rows = q_ref.shape[0]

    @pl.when(pair == 0)
    def _():
        places, keys = at_ref[...], key_ref[...]
        seen = (keys <= places) & ((keys < prompt) | (keys >= start_ref[...]))
        bias_ref[...] = jnp.where(seen, 0.0, masked_score)
        total_ref[...] = jnp.zeros_like(total_ref)

    queries = split_heads(q_ref[...] * HEAD_DIM ** (-0.5))
    keys, values = k_ref[...], v_ref[...]
    lane = lax.broadcasted_iota(jnp.int32, (rows, LANES), 1)
    outs = []
    totals = total_ref[...]
    for side in range(2):
        scores = dot_nt(queries[side * rows : (side + 1) * rows], keys) + bias_ref[...]
        top = jnp.max(scores, axis=1, keepdims=True)
        expo = jnp.exp(scores - top)
        total = jnp.sum(expo, axis=1, keepdims=True)
        outs.append(dot_nn(expo.astype(bf16), values) / total)
        totals = jnp.where(lane == 2 * pair + side, top + jnp.log(total), totals)
    o_ref[...] = jnp.where(lane < HEAD_DIM, outs[0], outs[1])
    total_ref[...] = totals


def attend(queries, keys, values, places, starts, key_places, prompt):
    rows, width = places.shape[0], queries.shape[1]
    length = keys.shape[0]
    own = pl.BlockSpec((rows, LANES), lambda j: (0, j))
    every = pl.BlockSpec((length, LANES), lambda j: (0, j))
    column = pl.BlockSpec((rows, 1), lambda j: (0, 0))
    line = pl.BlockSpec((1, length), lambda j: (0, 0))
    return pl.pallas_call(
        functools.partial(attend_kernel, prompt),
        grid=(PAIRS,),
        in_specs=[own, every, every, column, column, line],
        out_specs=[own, pl.BlockSpec((rows, LANES), lambda j: (0, 0))],
        out_shape=[
            jax.ShapeDtypeStruct((rows, width), f32),
            jax.ShapeDtypeStruct((rows, LANES), f32),
        ],
        scratch_shapes=[pltpu.VMEM((rows, length), f32)],
        compiler_params=kernel_params(1),
        cost_estimate=pl.CostEstimate(
            flops=8 * rows * length * width,
            bytes_accessed=4 * length * width,
            transcendentals=rows * length * HEADS,
        ),
    )(queries, keys, values, places, starts, key_places)


def pick_column(table, at):
    lane = lax.broadcasted_iota(jnp.int32, table.shape, 1)
    return jnp.sum(jnp.where(lane == at, table, 0.0), axis=1, keepdims=True)


def query_kernel(
    prompt,
    start,
    q_ref,
    g_ref,
    k_ref,
    v_ref,
    total_ref,
    delta_ref,
    at_ref,
    start_ref,
    key_ref,
    cos_ref,
    sin_ref,
    out_ref,
    bias_ref,
):
    pair = pl.program_id(0) + start
    rows = q_ref.shape[0]

    @pl.when(pair == start)
    def _():
        places, keys = at_ref[...], key_ref[...]
        seen = (keys <= places) & ((keys < prompt) | (keys >= start_ref[...]))
        bias_ref[...] = jnp.where(seen, 0.0, masked_score)

    scale = HEAD_DIM ** (-0.5)
    queries = split_heads(q_ref[...] * scale)
    grads = split_heads(g_ref[...])
    keys, values = k_ref[...], v_ref[...]
    lane = lax.broadcasted_iota(jnp.int32, (rows, LANES), 1)
    outs = []
    for side in range(2):
        part = slice(side * rows, (side + 1) * rows)
        total = pick_column(total_ref[...], 2 * pair + side)
        delta = pick_column(delta_ref[...], 2 * pair + side)
        scores = dot_nt(queries[part], keys) + bias_ref[...]
        probs = jnp.exp(scores - total)
        prob_grad = dot_nt(grads[part], values)
        score_grad = (probs * (prob_grad - delta)).astype(bf16)
        outs.append(dot_nn(score_grad, keys))
    out = jnp.where(lane < HEAD_DIM, outs[0], outs[1]) * scale
    out_ref[...] = turn_lanes(out, cos_ref[...], -sin_ref[...]).astype(bf16)


def query_back(
    start, count, queries, grads, keys, values, totals, delta, places, starts, key_places, cosine, sine, prompt
):
    rows = places.shape[0]
    length = keys.shape[0]
    own = pl.BlockSpec((rows, LANES), lambda j: (0, j + start))
    every = pl.BlockSpec((length, LANES), lambda j: (0, j + start))
    same = pl.BlockSpec((rows, LANES), lambda j: (0, 0))
    column = pl.BlockSpec((rows, 1), lambda j: (0, 0))
    line = pl.BlockSpec((1, length), lambda j: (0, 0))
    width = count * LANES
    return pl.pallas_call(
        functools.partial(query_kernel, prompt, start),
        grid=(count,),
        in_specs=[own, own, every, every, same, same, column, column, line, same, same],
        out_specs=pl.BlockSpec((rows, LANES), lambda j: (0, j)),
        out_shape=jax.ShapeDtypeStruct((rows, width), bf16),
        scratch_shapes=[pltpu.VMEM((rows, length), f32)],
        compiler_params=kernel_params(1),
        cost_estimate=pl.CostEstimate(
            flops=12 * rows * length * width,
            bytes_accessed=4 * length * width,
            transcendentals=rows * length * HEADS,
        ),
    )(queries, grads, keys, values, totals, delta, places, starts, key_places, cosine, sine)


def key_kernel(
    prompt,
    k_ref,
    v_ref,
    q_ref,
    g_ref,
    stat_ref,
    own_ref,
    at_ref,
    start_ref,
    cos_ref,
    sin_ref,
    dk_ref,
    dv_ref,
    bias_ref,
    lines_ref,
):
    pair = pl.program_id(0)
    rows = k_ref.shape[0]

    @pl.when(pair == 0)
    def _():
        keys, places = own_ref[...], at_ref[...]
        seen = (keys <= places) & ((keys < prompt) | (keys >= start_ref[...]))
        bias_ref[...] = jnp.where(seen, 0.0, masked_score)
        flat = stat_ref[...].astype(f32).T
        for head in range(HEADS):
            lines_ref[head] = flat[head : head + 1] + flat[16 + head : 17 + head]
            lines_ref[16 + head] = flat[32 + head : 33 + head] + flat[48 + head : 49 + head]

    scale = HEAD_DIM ** (-0.5)
    own_keys = split_heads(k_ref[...] * scale)
    own_values = split_heads(v_ref[...])
    queries, grads = q_ref[...], g_ref[...]
    lane = lax.broadcasted_iota(jnp.int32, (rows, LANES), 1)
    key_outs, value_outs = [], []
    for side in range(2):
        part = slice(side * rows, (side + 1) * rows)
        total = lines_ref[2 * pair + side]
        delta = lines_ref[16 + 2 * pair + side]
        scores = dot_nt(own_keys[part], queries) + bias_ref[...]
        probs = jnp.exp(scores - total)
        value_outs.append(dot_nn(probs.astype(bf16), grads))
        prob_grad = dot_nt(own_values[part], grads)
        score_grad = (probs * (prob_grad - delta)).astype(bf16)
        key_outs.append(dot_nn(score_grad, queries))
    left = lane < HEAD_DIM
    dk = jnp.where(left, key_outs[0], key_outs[1]) * scale
    dk_ref[...] = turn_lanes(dk, cos_ref[...], -sin_ref[...]).astype(bf16)
    dv_ref[...] = jnp.where(left, value_outs[0], value_outs[1]).astype(bf16)


def key_back(own_keys, own_values, queries, sent, own_places, places, starts, cosine, sine, prompt):
    rows = own_places.shape[0]
    length, width = queries.shape
    own = pl.BlockSpec((rows, LANES), lambda j: (0, j))
    every = pl.BlockSpec((length, LANES), lambda j: (0, j))
    stats = pl.BlockSpec((length, LANES), lambda j: (0, PAIRS))
    same = pl.BlockSpec((rows, LANES), lambda j: (0, 0))
    column = pl.BlockSpec((rows, 1), lambda j: (0, 0))
    line = pl.BlockSpec((1, length), lambda j: (0, 0))
    return pl.pallas_call(
        functools.partial(key_kernel, prompt),
        grid=(PAIRS,),
        in_specs=[own, own, every, every, stats, column, line, line, same, same],
        out_specs=[own, own],
        out_shape=[jax.ShapeDtypeStruct((rows, width), bf16)] * 2,
        scratch_shapes=[
            pltpu.VMEM((rows, length), f32),
            pltpu.VMEM((32, 1, length), f32),
        ],
        compiler_params=kernel_params(1),
        cost_estimate=pl.CostEstimate(
            flops=16 * rows * length * width,
            bytes_accessed=4 * length * width,
            transcendentals=rows * length * HEADS,
        ),
    )(own_keys, own_values, queries, sent, sent, own_places, places, starts, cosine, sine)


def cross(x, flag_ref):
    tall = x.shape[0]
    far = jnp.full((tall, LANES), flag_ref[0, 0], jnp.int32) > 0
    near = jnp.full((tall, LANES), flag_ref[0, 1], jnp.int32) > 0
    left, right = x[:, :LANES], x[:, LANES:]
    left = jnp.where(near, pltpu.roll(left, HEAD_DIM, 1), left)
    right = jnp.where(near, pltpu.roll(right, HEAD_DIM, 1), right)
    return jnp.concatenate(
        [jnp.where(far, right, left), jnp.where(far, left, right)], axis=1
    )


def stack_rows(refs):
    return jnp.concatenate([ref[...] for ref in refs], axis=0)


def expert_kernel(flag_ref, x_ref, *refs):
    gates, ups, downs = refs[:4], refs[4:8], refs[8:12]
    gate_ref, up_ref, out_ref, acc_ref = refs[12:]
    step = pl.program_id(0)
    x = x_ref[...]
    gate = dot_nn(x, stack_rows(gates))
    up = dot_nn(x, stack_rows(ups))
    gate_ref[...] = gate
    up_ref[...] = up
    inner = cross(gate * jax.nn.sigmoid(gate) * up, flag_ref).astype(bf16)
    out = dot_nn(inner, stack_rows(downs))

    @pl.when(step == 0)
    def _():
        acc_ref[...] = out

    @pl.when(step > 0)
    def _():
        acc_ref[...] += out

    @pl.when(step == pl.num_programs(0) - 1)
    def _():
        out_ref[...] = acc_ref[...].astype(bf16)


def expert_specs(width, hidden):
    tile = hidden // EXPERTS
    tall = pl.BlockSpec((width // 4, tile), lambda j: (0, j))
    flat = pl.BlockSpec((tile // 4, width), lambda j: (j, 0))
    return tile, [tall] * 8 + [flat] * 4


def run_expert(flags, x, gates, ups, downs):
    rows, width = x.shape
    hidden = gates[0].shape[1]
    tile, specs = expert_specs(width, hidden)
    whole = pl.BlockSpec((rows, width), lambda j: (0, 0))
    column = pl.BlockSpec((rows, tile), lambda j: (0, j))
    return pl.pallas_call(
        expert_kernel,
        grid=(EXPERTS,),
        in_specs=[pl.BlockSpec(memory_space=pltpu.SMEM), whole] + specs,
        out_specs=[column, column, whole],
        out_shape=[
            jax.ShapeDtypeStruct((rows, hidden), f32),
            jax.ShapeDtypeStruct((rows, hidden), f32),
            jax.ShapeDtypeStruct((rows, width), bf16),
        ],
        scratch_shapes=[pltpu.VMEM((rows, width), f32)],
        compiler_params=kernel_params(1),
        cost_estimate=pl.CostEstimate(
            flops=6 * rows * width * hidden,
            bytes_accessed=6 * width * hidden + 8 * rows * hidden,
            transcendentals=rows * hidden,
        ),
    )(flags, x, *gates, *ups, *downs)


def expert_back_kernel(both, flag_ref, x_ref, grad_ref, order_ref, *refs):
    if not both:
        gate_ref, up_ref = refs[:2]
        refs = refs[2:]
    gates, ups, downs = refs[:4], refs[4:8], refs[8:12]
    outs, back_ref = refs[12:18], refs[18]
    acc_ref, turned_ref = refs[19:21]
    step = pl.program_id(0)
    last = step == pl.num_programs(0) - 1
    width = x_ref.shape[1]

    @pl.when(step == 0)
    def _():
        turned_ref[...] = x_ref[...].astype(f32).T.astype(bf16)

    grad = grad_ref[...]
    gate_w, up_w, down_w = stack_rows(gates), stack_rows(ups), stack_rows(downs)
    if both:
        x = x_ref[...]
        gate, up = dot_nn(x, gate_w), dot_nn(x, up_w)
    else:
        gate, up = gate_ref[...], up_ref[...]
    sigma = jax.nn.sigmoid(gate)
    gated = gate * sigma
    inner = cross(gated * up, flag_ref)
    inner_grad = cross(dot_nt(grad, down_w), flag_ref)
    up_low = (inner_grad * gated).astype(bf16)
    gate_low = (inner_grad * up * (sigma + gated * (1.0 - sigma))).astype(bf16)
    parts = [dot_nt(gate_low, gate_w) + dot_nt(up_low, up_w)]
    if both:
        parts.append(dot_nn(inner.astype(bf16), down_w))
    part = jnp.concatenate(parts, axis=1) if both else parts[0]

    @pl.when(step == 0)
    def _():
        acc_ref[...] = part

    @pl.when(step > 0)
    def _():
        acc_ref[...] += part

    @pl.when(last)
    def _():
        in_low = acc_ref[:, :width].astype(bf16)
        back_ref[:, :width] = dot_nt(in_low, order_ref[...]).astype(bf16)
        if both:
            back_ref[:, width:] = acc_ref[:, width:].astype(bf16)

    turned = turned_ref[...]
    members = (
        dot_nn(turned, gate_low).astype(bf16),
        dot_nn(turned, up_low).astype(bf16),
        dot_nn(inner.T.astype(bf16), grad).astype(bf16),
    )
    for at, member in enumerate(members):
        half = member.shape[0] // 2
        outs[2 * at][...] = member[:half]
        outs[2 * at + 1][...] = member[half:]


def run_expert_back(flags, received, order, gate, up, gates, ups, downs):
    both = gate is None
    if both:
        rows, width = received[0].shape[0], received[0].shape[1] // 2
    else:
        rows, width = received[0].shape
    hidden = gates[0].shape[1]
    tile, specs = expert_specs(width, hidden)
    first = pl.BlockSpec((rows, width), lambda j: (0, 0))
    beside = pl.BlockSpec((rows, width), lambda j: (0, 1)) if both else first
    table = pl.BlockSpec((width, width), lambda j: (0, 0))
    column = pl.BlockSpec((rows, tile), lambda j: (0, j))
    tall = pl.BlockSpec((width // 2, tile), lambda j: (0, j))
    flat = pl.BlockSpec((None, tile // 2, width), lambda j: (j, 0, 0))
    tall_shape = jax.ShapeDtypeStruct((width // 2, hidden), bf16)
    flat_shape = jax.ShapeDtypeStruct((EXPERTS, tile // 2, width), bf16)
    wide = 2 * width if both else width
    *halves, back = pl.pallas_call(
        functools.partial(expert_back_kernel, both),
        grid=(EXPERTS,),
        in_specs=[pl.BlockSpec(memory_space=pltpu.SMEM), first, beside, table]
        + ([] if both else [column, column])
        + specs,
        out_specs=[tall] * 4 + [flat] * 2 + [pl.BlockSpec((rows, wide), lambda j: (0, 0))],
        out_shape=[tall_shape] * 4
        + [flat_shape] * 2
        + [jax.ShapeDtypeStruct((rows, wide), bf16)],
        scratch_shapes=[pltpu.VMEM((rows, wide), f32), pltpu.VMEM((width, rows), bf16)],
        compiler_params=kernel_params(1),
        cost_estimate=pl.CostEstimate(
            flops=(18 if both else 12) * rows * width * hidden,
            bytes_accessed=12 * width * hidden + 8 * rows * hidden,
            transcendentals=rows * hidden,
        ),
    )(flags, *received, order, *([] if both else [gate, up]), *gates, *ups, *downs)
    return halves, back


def product_kernel(x_ref, g_ref, *refs):
    thin_ref = refs[0] if len(refs) == 3 else None
    kept_ref, given_ref = refs[-2:]
    turned = x_ref[...].astype(f32).T.astype(bf16)
    half = turned.shape[0] // 2
    wide = g_ref.shape[1]
    span = turned.shape[0]
    for at in range(0, wide, span):
        part = dot_nn(turned, g_ref[:, at : at + span]).astype(bf16)
        kept_ref[:, at : at + span] = part[:half]
        given_ref[:, at : at + span] = part[half:]
    if thin_ref is not None:
        kept_ref[:, wide:] = thin_ref[:half]
        given_ref[:, wide:] = thin_ref[half:]


def weight_product(x, grad, thin=None):
    rows, width = x.shape
    wide = grad.shape[1] + (0 if thin is None else thin.shape[1])
    shape = jax.ShapeDtypeStruct((width // 2, wide), bf16)
    vmem = pl.BlockSpec(memory_space=pltpu.VMEM)
    return pl.pallas_call(
        product_kernel,
        in_specs=[vmem] * (2 if thin is None else 3),
        out_specs=[vmem] * 2,
        out_shape=[shape] * 2,
        compiler_params=pltpu.CompilerParams(vmem_limit_bytes=VMEM_LIMIT),
        cost_estimate=pl.CostEstimate(
            flops=2 * rows * width * wide,
            bytes_accessed=2 * (width * wide + rows * (width + wide)),
            transcendentals=0,
        ),
    )(x, grad, *([] if thin is None else [thin]))


def lanes_of(rows):
    return lax.broadcasted_iota(jnp.int32, (rows, LANES), 1)


def two_part_nn(a, b):
    top = a.astype(bf16)
    return dot_nn(top, b) + dot_nn((a - top.astype(f32)).astype(bf16), b)


def two_part_nt(a, b):
    top = a.astype(bf16)
    return dot_nt(top, b) + dot_nt((a - top.astype(f32)).astype(bf16), b)


def root_scale(x):
    return lax.rsqrt(jnp.mean(x * x, axis=1, keepdims=True) + norm_eps)


def line_of(small_ref, at):
    return small_ref[...].astype(f32).T[at : at + 1]


def norm_kernel(x_ref, small_ref, out_ref, line_ref):
    @pl.when(pl.program_id(0) == 0)
    def _():
        line_ref[...] = line_of(small_ref, AT_ATTN)

    x = x_ref[...].astype(f32)
    out_ref[...] = (x * root_scale(x) * line_ref[...]).astype(bf16)


def norm_rows(x, packed):
    count, width = x.shape
    tile = min(count, 512)
    spec = pl.BlockSpec((tile, width), lambda i: (i, 0))
    return pl.pallas_call(
        norm_kernel,
        grid=(count // tile,),
        in_specs=[spec, pl.BlockSpec((width, LANES), lambda i: (0, 3 * width // LANES))],
        out_specs=spec,
        out_shape=jax.ShapeDtypeStruct((count, width), bf16),
        scratch_shapes=[pltpu.VMEM((1, width), f32)],
        compiler_params=kernel_params(1),
        cost_estimate=pl.CostEstimate(
            flops=8 * count * width, bytes_accessed=4 * count * width, transcendentals=0
        ),
    )(x, packed)


def pair_partner(x):
    lane = lanes_of(x.shape[0])
    return jnp.where(lane % 2 == 0, pltpu.roll(x, LANES - 1, 1), pltpu.roll(x, 1, 1))


def side_weights(chances, mixes, chosen):
    weight = chances * chosen
    last = [pick_column(weight, 9 + at) for at in range(3)]
    mix = [pick_column(mixes, AT_CONST + at) for at in range(4)]
    alpha = last[0] + last[1] * mix[0] + last[2] * mix[2]
    return last, mix, alpha, (last[1] * mix[1], last[2] * mix[3])


def slots_of_grad(grad, chances, picks, slot_pairs):
    parts = [jnp.sum(chances * pick, axis=1, keepdims=True) * grad for pick in picks]
    return dot_nn(slot_pairs, jnp.concatenate(parts, axis=0).astype(bf16)).astype(bf16)


def to_expert_kernel(
    final,
    att_ref,
    hidden_ref,
    wout_ref,
    small_ref,
    previous_ref,
    slot_tokens_ref,
    order_ref,
    *refs,
):
    if final:
        grad_ref, first_ref, second_ref, slot_pairs_ref = refs[:4]
        refs = refs[4:]
    mid_ref, logit_ref, chance_ref, mix_ref, message_ref = refs
    mid = hidden_ref[...] + dot_nn(att_ref[...].astype(bf16), wout_ref[...])
    mid_ref[...] = mid
    low = (mid * root_scale(mid) * line_of(small_ref, AT_MOE)).astype(bf16)
    thin = dot_nn(low, small_ref[...])
    lane = lanes_of(mid.shape[0])
    logits = jnp.where(lane < ROUTED, thin + previous_ref[...], 0.0)
    logit_ref[...] = logits
    top = jnp.max(jnp.where(lane < ROUTED, logits, masked_score), axis=1, keepdims=True)
    expo = jnp.where(lane < ROUTED, jnp.exp(logits - top), 0.0)
    chances = expo / jnp.sum(expo, axis=1, keepdims=True)
    chance_ref[...] = chances
    inside = (lane >= AT_CONST) & (lane < AT_CONST + 4)
    apart = jnp.where(inside, thin - pair_partner(thin), 0.0)
    mix_ref[...] = jnp.where(inside, jax.nn.sigmoid(apart), 0.0)
    width = mid.shape[1]
    moved = dot_nn(low, order_ref[...]).astype(bf16)
    message_ref[:, :width] = dot_nn(slot_tokens_ref[...], moved).astype(bf16)
    if final:
        message_ref[:, width:] = slots_of_grad(
            grad_ref[...].astype(f32),
            chances,
            (first_ref[...], second_ref[...]),
            slot_pairs_ref[...],
        )


def from_expert_kernel(
    final, mid_ref, chance_ref, mix_ref, first_ref, second_ref, small_ref, pair_slots_ref, back_ref, *refs
):
    if final:
        (out_ref,) = refs
    else:
        next_ref, out_ref, normed_ref = refs
    mid = mid_ref[...]
    rows, width = mid.shape
    picks = (first_ref[...], second_ref[...])
    chances = chance_ref[...]
    _, _, alpha, betas = side_weights(chances, mix_ref[...], picks[0] + picks[1])
    lines = small_ref[...].astype(f32).T
    out = mid + alpha * (mid * root_scale(mid) * lines[AT_MOE : AT_MOE + 1])
    out += betas[0] * lines[AT_CVEC : AT_CVEC + 1] + betas[1] * lines[AT_CVEC + 1 : AT_CVEC + 2]
    pairs = dot_nn(pair_slots_ref[...], back_ref[...])
    for at in range(TOP):
        picked = jnp.sum(chances * picks[at], axis=1, keepdims=True)
        out += picked * pairs[at * rows : (at + 1) * rows]
    out_ref[...] = out.astype(out_ref.dtype)
    if not final:
        normed_ref[...] = (out * root_scale(out) * line_of(next_ref, AT_ATTN)).astype(bf16)


def rms_back_rows(values, gain, grad):
    scale = root_scale(values)
    inner = grad * gain
    along = jnp.mean(inner * values, axis=1, keepdims=True)
    gain_grad = jnp.sum(grad * values * scale, axis=0, keepdims=True)
    return scale * inner - values * (scale * scale * scale * along), gain_grad


def to_attention_kernel(
    grad_ref,
    mid_ref,
    chance_ref,
    mix_ref,
    first_ref,
    second_ref,
    small_ref,
    pair_slots_ref,
    token_slots_ref,
    back_ref,
    in_back_ref,
    next_ref,
    wout_ref,
    att_ref,
    total_ref,
    head_ref,
    mid_grad_ref,
    mid_low_ref,
    sent_ref,
    delta_ref,
    thin_grad_ref,
    thin_w_ref,
    line_grad_ref,
):
    grad, mid = grad_ref[...].astype(f32), mid_ref[...]
    rows, width = mid.shape
    picks = (first_ref[...], second_ref[...])
    chosen = picks[0] + picks[1]
    chances, mixes = chance_ref[...], mix_ref[...]
    last, mix, alpha, betas = side_weights(chances, mixes, chosen)
    lines = small_ref[...].astype(f32).T
    gain = lines[AT_MOE : AT_MOE + 1]
    cvecs = [lines[AT_CVEC + c : AT_CVEC + 1 + c] for c in range(2)]
    mixed = mid * root_scale(mid) * gain
    pairs = dot_nn(pair_slots_ref[...], back_ref[...])
    along = jnp.sum(grad * mixed, axis=1, keepdims=True)
    across = [jnp.sum(grad * cvecs[c], axis=1, keepdims=True) for c in range(2)]
    lane = lanes_of(rows)
    chance_grad = jnp.where(lane == 9, along, 0.0)
    for c in range(2):
        both = mix[2 * c] * along + mix[2 * c + 1] * across[c]
        chance_grad = jnp.where(lane == 10 + c, both, chance_grad)
    chance_grad *= chosen
    for at in range(TOP):
        part = jnp.sum(grad * pairs[at * rows : (at + 1) * rows], axis=1, keepdims=True)
        chance_grad += picks[at] * part
    logit_grad = chances * (
        chance_grad - jnp.sum(chances * chance_grad, axis=1, keepdims=True)
    ) + jnp.where(lane < ROUTED, next_ref[...], 0.0)
    mix_grad = jnp.zeros_like(mixes)
    for c in range(2):
        mix_grad = jnp.where(lane == AT_CONST + 2 * c, last[1 + c] * along, mix_grad)
        mix_grad = jnp.where(lane == AT_CONST + 2 * c + 1, last[1 + c] * across[c], mix_grad)
    product = mixes * mix_grad
    thin_grad = logit_grad + mixes * (mix_grad - (product + pair_partner(product)))
    thin_grad_ref[...] = thin_grad
    low_grad = (
        alpha * grad
        + two_part_nt(thin_grad, small_ref[...])
        + dot_nn(token_slots_ref[...], in_back_ref[...])
    )
    mid_part, gain_grad = rms_back_rows(mid, gain, low_grad)
    mid_grad = grad + mid_part
    mid_grad_ref[...] = mid_grad
    mid_low = mid_grad.astype(bf16)
    mid_low_ref[...] = mid_low
    att_grad = dot_nt(mid_low, wout_ref[...]).astype(bf16)
    delta = two_part_nn(att_grad.astype(f32) * att_ref[...], head_ref[...])
    delta_ref[...] = delta
    sent_ref[:, :width] = att_grad
    stats = jnp.zeros((rows, LANES), f32)
    for at, stat in enumerate((total_ref[...], delta)):
        top = stat.astype(bf16).astype(f32)
        for part, piece in enumerate((top, stat - top)):
            place = 32 * at + 16 * part
            stats += pltpu.roll(piece, place, 1) if place else piece
    sent_ref[:, width:] = stats.astype(bf16)
    turned = mixed.T.astype(bf16)
    thin_w_ref[...] = two_part_tn(turned, thin_grad)
    line_grad_ref[...] = jnp.concatenate(
        [gain_grad]
        + [jnp.sum(betas[c] * grad, axis=0, keepdims=True) for c in range(2)]
        + [jnp.zeros((5, width), f32)],
        axis=0,
    )


def two_part_tn(turned, x):
    top = x.astype(bf16)
    return dot_nn(turned, top) + dot_nn(turned, (x - top.astype(f32)).astype(bf16))


def from_attention_kernel(final, q_ref, k_ref, v_ref, wq_ref, wk_ref, wv_ref, hidden_ref, small_ref, mid_grad_ref, *refs):
    if final:
        grad_ref, line_grad_ref = refs
    else:
        chance_ref, first_ref, second_ref, slot_pairs_ref, grad_ref, line_grad_ref, message_ref = refs
    normed_grad = dot_nt(q_ref[...], wq_ref[...])
    normed_grad += dot_nt(k_ref[...], wk_ref[...])
    normed_grad += dot_nt(v_ref[...], wv_ref[...])
    part, gain_grad = rms_back_rows(
        hidden_ref[...], line_of(small_ref, AT_ATTN), normed_grad
    )
    grad = mid_grad_ref[...] + part
    grad_ref[...] = grad
    line_grad_ref[...] = jnp.concatenate(
        [gain_grad, jnp.zeros((7, gain_grad.shape[1]), f32)], axis=0
    )
    if not final:
        message_ref[...] = slots_of_grad(
            grad, chance_ref[...], (first_ref[...], second_ref[...]), slot_pairs_ref[...]
        )


class Block:
    def __init__(self, array, wide, at):
        self.array, self.wide, self.at = array, wide, at


def run_fused(kernel, args, outs, flops):
    arrays, specs = [], []
    for arg in args:
        if isinstance(arg, Block):
            arrays.append(arg.array)
            specs.append(
                pl.BlockSpec(
                    (arg.array.shape[0], arg.wide),
                    functools.partial(lambda at, i: (0, at), arg.at),
                )
            )
        else:
            arrays.append(arg)
            specs.append(pl.BlockSpec(arg.shape, lambda i: (0, 0)))
    return pl.pallas_call(
        kernel,
        grid=(1,),
        in_specs=specs,
        out_specs=[pl.BlockSpec(shape, lambda i: (0, 0)) for shape, _ in outs],
        out_shape=[jax.ShapeDtypeStruct(shape, dtype) for shape, dtype in outs],
        compiler_params=kernel_params(1),
        cost_estimate=pl.CostEstimate(flops=flops, bytes_accessed=1 << 22, transcendentals=0),
    )(*arrays)


def after(x, *things):
    return lax.optimization_barrier((x,) + things)[0]


def swap(x, axis):
    return lax.ppermute(x, axis, [(0, 1), (1, 0)])


def fold(x, axis, at):
    given = lax.dynamic_index_in_dim(x, 1 - at, 1, keepdims=False)
    kept = lax.dynamic_index_in_dim(x, at, 1, keepdims=False)
    return (kept.astype(f32) + swap(given, axis).astype(f32)).astype(bf16)


def gather_rows(x, axes, fillers=()):
    far, near, core = axes[:-2], axes[-2], axes[-1]
    count = 2 ** len(far)
    found = [x]
    for step in range(1, count):
        pairs = [(at, (at + step) % count) for at in range(count)]
        found.append(lax.ppermute(x, far, pairs))
    blocks, filled = [], []
    for step, block in enumerate(found):
        beside = swap(block, near)
        if step < len(fillers):
            filled.append(fillers[step](beside if step == 0 else block))
        pair = jnp.concatenate([block, beside], axis=0)
        blocks += [pair, swap(pair, core)]
    rows = jnp.concatenate(blocks, axis=0)
    return (rows, filled) if fillers else rows


def gathered_order(axes):
    count = 2 ** (len(axes) - 2)
    me = lax.axis_index(axes)
    far, near, core = me // 4, me // 2 % 2, me % 2
    order = []
    for step in range(count):
        for other_core in range(2):
            for other_near in range(2):
                order.append(
                    (far - step) % count * 4 + (near ^ other_near) * 2 + (core ^ other_core)
                )
    return jnp.stack(order).astype(jnp.int32)


def shards(
    axes,
    tokens,
    prev_logits,
    routes,
    order,
    deal,
    w_qkv,
    w_out,
    w_gate,
    w_up,
    w_down,
    norm_attn,
    norm_moe,
    w_router,
    w_const,
    const_vec,
    grad_out,
):
    rows, width = tokens.shape[1], tokens.shape[2]
    ex_axes, sub_axes = axes[:3], axes[3:]
    every_axis = axes + (FS,)
    subs = 2 ** len(sub_axes)
    ctx_size = EXPERTS * subs
    length = rows * ctx_size
    prompt = length // 2
    cont_len = prompt // (ctx_size // 8)
    block_rows = rows // 2
    own_rows = w_qkv.shape[1]
    fs_at = lax.axis_index(FS)
    sub_at = lax.axis_index(sub_axes)

    ex_at = lax.axis_index(ex_axes)

    def deal_out(x):
        return lax.all_to_all(x, ex_axes, 0, 0, tiled=True)

    def dispatch(x):
        blocks = [x[:SLOTS]]
        for step in range(1, EXPERTS):
            block = x[step * SLOTS : (step + 1) * SLOTS]
            pairs = [(at, at ^ step) for at in range(EXPERTS)]
            blocks.append(lax.ppermute(block, ex_axes, pairs))
        return jnp.concatenate(blocks, axis=0)

    def blank(count):
        return jnp.zeros((own_rows, count), bf16)

    def fetch_packed(layer, *wait):
        mine = jnp.concatenate(
            [
                w_qkv[layer],
                w_router[layer],
                blank(AT_CONST - ROUTED),
                w_const[layer],
                blank(AT_CVEC - AT_CONST - 4),
                const_vec[layer],
                blank(AT_ATTN - AT_CVEC - 2),
                norm_attn[layer][:, None],
                norm_moe[layer][:, None],
                blank(LANES - AT_MOE - 1),
            ],
            axis=1,
        )
        return lax.all_gather(after(mine, *wait), every_axis, axis=0, tiled=True)

    by_chunks = subs == 2
    flags = jnp.stack([sub_at, fs_at]).astype(jnp.int32)[None, :]

    def move_in(member, *wait):
        moved = deal_out(after(member, *wait))
        return moved.reshape(-1, moved.shape[2]) if by_chunks else moved

    def spread(moved, *wait):
        moved = after(moved, *wait)
        if not by_chunks:
            whole = lax.all_gather(moved, sub_axes + (FS,), axis=1, tiled=True)
            return (whole.reshape(-1, whole.shape[2]),)
        across = swap(moved, FS)
        return (moved, across)

    def share(parts, *wait):
        if not by_chunks:
            return parts[0]
        moved, across = after(parts[0], *wait), parts[1]
        return (moved, across, swap(moved, sub_axes[0]), swap(across, sub_axes[0]))

    if not by_chunks:
        to_chunks = jnp.eye(width, dtype=bf16)
    else:
        place = jnp.arange(width, dtype=jnp.int32)
        chunk, inside = place // (width // 4), place % (width // 4)
        source = (
            inside // own_rows * 4 + (chunk ^ (sub_at * 2 + fs_at)).astype(jnp.int32)
        ) * own_rows + inside % own_rows
        to_chunks = (place[:, None] == source[None, :]).astype(bf16)

    tokens_all = gather_rows(tokens[0], axes)
    def fetch_out(layer, *wait):
        return lax.all_gather(after(w_out[layer], *wait), every_axis, axis=0, tiled=True)

    all_packed = [fetch_packed(0)]
    all_out = [fetch_out(0)]
    gate_moved = move_in(w_gate[0])
    up_moved = move_in(w_up[0], gate_moved)
    gate_parts = spread(gate_moved)
    down_moved = move_in(w_down[0], up_moved, *gate_parts, tokens_all)
    up_parts = spread(up_moved)
    all_experts = []

    block_order = gathered_order(axes)
    deal_pairs = deal.reshape(ctx_size, 2)
    own_blocks = jnp.sum(
        jnp.where(
            (block_order[:, None] == jnp.arange(ctx_size, dtype=jnp.int32)[None, :])[:, :, None],
            deal_pairs[None],
            0,
        ),
        axis=1,
    ).reshape(2 * ctx_size)
    all_places = (
        own_blocks[:, None] * block_rows + jnp.arange(block_rows, dtype=jnp.int32)[None, :]
    ).reshape(length)
    within = jnp.where(all_places < prompt, all_places, prompt + (all_places - prompt) % cont_len)
    all_starts = jnp.where(all_places < prompt, 0, all_places - (all_places - prompt) % cont_len)
    lane = jnp.arange(LANES, dtype=jnp.int32)
    half = HEAD_DIM // 2
    frequency = 10000.0 ** (-(lane % half).astype(f32) / half)
    angles = within.astype(f32)[:, None] * frequency[None, :]
    cosine = jnp.cos(angles)
    sine = jnp.sin(angles) * jnp.where(lane % HEAD_DIM < half, -1.0, 1.0)[None, :]
    own_cos, own_sin = cosine, sine
    own_places, own_starts = all_places[:rows, None], all_starts[:rows, None]
    place_line, start_line = all_places[None, :], all_starts[None, :]

    first_things = [tokens_all, *gate_parts, up_moved, cosine, sine]

    route_rows = routes[0]
    flat_routes = jnp.concatenate([route_rows[:, k] for k in range(TOP)])
    flat_order = jnp.concatenate([order[0].reshape(rows, TOP)[:, k] for k in range(TOP)])
    earlier = (flat_routes[None, :] == flat_routes[:, None]) & (
        flat_order[None, :] < flat_order[:, None]
    )
    slot = jnp.sum(earlier.astype(jnp.int32), axis=1)
    in_slot = (flat_routes < EXPERTS) & (slot < CAP)
    target = jnp.where(in_slot, (flat_routes ^ ex_at) * SLOTS + slot, -1)
    slot_ids = jnp.arange(EXPERTS * SLOTS, dtype=jnp.int32)
    pair_slots = (target[:, None] == slot_ids[None, :]).astype(bf16)
    slot_pairs = (slot_ids[:, None] == target[None, :]).astype(bf16)
    slot_tokens = slot_pairs[:, :rows] + slot_pairs[:, rows:]
    token_slots = pair_slots[:rows] + pair_slots[rows:]
    picks = [(route_rows[:, k : k + 1] == lane[None, :]).astype(f32) for k in range(TOP)]
    head_of = (jnp.arange(width, dtype=jnp.int32)[:, None] // HEAD_DIM == lane[None, :]).astype(
        bf16
    )

    table = (rows, LANES)
    full = (rows, width)
    core_axis = sub_axes[0]

    def join_cores(kept, given, *wait):
        part = kept.astype(f32) + swap(after(given, *wait), core_axis).astype(f32)
        if part.ndim == 3:
            half = part.shape[1] // 2
            return part[:, :half].astype(bf16), part[:, half:].astype(bf16)
        half = part.shape[0] // 2
        return part[:half].astype(bf16), part[half:].astype(bf16)

    def join_groups(pieces, *wait):
        kept, given = pieces
        part = (kept.astype(f32) + swap(after(given, *wait), FS).astype(f32)).astype(bf16)
        return part.reshape(EXPERTS, -1, part.shape[-1])

    def reduce_rows(part):
        part = part.reshape(-1, part.shape[2])
        return lax.psum_scatter(part, ex_axes, scatter_dimension=0, tiled=True)

    def scatter_whole(member):
        cut = member.astype(bf16).reshape(EXPERTS, subs * 2, -1, member.shape[1])
        part = lax.psum_scatter(cut, sub_axes + (FS,), scatter_dimension=1, tiled=True)
        return part.reshape((EXPERTS,) + part.shape[2:])

    def expert_plain_back(x, out_grad, gate_act, upward, weights):
        wgate, wup, wdown = weights
        sigma = jax.nn.sigmoid(gate_act)
        gated = gate_act * sigma
        inner = (gated * upward).astype(bf16)
        inner_grad = dot_nt(out_grad, wdown)
        up_grad = (inner_grad * gated).astype(bf16)
        gate_grad = (inner_grad * upward * (sigma + gated * (1.0 - sigma))).astype(bf16)
        in_grad = (dot_nt(gate_grad, wgate) + dot_nt(up_grad, wup)).astype(bf16)
        products = (dot_tn(x, gate_grad), dot_tn(x, up_grad), dot_tn(inner, out_grad))
        return [scatter_whole(member) for member in products], in_grad

    def expert_plain(x, weights):
        wgate, wup, wdown = weights
        gate_act, upward = dot_nn(x, wgate), dot_nn(x, wup)
        inner = (jax.nn.silu(gate_act) * upward).astype(bf16)
        return gate_act, upward, dot_nn(inner, wdown).astype(bf16)

    hidden = tokens[0].astype(f32)
    previous = jnp.pad(prev_logits[0], ((0, 0), (0, LANES - ROUTED)))
    grad = grad_out[0]
    all_packed[0] = after(all_packed[0], *first_things, slot_tokens, previous)
    saved_all = []
    for layer in range(LAYERS):
        final = layer == LAYERS - 1
        packed = all_packed[layer]
        if layer == 0:
            normed_all = norm_rows(tokens_all, packed)
            normed = normed_all[:rows]
        else:
            up_moved = move_in(w_up[layer], normed)
            normed_all = gather_rows(normed, axes)
            normed_all = after(normed_all, *gate_parts, up_moved)
            down_moved = move_in(w_down[layer], normed_all)
            up_parts = spread(up_moved, normed_all)
        normed_used = normed
        all_queries, keys, values = project(
            normed_all, packed, (0, 1, 2), (True, True, False), cosine, sine
        )
        queries = all_queries
        if layer == 0:
            all_packed.append(fetch_packed(1, keys))
            all_out.append(fetch_out(1, keys))
        attended, totals = attend(
            queries, keys, values, own_places, own_starts, place_line, prompt
        )
        if final:
            attended = after(attended, down_moved, *up_parts)
        down_parts = spread(down_moved)
        small = Block(packed, LANES, 3 * width // LANES)
        wout = all_out[layer]
        midway, logits, chances, mixing, slot_in = run_fused(
            functools.partial(to_expert_kernel, final),
            [attended, hidden, wout, small, previous, slot_tokens, to_chunks]
            + ([grad, picks[0], picks[1], slot_pairs] if final else []),
            [
                (full, f32),
                (table, f32),
                (table, f32),
                (table, f32),
                ((EXPERTS * SLOTS, (2 if final else 1) * width), bf16),
            ],
            6 * rows * width * width,
        )
        if layer == 0:
            slot_in = after(slot_in, down_moved, *up_parts)
        expert_in = dispatch(slot_in)
        weights = [share(parts, slot_in) for parts in (gate_parts, up_parts, down_parts)]
        if not final:
            next_gate = move_in(w_gate[layer + 1], expert_in)
        gate_act = upward = halves = None
        if by_chunks and final:
            halves, expert_out = run_expert_back(
                flags, (expert_in, expert_in), to_chunks, None, None, *weights
            )
        elif by_chunks:
            gate_act, upward, expert_out = run_expert(flags, expert_in, *weights)
        elif final:
            half_in, half_grad = expert_in[:, :width], expert_in[:, width:]
            gate_act, upward, expert_out = expert_plain(half_in, weights)
            halves, in_grad = expert_plain_back(half_in, half_grad, gate_act, upward, weights)
            expert_out = jnp.concatenate([in_grad, expert_out], axis=1)
        else:
            gate_act, upward, expert_out = expert_plain(expert_in, weights)
        if not final:
            expert_out = after(expert_out, next_gate)
            gate_parts = spread(next_gate, expert_out)
        back = dispatch(expert_out)
        in_back = None
        if final:
            in_back, back = back[:, :width], back[:, width:]
        if final:
            (output_rows,) = run_fused(
                functools.partial(from_expert_kernel, True),
                [midway, chances, mixing, picks[0], picks[1], small, pair_slots, back],
                [(full, bf16)],
                2 * rows * width * EXPERTS * SLOTS,
            )
        else:
            all_packed[layer + 1] = after(all_packed[layer + 1], expert_out)
            output, normed = run_fused(
                functools.partial(from_expert_kernel, False),
                [midway, chances, mixing, picks[0], picks[1], small, pair_slots, back]
                + [Block(all_packed[layer + 1], LANES, 3 * width // LANES)],
                [(full, f32), (full, bf16)],
                2 * rows * width * EXPERTS * SLOTS,
            )
        saved_all.append(
            (
                hidden,
                normed_used,
                normed_all,
                all_queries,
                queries,
                keys,
                values,
                attended,
                totals,
                midway,
                chances,
                mixing,
                expert_in,
                gate_act,
                upward,
                halves,
                in_back,
                weights,
                back,
            )
        )
        if not final:
            hidden = output
        previous = logits

    logit_next = jnp.zeros(table, f32)
    results = [None] * LAYERS
    moved_grads = [[None] * 3 for _ in range(LAYERS)]
    out_folded = [None] * LAYERS
    for layer in reversed(range(LAYERS)):
        final = layer == LAYERS - 1
        (
            hidden,
            normed,
            normed_all,
            all_queries,
            queries,
            keys,
            values,
            attended,
            totals,
            midway,
            chances,
            mixing,
            expert_in,
            gate_act,
            upward,
            halves,
            in_back,
            weights,
            back,
        ) = saved_all[layer]
        packed = all_packed[layer]
        small = Block(packed, LANES, 3 * width // LANES)
        wout = all_out[layer]
        if not final:
            if by_chunks:
                slot_grad = after(slot_grad, moved_grads[1][1])
            out_grad = dispatch(slot_grad)
            if by_chunks:
                out_grad = after(out_grad, *qkv_joined)
                moved_grads[1][2] = deal_out(after(folded[1][2], out_grad))
                halves, in_grad = run_expert_back(
                    flags, (expert_in, out_grad), to_chunks, gate_act, upward, *weights
                )
                in_grad = after(in_grad, moved_grads[1][2])
            else:
                halves, in_grad = expert_plain_back(
                    expert_in, out_grad, gate_act, upward, weights
                )
            in_back = dispatch(in_grad)
            if by_chunks:
                in_back = after(in_back, qkv_folded, out_folded[1])
                owned = reduce_rows(
                    jnp.concatenate([out_folded[1], after(qkv_folded, in_back)], axis=2)
                )
        if final:
            folded = [None] * LAYERS
        if by_chunks:
            joined = [join_cores(halves[2 * at], halves[2 * at + 1]) for at in range(3)]
            in_back = after(in_back, *joined[0])
            folded[layer] = [join_groups(joined[at]) for at in range(3)]
        mid_grad, mid_low, sent, delta, logit_next, thin_w, line_grads = run_fused(
            to_attention_kernel,
            [grad, midway, chances, mixing, picks[0], picks[1], small, pair_slots]
            + [token_slots, back, in_back, logit_next, wout, attended, totals, head_of],
            [
                (full, f32),
                (full, bf16),
                ((rows, width + LANES), bf16),
                (table, f32),
                (table, f32),
                ((width, LANES), f32),
                ((8, width), f32),
            ],
            6 * rows * width * width,
        )
        def some_queries(start, dependence):
            return query_back(
                start,
                2,
                after(queries, dependence),
                sent,
                keys,
                values,
                totals,
                delta,
                own_places,
                own_starts,
                place_line,
                own_cos,
                own_sin,
                prompt,
            )

        sent_all, query_grads = gather_rows(
            sent, axes, [functools.partial(some_queries, start) for start in range(0, PAIRS, 2)]
        )
        late_low = after(mid_low, sent)
        if by_chunks:
            att_rel = dot_nn(attended.astype(bf16), to_chunks).astype(bf16)
            out_joined = join_cores(*weight_product(att_rel, late_low))
        else:
            out_w_grad = dot_tn(attended.astype(bf16), late_low).astype(bf16)
        query_grad = jnp.concatenate(query_grads, axis=1)
        if by_chunks:
            sent_all = after(sent_all, folded[layer][0], query_grad)
            moved_grads[layer][0] = deal_out(after(folded[layer][0], sent_all))
        key_grad, value_grad = key_back(
            keys,
            values,
            all_queries,
            sent_all,
            own_places,
            place_line,
            start_line,
            own_cos,
            own_sin,
            prompt,
        )
        if by_chunks and final:
            key_grad = after(key_grad, moved_grads[layer][0], folded[layer][1])
            moved_grads[layer][1] = deal_out(after(folded[layer][1], key_grad))
        proj_grad = jnp.concatenate([query_grad, key_grad, value_grad], axis=1)
        before = []
        if layer > 0:
            before = [saved_all[layer - 1][10], picks[0], picks[1], slot_pairs]
        grad, gain_grads, *slot_grad = run_fused(
            functools.partial(from_attention_kernel, layer == 0),
            [query_grad, key_grad, value_grad]
            + [Block(packed, width, at) for at in range(3)]
            + [hidden, small, mid_grad]
            + before,
            [(full, f32), ((8, width), f32)]
            + ([((EXPERTS * SLOTS, width), bf16)] if layer > 0 else []),
            6 * rows * width * width,
        )
        slot_grad = slot_grad[0] if slot_grad else None
        some = jnp.concatenate([gain_grads[:1], line_grads[:3]], axis=0)
        wanted = jnp.array([AT_ATTN, AT_MOE, AT_CVEC, AT_CVEC + 1], dtype=jnp.int32)
        spread_out = (wanted[:, None] == lane[None, :]).astype(f32)
        thin_part = thin_w + jnp.dot(some.T, spread_out, precision=highest)
        if by_chunks:
            out_folded[layer] = join_groups(out_joined)
        if by_chunks and final:
            thin_low = dot_tn(to_chunks, thin_part.astype(bf16)).astype(bf16)
            normed_rel = dot_nn(normed, to_chunks).astype(bf16)
            qkv_joined = join_cores(*weight_product(normed_rel, after(proj_grad, grad), thin_low))
            qkv_folded = join_groups(qkv_joined)
            continue
        share_of = 3 * width // ctx_size
        columns = proj_grad.reshape(rows, ctx_size, share_of).transpose(1, 0, 2)
        if by_chunks:
            columns = after(columns, moved_grads[0][0])
        columns = lax.all_to_all(columns, axes, 0, 0, tiled=True)
        if by_chunks:
            moved_grads[0][1] = deal_out(after(folded[0][1], columns))
        columns = jnp.take(columns, block_order, axis=0).reshape(length, share_of)
        part = jnp.concatenate([dot_tn(columns, normed_all).T, thin_part], axis=1).astype(bf16)
        part = fold(part.reshape(ctx_size, 2, own_rows, share_of + LANES), FS, fs_at)
        if by_chunks:
            part = after(part, moved_grads[0][1])
        part = lax.all_to_all(part, axes, 0, 0, tiled=True)
        if by_chunks:
            last = jnp.concatenate([folded[0][2], out_folded[0]], axis=1)
            last = deal_out(after(last, part))
            tall = folded[0][2].shape[1]
            moved_grads[0][2], last_out = last[:, :tall], last[:, tall:]
        part = part.astype(f32)
        qkv_owned = part[:, :, :share_of].transpose(1, 0, 2).reshape(own_rows, 3 * width)
        thin_owned = jnp.sum(part[:, :, share_of:], axis=0)
        if by_chunks:
            out_owned = jnp.sum(last_out.astype(f32), axis=0)
        else:
            moved_grads[layer] = [deal_out(part) for part in halves]
            out_owned = lax.psum_scatter(
                out_w_grad, every_axis, scatter_dimension=0, tiled=True
            ).astype(f32)
        results[layer] = (qkv_owned, out_owned, thin_owned)
    if by_chunks:
        owned = owned.astype(f32)
        results[1] = (owned[:, width : 4 * width], owned[:, :width], owned[:, 4 * width :])

    def stack(parts):
        return jnp.stack(parts)

    thin_all = [results[layer][2] for layer in range(LAYERS)]
    return (
        output_rows[None],
        grad[None],
        stack([results[layer][0] for layer in range(LAYERS)]),
        stack([results[layer][1] for layer in range(LAYERS)]),
        stack([moved_grads[layer][0].astype(f32) for layer in range(LAYERS)]),
        stack([moved_grads[layer][1].astype(f32) for layer in range(LAYERS)]),
        stack([moved_grads[layer][2].astype(f32) for layer in range(LAYERS)]),
        stack([thin[:, AT_ATTN] for thin in thin_all]),
        stack([thin[:, AT_MOE] for thin in thin_all]),
        stack([thin[:, :ROUTED] for thin in thin_all]),
        stack([thin[:, AT_CONST : AT_CONST + 4] for thin in thin_all]),
        stack([thin[:, AT_CVEC : AT_CVEC + 2] for thin in thin_all]),
    )


def solution(mesh):
    devices = mesh.devices
    axes = ctx_axes(devices.shape[0])
    every_axis = axes + (FS,)
    finer = Mesh(devices.reshape((2,) * len(axes) + (devices.shape[1],)), every_axis)
    token_spec = P(FS, axes, None)
    row_spec = P(None, every_axis, None)
    expert_spec = P(None, None, every_axis, None)
    gain_spec = P(None, every_axis)
    return jax.shard_map(
        functools.partial(shards, axes),
        mesh=finer,
        in_specs=(
            token_spec,
            token_spec,
            token_spec,
            P(FS, axes),
            P(),
            row_spec,
            row_spec,
            expert_spec,
            expert_spec,
            expert_spec,
            gain_spec,
            gain_spec,
            row_spec,
            row_spec,
            row_spec,
            token_spec,
        ),
        out_specs=(
            token_spec,
            token_spec,
            row_spec,
            row_spec,
            expert_spec,
            expert_spec,
            expert_spec,
            gain_spec,
            gain_spec,
            row_spec,
            row_spec,
            row_spec,
        ),
        check_vma=False,
    )
```

time: 1180 us -> 831 us (0.70)
  waiting for transfers between devices: 557 us -> 215 us
  blocking collectives: 173 us -> 0 us
  starting transfers between devices: 65.4 us -> 206 us
  matrix products: 91.3 us -> 9.36 us
  Pallas kernels: 109 us -> 188 us
  local copies, waits for them, and re-layouts: 96.9 us -> 114 us
  other arithmetic: 54.5 us -> 70.7 us
    unnamed x22 -> x6, waiting for transfers between devices: 187 us -> 0.11 us
    all_to_all x6 -> x0, blocking collectives: 173 us -> none  [dispatch(): return lax.all_to_all(x, EX, 0, 0, tiled=True)]
    all_gather x12 -> x4, waiting for transfers between devices: 173 us -> 20.6 us  [the longest x2 19.1 us: fetch_out(): lax.all_gather(after(w_out[layer], *wait), every_axis, axis=0, tiled=True)]
    ppermute x0 -> x123, waiting for transfers between devices: none -> 147 us  [the longest x69 80.9 us: swap(): return lax.ppermute(x, axis, [(0, 1), (1, 0)])]
    ppermute x0 -> x123, starting transfers between devices: none -> 136 us  [the longest x42 70.8 us: dispatch(): blocks.append(lax.ppermute(block, ex_axes, pairs))]
    reduce_scatter x6 -> x0, waiting for transfers between devices: 107 us -> none  [shards(): part = lax.psum_scatter(cut, (SUB, FS), scatter_dimension=1, tiled=True)]
    pallas_call x2 -> x21, Pallas kernels: 19.2 us -> 122 us  [the longest x2 35 us: run_expert_back(): pl.pallas_call(functools.partial(expert_back_kernel, both), grid=(EXPERTS...]
    all_to_all x14, waiting for transfers between devices: 90 us -> 47.4 us  [the longest x12 36.4 us: deal_out(): return lax.all_to_all(x, ex_axes, 0, 0, tiled=True)]
  transfers between devices with their start and end apart: 34 -> 142, of which waited for: 22 -> 50; matrix products, arithmetic and copies ran while one was open for 15% -> 20% of each run, Pallas kernels for 9% -> 20%
where the time goes in v2:
time: 831 us; the launch traced here: 819 us
  waiting for transfers between devices  215 us (26%)
  starting transfers between devices  206 us (25%)
  Pallas kernels  188 us (23%)
  local copies, waits for them, and re-layouts  114 us (14%)
  other arithmetic  70.7 us (9%)
  between operations  15.9 us (2%)
  matrix products  9.36 us (1%)
    ppermute x69, waiting for transfers between devices, swap(): return lax.ppermute(x, axis, [(0, 1), (1, 0)])  80.9 us
    ppermute x42, starting transfers between devices, dispatch(): blocks.append(lax.ppermute(block, ex_axes, pairs))  70.8 us
    all_to_all x12, starting transfers between devices, deal_out(): return lax.all_to_all(x, ex_axes, 0, 0, tiled=True)  59.7 us
    unnamed x273, local copies, waits for them, and re-layouts  50.9 us
    ppermute x69, starting transfers between devices, swap(): return lax.ppermute(x, axis, [(0, 1), (1, 0)])  43.5 us
    ppermute x42, waiting for transfers between devices, dispatch(): blocks.append(lax.ppermute(block, ex_axes, pairs))  42.6 us
    all_to_all x12, waiting for transfers between devices, deal_out(): return lax.all_to_all(x, ex_axes, 0, 0, tiled=True)  36.4 us
    pallas_call x2, Pallas kernels, run_expert_back(): pl.pallas_call(functools.partial(expert_back_kernel, both), grid=(EXPERTS...  35 us
  transfers between devices with their start and end apart: 142, of which 50 were waited for; matrix products, arithmetic and copies ran while one was open for 20% of the time, Pallas kernels for 20%

profile of v2, /device:TPU:0, one launch (start us, length us, event | category | flops | bytes accessed | tf_op | source)
XLA Modules:
  0.0 818.9 jit_solution(7452930886554921572)
XLA Ops:
  27.7 4.3 all-to-all-start
  36.7 5.6 fusion.13
  66.3 5.1 all-to-all-start.1
  83.6 13.6 %collective-permute-done.11.refs_1_.refs_3_ = bf16[192,2048]{1,0:T(8,128)(2,1)} collective-permute-done((bf16[192,2048]{1,0:T(8,128)(2,1)}, bf16[192,2048]{1,0:T(8,128)(2,1)}, u32[]{:S(2)}, u32[]{:S(2)}) %collective-permute-start.11) | collective-permute-done | bytes 786464 | tf_op jit(solution)/shard_map/ppermute | solution.py:831
  100.4 4.8 shard_map.265.a_ref
  105.3 12.2 %shard_map.266 = (bf16[2048,768]{1,0:T(8,128)(2,1)}, bf16[2048,768]{1,0:T(8,128)(2,1)}, bf16[2048,768]{1,0:T(8,128)(2,1)}) custom-call(bf16[2048,768]{1,0:T(8,128)(2,1)} %shard_map.265.a_ref, bf16[768,2432]{1,0:T(8,128)(2,1)} %all-gather.5.cloned.1.call-done.small_ref.refs_0_.refs_1_.refs_2_.wq_ref.wk_ref.wv_ref, ...), custom_call_target="tpu_custom_call" | custom-call | flops 7247757312 | bytes 16121856 | tf_op jit(solution)/shard_map/pallas_call | solution.py:93
  129.0 10.1 %shard_map.267 = (f32[128,768]{1,0:T(8,128)}, f32[128,128]{1,0:T(8,128)}) custom-call(bf16[2048,768]{1,0:T(8,128)(2,1)} %get-tuple-element.210.q_ref, bf16[2048,768]{1,0:T(8,128)(2,1)} %get-tuple-element.129.k_ref, bf16[2048,768]{1,0:T(8,128)(2,1)} %get-tuple-element.130.v_ref, s32[128,1]{1,0:T(8,128)} %broadcast_in_dim.105.at_ref.own_ref, ...), custom_call_target="tpu_custom_call" | custom-call | flops 1610612736 | bytes 6291456 | tf_op jit(solution)/shard_map/pallas_call | solution.py:158
  139.0 19.0 %all-gather.7.cloned.1.call-done.wout_ref = bf16[768,768]{1,0:T(8,128)(2,1)} async-done(((bf16[24,768]{1,0:T(8,128)(2,1)}), bf16[768,768]{1,0:T(8,128)(2,1)}) %all-gather.7.cloned.1.call-update) | async-done | bytes 1179664 | tf_op jit(solution)/shard_map/all_gather | solution.py:971
  183.8 4.2 all-to-all-start.3
  197.3 11.2 %shard_map.269 = (f32[256,2048]{1,0:T(8,128)}, f32[256,2048]{1,0:T(8,128)}, bf16[256,768]{1,0:T(8,128)(2,1)}) custom-call(s32[1,2]{1,0:T(1,128)} %add_bitcast_fusion.flag_ref, bf16[256,768]{1,0:T(8,128)(2,1)} %copy-done.53, bf16[192,2048]{1,0:T(8,128)(2,1)} %bitcast.8.refs_0_.refs_2_, bf16[192,2048]{1,0:T(8,128)(2,1)} %collective-permute-done.11.refs_1_.refs_3_, ...), custom_call_target="tpu_custom_call" | custom-call | flops 2415919104 | bytes 13631488 | tf_op jit(solution)/shard_map/pallas_call | solution.py:388
  255.4 6.8 collective-permute-done.40
  262.2 7.5 collective-permute-done.43
  274.7 6.3 all-to-all-start.5
  281.9 12.0 %shard_map.271 = (bf16[2048,768]{1,0:T(8,128)(2,1)}, bf16[2048,768]{1,0:T(8,128)(2,1)}, bf16[2048,768]{1,0:T(8,128)(2,1)}) custom-call(bf16[2048,768]{1,0:T(8,128)(2,1)} %copy-done.63, bf16[768,2432]{1,0:T(8,128)(2,1)} %all-gather.9.cloned.1.call-done.refs_0_.refs_1_.refs_2_.small_ref.wq_ref.wk_ref.wv_ref, ...), custom_call_target="tpu_custom_call" | custom-call | flops 7247757312 | bytes 16121856 | tf_op jit(solution)/shard_map/pallas_call | solution.py:93
  293.9 10.1 %shard_map.272 = (f32[128,768]{1,0:T(8,128)}, f32[128,128]{1,0:T(8,128)}) custom-call(bf16[2048,768]{1,0:T(8,128)(2,1)} %get-tuple-element.173.q_ref, bf16[2048,768]{1,0:T(8,128)(2,1)} %get-tuple-element.151.k_ref, bf16[2048,768]{1,0:T(8,128)(2,1)} %get-tuple-element.152.v_ref, s32[128,1]{1,0:T(8,128)} %broadcast_in_dim.105.at_ref.own_ref, ...), custom_call_target="tpu_custom_call" | custom-call | flops 1610612736 | bytes 6291456 | tf_op jit(solution)/shard_map/pallas_call | solution.py:158
  304.7 4.5 shard_map.273
  327.8 6.9 collective-permute-done.51
  341.3 18.7 %shard_map.274 = (bf16[384,2048]{1,0:T(8,128)(2,1)}, bf16[384,2048]{1,0:T(8,128)(2,1)}, bf16[384,2048]{1,0:T(8,128)(2,1)}, bf16[384,2048]{1,0:T(8,128)(2,1)}, bf...) custom-call(s32[1,2]{1,0:T(1,128)} %add_bitcast_fusion.flag_ref, ...), custom_call_target="tpu_custom_call" | custom-call | flops 7247757312 | bytes 23068672 | tf_op jit(solution)/shard_map/pallas_call | solution.py:485
  374.0 6.4 collective-permute-done.64
  385.5 5.1 shard_map.276
  390.6 4.6 collective-permute-start.71
  402.8 9.1 %collective-permute-done.71 = bf16[128,896]{1,0:T(8,128)(2,1)S(1)} collective-permute-done((bf16[128,896]{1,0:T(8,128)(2,1)}, bf16[128,896]{1,0:T(8,128)(2,1)S(1)}, u32[]{:S(2)}, u32[]{:S(2)}) %collective-permute-start.71) | collective-permute-done | bytes 229408 | tf_op jit(solution)/shard_map/ppermute | solution.py:846
  411.8 4.6 shard_map.279
  416.4 4.6 shard_map.278
  421.0 4.7 shard_map.277
  439.3 4.4 collective-permute-done.78
  454.2 6.2 all-to-all-start.6
  466.7 10.9 %shard_map.280 = (bf16[128,768]{1,0:T(8,128)(2,1)}, bf16[128,768]{1,0:T(8,128)(2,1)}) custom-call(bf16[2048,768]{1,0:T(8,128)(2,1)} %get-tuple-element.151.k_ref, bf16[2048,768]{1,0:T(8,128)(2,1)} %get-tuple-element.152.v_ref, bf16[2048,768]{1,0:T(8,128)(2,1)} %get-tuple-element.173.q_ref, ...), custom_call_target="tpu_custom_call" | custom-call | flops 3221225472 | bytes 6291456 | tf_op jit(solution)/shard_map/pallas_call | solution.py:315
  485.6 5.2 shard_map.281
  508.7 11.4 %collective-permute-done.92 = bf16[8,64,768]{2,1,0:T(8,128)(2,1)} collective-permute-done((bf16[8,64,768]{2,1,0:T(8,128)(2,1)S(1)}, bf16[8,64,768]{2,1,0:T(8,128)(2,1)}, u32[]{:S(2)}, u32[]{:S(2)}) %collective-permute-start.92) | collective-permute-done | bytes 786464 | tf_op jit(solution)/shard_map/ppermute | solution.py:831
  544.1 5.1 all-to-all-start.8
  562.9 16.4 %shard_map.283 = (bf16[384,2048]{1,0:T(8,128)(2,1)}, bf16[384,2048]{1,0:T(8,128)(2,1)}, bf16[384,2048]{1,0:T(8,128)(2,1)}, bf16[384,2048]{1,0:T(8,128)(2,1)}, bf...) custom-call(s32[1,2]{1,0:T(1,128)} %add_bitcast_fusion.flag_ref, ...), custom_call_target="tpu_custom_call" | custom-call | flops 4831838208 | bytes 23068672 | tf_op jit(solution)/shard_map/pallas_call | solution.py:485
  608.1 5.2 shard_map.284
  623.6 10.8 %collective-permute-done.104 = bf16[128,896]{1,0:T(8,128)(2,1)S(1)} collective-permute-done((bf16[128,896]{1,0:T(8,128)(2,1)}, bf16[128,896]{1,0:T(8,128)(2,1)S(1)}, u32[]{:S(2)}, u32[]{:S(2)}) %collective-permute-start.104) | collective-permute-done | bytes 229408 | tf_op jit(solution)/shard_map/ppermute | solution.py:846
  634.5 4.6 shard_map.287
  639.1 4.6 shard_map.286
  643.7 4.7 shard_map.285
  653.0 4.6 collective-permute-done.106
  663.1 5.8 collective-permute-done.111
  680.0 9.3 %all-to-all-start.9 = ((bf16[8,24,2048]{2,1,0:T(8,128)(2,1)}), bf16[8,24,2048]{2,1,0:T(8,128)(2,1)}, u32[]{:S(2)}, u32[]{:S(2)}) async-start(bf16[8,24,2048]{2,1,0:T(8,128)(2,1)} %bitcast.56), calls=%async_computation.9 | async-start | bytes 1572864 | tf_op jit(solution)/shard_map/all_to_all | solution.py:907
  700.6 10.9 %shard_map.288 = (bf16[128,768]{1,0:T(8,128)(2,1)}, bf16[128,768]{1,0:T(8,128)(2,1)}) custom-call(bf16[2048,768]{1,0:T(8,128)(2,1)} %get-tuple-element.129.k_ref, bf16[2048,768]{1,0:T(8,128)(2,1)} %get-tuple-element.130.v_ref, bf16[2048,768]{1,0:T(8,128)(2,1)} %get-tuple-element.210.q_ref, ...), custom_call_target="tpu_custom_call" | custom-call | flops 3221225472 | bytes 6291456 | tf_op jit(solution)/shard_map/pallas_call | solution.py:315
  716.9 6.3 all-to-all-start.10
  728.1 4.7 shard_map.289
  734.1 4.7 all-to-all-done.10
  738.8 4.3 all-to-all-start.11
  758.4 5.3 all-to-all-done.11
  771.8 6.2 all-to-all-done.12
  788.5 19.9 %all-to-all-done.13 = bf16[8,88,768]{2,1,0:T(8,128)(2,1)S(1)} async-done(((bf16[8,88,768]{2,1,0:T(8,128)(2,1)}), bf16[8,88,768]{2,1,0:T(8,128)(2,1)S(1)}, u32[]{:S(2)}, u32[]{:S(2)}) %all-to-all-start.13) | async-done | bytes 1081376 | tf_op jit(solution)/shard_map/all_to_all | solution.py:907
  (726 shorter events, 428.9 us)
Async XLA Ops:
  7.2 93.2 %all-gather.5.cloned.1.call-start = ((), (), s32[]{:S(2)}) async-start(), calls=%async_computation.15 | async-start | bytes 3852288 | tf_op jit(solution)/shard_map/all_gather | solution.py:936
  16.5 41.8 %collective-permute-start = (bf16[128,768]{1,0:T(8,128)(2,1)}, bf16[128,768]{1,0:T(8,128)(2,1)}, u32[]{:S(2)}, u32[]{:S(2)}) collective-permute-start(bf16[128,768]{1,0:T(8,128)(2,1)} %bitcast.159), channel_id=1, source_target_pairs={{0,4},{4,0},{1,5},{5,1},{2,6},{6,2},{3,7},{7,3},{8,12},{12,8},{9,1... | collective-permute-start | bytes 589832 | tf_op jit(solution)/shard_map/ppermute | solution.py:831
  19.5 36.9 %collective-permute-start.2 = (bf16[128,768]{1,0:T(8,128)(2,1)}, bf16[128,768]{1,0:T(8,128)(2,1)}, u32[]{:S(2)}, u32[]{:S(2)}) collective-permute-start(bf16[128,768]{1,0:T(8,128)(2,1)} %bitcast.160), channel_id=1, source_target_pairs={{0,8},{8,16},{16,24},{24,0},{1,9},{9,17},{17,25},{25,1},{2,10},{10... | collective-permute-start | bytes 589832 | tf_op jit(solution)/shard_map/ppermute | solution.py:846
  21.1 38.9 %collective-permute-start.5 = (bf16[128,768]{1,0:T(8,128)(2,1)}, bf16[128,768]{1,0:T(8,128)(2,1)}, u32[]{:S(2)}, u32[]{:S(2)}) collective-permute-start(bf16[128,768]{1,0:T(8,128)(2,1)} %bitcast.161), channel_id=1, source_target_pairs={{0,16},{8,24},{16,0},{24,8},{1,17},{9,25},{17,1},{25,9},{2,18},{10... | collective-permute-start | bytes 589832 | tf_op jit(solution)/shard_map/ppermute | solution.py:846
  23.7 37.4 %collective-permute-start.8 = (bf16[128,768]{1,0:T(8,128)(2,1)}, bf16[128,768]{1,0:T(8,128)(2,1)}, u32[]{:S(2)}, u32[]{:S(2)}) collective-permute-start(bf16[128,768]{1,0:T(8,128)(2,1)} %bitcast.162), channel_id=1, source_target_pairs={{0,24},{8,0},{16,8},{24,16},{1,25},{9,1},{17,9},{25,17},{2,26},{10... | collective-permute-start | bytes 589832 | tf_op jit(solution)/shard_map/ppermute | solution.py:846
  27.7 38.6 %all-to-all-start = ((bf16[8,24,2048]{2,1,0:T(8,128)(2,1)}), bf16[8,24,2048]{2,1,0:T(8,128)(2,1)}, u32[]{:S(2)}, u32[]{:S(2)}) async-start(bf16[8,24,2048]{2,1,0:T(8,128)(2,1)} %get-tuple-element.323), calls=%async_computation | async-start | bytes 1572864 | tf_op jit(solution)/shard_map/all_to_all | solution.py:907
  32.1 126.0 %all-gather.7.cloned.1.call-start = ((), (), s32[]{:S(2)}) async-start(), calls=%async_computation.16 | async-start | bytes 1216512 | tf_op jit(solution)/shard_map/all_gather | solution.py:971
  66.3 34.1 %all-to-all-start.1 = ((bf16[8,24,2048]{2,1,0:T(8,128)(2,1)}), bf16[8,24,2048]{2,1,0:T(8,128)(2,1)}, u32[]{:S(2)}, u32[]{:S(2)}) async-start(bf16[8,24,2048]{2,1,0:T(8,128)(2,1)} %get-tuple-element.126), calls=%async_computation.1 | async-start | bytes 1572864 | tf_op jit(solution)/shard_map/all_to_all | solution.py:907
  71.4 160.6 %all-gather.9.cloned.1.call-start = ((), (), s32[]{:S(2)}) async-start(), calls=%async_computation.17 | async-start | bytes 3852288 | tf_op jit(solution)/shard_map/all_gather | solution.py:936
  118.8 43.3 %all-to-all-start.2 = ((bf16[8,64,768]{2,1,0:T(8,128)(2,1)}), bf16[8,64,768]{2,1,0:T(8,128)(2,1)S(1)}, u32[]{:S(2)}, u32[]{:S(2)}) async-start(bf16[8,64,768]{2,1,0:T(8,128)(2,1)} %get-tuple-element.136), calls=%async_computation.2 | async-start | bytes 1572864 | tf_op jit(solution)/shard_map/all_to_all | solution.py:907
  125.2 36.8 %collective-permute-start.12 = (bf16[192,2048]{1,0:T(8,128)(2,1)}, bf16[192,2048]{1,0:T(8,128)(2,1)S(1)}, u32[]{:S(2)}, u32[]{:S(2)}) collective-permute-start(bf16[192,2048]{1,0:T(8,128)(2,1)} %bitcast.10.refs_4_.refs_6_), channel_id=1, source_target_pairs={{0,1},{1,0},{2,3},{3,2},{4,5},{5,4},{6,7},{7,6},{8,9},{9,8},{10,11... | collective-permute-start | bytes 2359304 | tf_op jit(solution)/shard_map/ppermute | solution.py:831
  165.1 24.5 %collective-permute-start.21 = (bf16[192,2048]{1,0:T(8,128)(2,1)}, bf16[192,2048]{1,0:T(8,128)(2,1)S(1)}, u32[]{:S(2)}, u32[]{:S(2)}) collective-permute-start(bf16[192,2048]{1,0:T(8,128)(2,1)} %collective-permute-done.11.refs_1_.refs_3_), channel_id=1, source_target_pairs={{0,2},{2,0},{1,3},{3,1},{4,6},{6,4},{5,7},{7,5},{8,10},{10,8},{9,1... | collective-permute-start | bytes 2359304 | tf_op jit(solution)/shard_map/ppermute | solution.py:831
  165.1 23.5 %collective-permute-start.24 = (bf16[512,768]{1,0:T(8,128)(2,1)S(1)}, bf16[512,768]{1,0:T(8,128)(2,1)S(1)}, u32[]{:S(2)}, u32[]{:S(2)}) collective-permute-start(bf16[512,768]{1,0:T(8,128)(2,1)S(1)} %bitcast.150), channel_id=1, source_target_pairs={{0,1},{1,0},{2,3},{3,2},{4,5},{5,4},{6,7},{7,6},{8,9},{9,8},{10,11... | collective-permute-start | bytes 2359304 | tf_op jit(solution)/shard_map/ppermute | solution.py:831
  183.8 26.9 %all-to-all-start.3 = ((bf16[8,24,2048]{2,1,0:T(8,128)(2,1)}), bf16[8,24,2048]{2,1,0:T(8,128)(2,1)}, u32[]{:S(2)}, u32[]{:S(2)}) async-start(bf16[8,24,2048]{2,1,0:T(8,128)(2,1)} %get-tuple-element.142), calls=%async_computation.3 | async-start | bytes 1572864 | tf_op jit(solution)/shard_map/all_to_all | solution.py:907
  188.0 116.7 %all-gather.11.cloned.1.call-start = ((), (), s32[]{:S(2)}) async-start(), calls=%async_computation.18 | async-start | bytes 1216512 | tf_op jit(solution)/shard_map/all_gather | solution.py:971
  237.3 36.0 %collective-permute-start.45 = (bf16[192,2048]{1,0:T(8,128)(2,1)}, bf16[192,2048]{1,0:T(8,128)(2,1)}, u32[]{:S(2)}, u32[]{:S(2)}) collective-permute-start(bf16[192,2048]{1,0:T(8,128)(2,1)} %bitcast.39.refs_0_), channel_id=1, source_target_pairs={{0,1},{1,0},{2,3},{3,2},{4,5},{5,4},{6,7},{7,6},{8,9},{9,8},{10,11... | collective-permute-start | bytes 2359304 | tf_op jit(solution)/shard_map/ppermute | solution.py:831
  241.2 33.5 %all-to-all-start.4 = ((bf16[8,24,2048]{2,1,0:T(8,128)(2,1)}), bf16[8,24,2048]{2,1,0:T(8,128)(2,1)S(1)}, u32[]{:S(2)}, u32[]{:S(2)}) async-start(bf16[8,24,2048]{2,1,0:T(8,128)(2,1)} %get-tuple-element.148), calls=%async_computation.4 | async-start | bytes 1572864 | tf_op jit(solution)/shard_map/all_to_all | solution.py:907
  274.7 30.0 %all-to-all-start.5 = ((bf16[8,64,768]{2,1,0:T(8,128)(2,1)}), bf16[8,64,768]{2,1,0:T(8,128)(2,1)S(1)}, u32[]{:S(2)}, u32[]{:S(2)}) async-start(bf16[8,64,768]{2,1,0:T(8,128)(2,1)} %get-tuple-element.154), calls=%async_computation.5 | async-start | bytes 1572864 | tf_op jit(solution)/shard_map/all_to_all | solution.py:907
  281.7 40.9 %collective-permute-start.55 = (bf16[192,2048]{1,0:T(8,128)(2,1)}, bf16[192,2048]{1,0:T(8,128)(2,1)S(1)}, u32[]{:S(2)}, u32[]{:S(2)}) collective-permute-start(bf16[192,2048]{1,0:T(8,128)(2,1)} %collective-permute-done.45.refs_1_), channel_id=1, source_target_pairs={{0,2},{2,0},{1,3},{3,1},{4,6},{6,4},{5,7},{7,5},{8,10},{10,8},{9,1... | collective-permute-start | bytes 2359304 | tf_op jit(solution)/shard_map/ppermute | solution.py:831
  281.7 22.3 %collective-permute-start.46 = (bf16[192,2048]{1,0:T(8,128)(2,1)S(1)}, bf16[192,2048]{1,0:T(8,128)(2,1)S(1)}, u32[]{:S(2)}, u32[]{:S(2)}) collective-permute-start(bf16[192,2048]{1,0:T(8,128)(2,1)S(1)} %bitcast.167), channel_id=1, source_target_pairs={{0,1},{1,0},{2,3},{3,2},{4,5},{5,4},{6,7},{7,6},{8,9},{9,8},{10,11... | collective-permute-start | bytes 2359304 | tf_op jit(solution)/shard_map/ppermute | solution.py:831
  312.2 23.2 %collective-permute-start.58 = (bf16[512,768]{1,0:T(8,128)(2,1)S(1)}, bf16[512,768]{1,0:T(8,128)(2,1)S(1)}, u32[]{:S(2)}, u32[]{:S(2)}) collective-permute-start(bf16[512,768]{1,0:T(8,128)(2,1)S(1)} %bitcast.170), channel_id=1, source_target_pairs={{0,1},{1,0},{2,3},{3,2},{4,5},{5,4},{6,7},{7,6},{8,9},{9,8},{10,11... | collective-permute-start | bytes 2359304 | tf_op jit(solution)/shard_map/ppermute | solution.py:831
  390.6 21.3 %collective-permute-start.71 = (bf16[128,896]{1,0:T(8,128)(2,1)}, bf16[128,896]{1,0:T(8,128)(2,1)S(1)}, u32[]{:S(2)}, u32[]{:S(2)}) collective-permute-start(bf16[128,896]{1,0:T(8,128)(2,1)} %get-tuple-element.172.g_ref), channel_id=1, source_target_pairs={{0,16},{8,24},{16,0},{24,8},{1,17},{9,25},{17,1},{25,9},{2,18},{10... | collective-permute-start | bytes 688136 | tf_op jit(solution)/shard_map/ppermute | solution.py:846
  395.2 25.8 %collective-permute-start.69 = (bf16[128,896]{1,0:T(8,128)(2,1)}, bf16[128,896]{1,0:T(8,128)(2,1)S(1)}, u32[]{:S(2)}, u32[]{:S(2)}) collective-permute-start(bf16[128,896]{1,0:T(8,128)(2,1)} %get-tuple-element.172.g_ref), channel_id=1, source_target_pairs={{0,4},{4,0},{1,5},{5,1},{2,6},{6,2},{3,7},{7,3},{8,12},{12,8},{9,1... | collective-permute-start | bytes 688136 | tf_op jit(solution)/shard_map/ppermute | solution.py:831
  396.5 33.7 %collective-permute-start.77 = (bf16[128,896]{1,0:T(8,128)(2,1)}, bf16[128,896]{1,0:T(8,128)(2,1)S(1)}, u32[]{:S(2)}, u32[]{:S(2)}) collective-permute-start(bf16[128,896]{1,0:T(8,128)(2,1)} %get-tuple-element.172.g_ref), channel_id=1, source_target_pairs={{0,24},{8,0},{16,8},{24,16},{1,25},{9,1},{17,9},{25,17},{2,26},{10... | collective-permute-start | bytes 688136 | tf_op jit(solution)/shard_map/ppermute | solution.py:846
  400.5 46.1 %collective-permute-start.80 = (bf16[192,2048]{1,0:T(8,128)(2,1)}, bf16[192,2048]{1,0:T(8,128)(2,1)}, u32[]{:S(2)}, u32[]{:S(2)}) collective-permute-start(bf16[192,2048]{1,0:T(8,128)(2,1)} %slice.514), channel_id=1, source_target_pairs={{0,1},{1,0},{2,3},{3,2},{4,5},{5,4},{6,7},{7,6},{8,9},{9,8},{10,11... | collective-permute-start | bytes 2359304 | tf_op jit(solution)/shard_map/ppermute | solution.py:831
  430.2 34.3 %collective-permute-start.82 = (bf16[192,2048]{1,0:T(8,128)(2,1)S(1)}, bf16[192,2048]{1,0:T(8,128)(2,1)}, u32[]{:S(2)}, u32[]{:S(2)}) collective-permute-start(bf16[192,2048]{1,0:T(8,128)(2,1)S(1)} %slice.516), channel_id=1, source_target_pairs={{0,1},{1,0},{2,3},{3,2},{4,5},{5,4},{6,7},{7,6},{8,9},{9,8},{10,11... | collective-permute-start | bytes 2359304 | tf_op jit(solution)/shard_map/ppermute | solution.py:831
  454.2 26.6 %all-to-all-start.6 = ((bf16[8,24,2048]{2,1,0:T(8,128)(2,1)}), bf16[8,24,2048]{2,1,0:T(8,128)(2,1)S(1)}, u32[]{:S(2)}, u32[]{:S(2)}) async-start(bf16[8,24,2048]{2,1,0:T(8,128)(2,1)} %bitcast.53), calls=%async_computation.6 | async-start | bytes 1572864 | tf_op jit(solution)/shard_map/all_to_all | solution.py:907
  461.7 36.2 %collective-permute-start.91 = (bf16[8,128,768]{2,1,0:T(8,128)(2,1)}, bf16[8,128,768]{2,1,0:T(8,128)(2,1)}, u32[]{:S(2)}, u32[]{:S(2)}) collective-permute-start(bf16[8,128,768]{2,1,0:T(8,128)(2,1)} %get-tuple-element.200), channel_id=1, source_target_pairs={{0,2},{2,0},{1,3},{3,1},{4,6},{6,4},{5,7},{7,5},{8,10},{10,8},{9,1... | collective-permute-start | bytes 4718600 | tf_op jit(solution)/shard_map/ppermute | solution.py:831
  481.8 24.1 %all-to-all-start.7 = ((bf16[8,24,2048]{2,1,0:T(8,128)(2,1)}), bf16[8,24,2048]{2,1,0:T(8,128)(2,1)S(1)}, u32[]{:S(2)}, u32[]{:S(2)}) async-start(bf16[8,24,2048]{2,1,0:T(8,128)(2,1)} %bitcast.54), calls=%async_computation.7 | async-start | bytes 1572864 | tf_op jit(solution)/shard_map/all_to_all | solution.py:907
  498.0 40.9 %collective-permute-start.90 = (bf16[384,2432]{1,0:T(8,128)(2,1)}, bf16[384,2432]{1,0:T(8,128)(2,1)}, u32[]{:S(2)}, u32[]{:S(2)}) collective-permute-start(bf16[384,2432]{1,0:T(8,128)(2,1)} %get-tuple-element.194), channel_id=1, source_target_pairs={{0,2},{2,0},{1,3},{3,1},{4,6},{6,4},{5,7},{7,5},{8,10},{10,8},{9,1... | collective-permute-start | bytes 5603336 | tf_op jit(solution)/shard_map/ppermute | solution.py:831
  505.0 44.5 %collective-permute-start.117 = (bf16[384,768]{1,0:T(8,128)(2,1)}, bf16[384,768]{1,0:T(8,128)(2,1)}, u32[]{:S(2)}, u32[]{:S(2)}) collective-permute-start(bf16[384,768]{1,0:T(8,128)(2,1)} %get-tuple-element.231), channel_id=1, source_target_pairs={{0,2},{2,0},{1,3},{3,1},{4,6},{6,4},{5,7},{7,5},{8,10},{10,8},{9,1... | collective-permute-start | bytes 1769480 | tf_op jit(solution)/shard_map/ppermute | solution.py:831
  544.1 35.8 %all-to-all-start.8 = ((bf16[8,64,768]{2,1,0:T(8,128)(2,1)}), bf16[8,64,768]{2,1,0:T(8,128)(2,1)}, u32[]{:S(2)}, u32[]{:S(2)}) async-start(bf16[8,64,768]{2,1,0:T(8,128)(2,1)} %add_convert_fusion.11), calls=%async_computation.8 | async-start | bytes 1572864 | tf_op jit(solution)/shard_map/all_to_all | solution.py:907
  549.2 203.5 %reduce-scatter.4.cloned.1.call-start = ((), (), s32[]{:S(2)}) async-start(), calls=%async_computation.19 | async-start | bytes 1382400
  559.7 23.8 %collective-permute-start.100 = (bf16[192,2432]{1,0:T(8,128)(2,1)}, bf16[192,2432]{1,0:T(8,128)(2,1)}, u32[]{:S(2)}, u32[]{:S(2)}) collective-permute-start(bf16[192,2432]{1,0:T(8,128)(2,1)} %slice.518), channel_id=1, source_target_pairs={{0,1},{1,0},{2,3},{3,2},{4,5},{5,4},{6,7},{7,6},{8,9},{9,8},{10,11... | collective-permute-start | bytes 2801672 | tf_op jit(solution)/shard_map/ppermute | solution.py:831
  579.3 25.3 %collective-permute-start.101 = (bf16[384,2048]{1,0:T(8,128)(2,1)}, bf16[384,2048]{1,0:T(8,128)(2,1)}, u32[]{:S(2)}, u32[]{:S(2)}) collective-permute-start(bf16[384,2048]{1,0:T(8,128)(2,1)} %get-tuple-element.205), channel_id=1, source_target_pairs={{0,2},{2,0},{1,3},{3,1},{4,6},{6,4},{5,7},{7,5},{8,10},{10,8},{9,1... | collective-permute-start | bytes 4718600 | tf_op jit(solution)/shard_map/ppermute | solution.py:831
  579.4 38.9 %collective-permute-start.115 = (bf16[384,2048]{1,0:T(8,128)(2,1)}, bf16[384,2048]{1,0:T(8,128)(2,1)S(1)}, u32[]{:S(2)}, u32[]{:S(2)}) collective-permute-start(bf16[384,2048]{1,0:T(8,128)(2,1)} %get-tuple-element.225), channel_id=1, source_target_pairs={{0,2},{2,0},{1,3},{3,1},{4,6},{6,4},{5,7},{7,5},{8,10},{10,8},{9,1... | collective-permute-start | bytes 4718600 | tf_op jit(solution)/shard_map/ppermute | solution.py:831
  614.8 28.9 %collective-permute-start.102 = (bf16[128,896]{1,0:T(8,128)(2,1)}, bf16[128,896]{1,0:T(8,128)(2,1)S(1)}, u32[]{:S(2)}, u32[]{:S(2)}) collective-permute-start(bf16[128,896]{1,0:T(8,128)(2,1)} %get-tuple-element.209.g_ref), channel_id=1, source_target_pairs={{0,4},{4,0},{1,5},{5,1},{2,6},{6,2},{3,7},{7,3},{8,12},{12,8},{9,1... | collective-permute-start | bytes 688136 | tf_op jit(solution)/shard_map/ppermute | solution.py:831
  616.4 36.5 %collective-permute-start.110 = (bf16[128,896]{1,0:T(8,128)(2,1)}, bf16[128,896]{1,0:T(8,128)(2,1)S(1)}, u32[]{:S(2)}, u32[]{:S(2)}) collective-permute-start(bf16[128,896]{1,0:T(8,128)(2,1)} %get-tuple-element.209.g_ref), channel_id=1, source_target_pairs={{0,24},{8,0},{16,8},{24,16},{1,25},{9,1},{17,9},{25,17},{2,26},{10... | collective-permute-start | bytes 688136 | tf_op jit(solution)/shard_map/ppermute | solution.py:846
  618.2 53.6 %collective-permute-start.113 = (bf16[192,2048]{1,0:T(8,128)(2,1)}, bf16[192,2048]{1,0:T(8,128)(2,1)}, u32[]{:S(2)}, u32[]{:S(2)}) collective-permute-start(bf16[192,2048]{1,0:T(8,128)(2,1)} %slice.522), channel_id=1, source_target_pairs={{0,1},{1,0},{2,3},{3,2},{4,5},{5,4},{6,7},{7,6},{8,9},{9,8},{10,11... | collective-permute-start | bytes 2359304 | tf_op jit(solution)/shard_map/ppermute | solution.py:831
  652.9 36.3 %collective-permute-start.119 = (bf16[8,128,768]{2,1,0:T(8,128)(2,1)}, bf16[8,128,768]{2,1,0:T(8,128)(2,1)S(1)}, u32[]{:S(2)}, u32[]{:S(2)}) collective-permute-start(bf16[8,128,768]{2,1,0:T(8,128)(2,1)} %get-tuple-element.234), channel_id=1, source_target_pairs={{0,2},{2,0},{1,3},{3,1},{4,6},{6,4},{5,7},{7,5},{8,10},{10,8},{9,1... | collective-permute-start | bytes 4718600 | tf_op jit(solution)/shard_map/ppermute | solution.py:831
  662.5 60.7 %collective-permute-start.116 = (bf16[192,2048]{1,0:T(8,128)(2,1)}, bf16[192,2048]{1,0:T(8,128)(2,1)}, u32[]{:S(2)}, u32[]{:S(2)}) collective-permute-start(bf16[192,2048]{1,0:T(8,128)(2,1)} %slice.524), channel_id=1, source_target_pairs={{0,1},{1,0},{2,3},{3,2},{4,5},{5,4},{6,7},{7,6},{8,9},{9,8},{10,11... | collective-permute-start | bytes 2359304 | tf_op jit(solution)/shard_map/ppermute | solution.py:831
  668.9 27.9 %collective-permute-start.121 = (bf16[384,768]{1,0:T(8,128)(2,1)}, bf16[384,768]{1,0:T(8,128)(2,1)}, u32[]{:S(2)}, u32[]{:S(2)}) collective-permute-start(bf16[384,768]{1,0:T(8,128)(2,1)} %get-tuple-element.238), channel_id=1, source_target_pairs={{0,2},{2,0},{1,3},{3,1},{4,6},{6,4},{5,7},{7,5},{8,10},{10,8},{9,1... | collective-permute-start | bytes 1769480 | tf_op jit(solution)/shard_map/ppermute | solution.py:831
  680.0 36.9 %all-to-all-start.9 = ((bf16[8,24,2048]{2,1,0:T(8,128)(2,1)}), bf16[8,24,2048]{2,1,0:T(8,128)(2,1)}, u32[]{:S(2)}, u32[]{:S(2)}) async-start(bf16[8,24,2048]{2,1,0:T(8,128)(2,1)} %bitcast.56), calls=%async_computation.9 | async-start | bytes 1572864 | tf_op jit(solution)/shard_map/all_to_all | solution.py:907
  693.8 31.8 %collective-permute-start.120 = (bf16[8,64,768]{2,1,0:T(8,128)(2,1)}, bf16[8,64,768]{2,1,0:T(8,128)(2,1)}, u32[]{:S(2)}, u32[]{:S(2)}) collective-permute-start(bf16[8,64,768]{2,1,0:T(8,128)(2,1)} %slice.530), channel_id=1, source_target_pairs={{0,1},{1,0},{2,3},{3,2},{4,5},{5,4},{6,7},{7,6},{8,9},{9,8},{10,11... | collective-permute-start | bytes 2359304 | tf_op jit(solution)/shard_map/ppermute | solution.py:831
  699.6 27.4 %collective-permute-start.122 = (bf16[192,768]{1,0:T(8,128)(2,1)}, bf16[192,768]{1,0:T(8,128)(2,1)S(1)}, u32[]{:S(2)}, u32[]{:S(2)}) collective-permute-start(bf16[192,768]{1,0:T(8,128)(2,1)} %slice.532), channel_id=1, source_target_pairs={{0,1},{1,0},{2,3},{3,2},{4,5},{5,4},{6,7},{7,6},{8,9},{9,8},{10,11... | collective-permute-start | bytes 884744 | tf_op jit(solution)/shard_map/ppermute | solution.py:831
  716.9 21.9 %all-to-all-start.10 = ((bf16[16,128,144]{1,2,0:T(8,128)(2,1)}), bf16[16,128,144]{1,2,0:T(8,128)(2,1)}, u32[]{:S(2)}, u32[]{:S(2)}) async-start(bf16[16,128,144]{1,2,0:T(8,128)(2,1)} %bitcast.158), calls=%async_computation.10 | async-start | bytes 1179648 | tf_op jit(solution)/shard_map/all_to_all | solution.py:1337
  738.8 24.9 %all-to-all-start.11 = ((bf16[8,24,2048]{2,1,0:T(8,128)(2,1)}), bf16[8,24,2048]{2,1,0:T(8,128)(2,1)S(1)}, u32[]{:S(2)}, u32[]{:S(2)}) async-start(bf16[8,24,2048]{2,1,0:T(8,128)(2,1)} %bitcast.83), calls=%async_computation.11 | async-start | bytes 1572864 | tf_op jit(solution)/shard_map/all_to_all | solution.py:907
  778.1 30.3 %all-to-all-start.13 = ((bf16[8,88,768]{2,1,0:T(8,128)(2,1)}), bf16[8,88,768]{2,1,0:T(8,128)(2,1)S(1)}, u32[]{:S(2)}, u32[]{:S(2)}) async-start(bf16[8,88,768]{2,1,0:T(8,128)(2,1)} %pad_maximum_fusion.1), calls=%async_computation.13 | async-start | bytes 2162688 | tf_op jit(solution)/shard_map/all_to_all | solution.py:907
  (184 other events, 1938.6 us)
Sparse Core Ops, SparseCore 0:
  16.6 83.3 all-gather.4
  103.0 55.0 all-gather.6
  161.1 70.8 all-gather.8
  237.5 66.2 all-gather.10
  604.7 71.8 reduce-scatter.3

commit v3 on v2

--- a/solution.py
+++ b/solution.py
@@ -32,6 +32,7 @@
 f32 = jnp.float32
 bf16 = jnp.bfloat16
 VMEM_LIMIT = 56 * 1024 * 1024
+SPLIT = 3
 
 AT_CONST = 16
 AT_CVEC = 24
@@ -65,44 +66,72 @@
     return x * cosine + partner * sine
 
 
-def project_kernel(turned, a_ref, *refs):
-    count = len(turned)
-    w_refs = refs[:count]
-    cos_ref, sin_ref = refs[count : count + 2]
-    out_refs = refs[count + 2 :]
-    a = a_ref[...]
-    for w_ref, out_ref, turn in zip(w_refs, out_refs, turned):
-        acc = dot_nn(a, w_ref[...])
-        if not turn:
-            out_ref[...] = acc.astype(bf16)
-            continue
-        for at in range(0, acc.shape[1], LANES):
-            part = turn_lanes(acc[:, at : at + LANES], cos_ref[...], sin_ref[...])
-            out_ref[:, at : at + LANES] = part.astype(bf16)
-
-
-def project(rows, packed, columns, turned, cosine, sine):
-    count, width = rows.shape
-    tile = min(count, 512)
-    w_specs = [
-        pl.BlockSpec((width, width), functools.partial(lambda at, i: (0, at), at))
-        for at in columns
-    ]
-    row_spec = pl.BlockSpec((tile, width), lambda i: (i, 0))
-    table = pl.BlockSpec((tile, LANES), lambda i: (i, 0))
+def once(shape, index):
+    return pl.BlockSpec(shape, index, pipeline_mode=pl.Buffered(1))
+
+
+def project_kernel(turned, count, fresh, *refs):
+    w_ref, small_ref, cos_ref, sin_ref, out_ref = refs[count : count + 5]
+    sources = [(ref, 0, ref.shape[0]) for ref in refs[:count]]
+    if fresh:
+        low_ref = refs[count + 5]
+
+        @pl.when(pl.program_id(0) == 0)
+        def _():
+            line = line_of(small_ref, AT_ATTN)
+            start = 0
+            for ref, _, tall in sources:
+                x = ref[...].astype(f32)
+                low_ref[start : start + tall] = (x * root_scale(x) * line).astype(bf16)
+                start += tall
+
+        sources = [(low_ref, 0, low_ref.shape[0])]
+    weights = w_ref[...]
+
+    def walk(turn):
+        start = 0
+        for a_ref, _, whole in sources:
+            for low in range(0, whole, 256):
+                tall = min(256, whole - low)
+                acc = dot_nn(a_ref[low : low + tall], weights)
+                place = slice(start + low, start + low + tall)
+                for at in range(0, acc.shape[1], LANES):
+                    part = acc[:, at : at + LANES]
+                    if turn:
+                        part = turn_lanes(part, cos_ref[place], sin_ref[place])
+                    out_ref[place, at : at + LANES] = part.astype(bf16)
+            start += whole
+
+    @pl.when(pl.program_id(0) < turned)
+    def _():
+        walk(True)
+
+    @pl.when(pl.program_id(0) >= turned)
+    def _():
+        walk(False)
+
+
+def project(blocks, packed, cosine, sine, fresh=False):
+    width = blocks[0].shape[1]
+    count = sum(block.shape[0] for block in blocks)
+    tile = width // SPLIT
+    table = once((count, LANES), lambda i: (0, 0))
     return pl.pallas_call(
-        functools.partial(project_kernel, turned),
-        grid=(count // tile,),
-        in_specs=[row_spec] + w_specs + [table, table],
-        out_specs=[row_spec] * len(columns),
-        out_shape=[jax.ShapeDtypeStruct((count, width), bf16)] * len(columns),
+        functools.partial(project_kernel, 2 * SPLIT, len(blocks), fresh),
+        grid=(3 * SPLIT,),
+        in_specs=[once(block.shape, lambda i: (0, 0)) for block in blocks]
+        + [pl.BlockSpec((width, tile), lambda i: (0, i))]
+        + [once((width, LANES), lambda i: (0, 4 * width // LANES)), table, table],
+        out_specs=pl.BlockSpec((count, tile), lambda i: (0, i)),
+        out_shape=jax.ShapeDtypeStruct((count, 3 * width), bf16),
+        scratch_shapes=[pltpu.VMEM((count, width), bf16)] if fresh else [],
         compiler_params=kernel_params(1),
         cost_estimate=pl.CostEstimate(
-            flops=2 * count * width * width * len(columns),
-            bytes_accessed=2 * width * (count * (1 + len(columns)) + width * len(columns)),
+            flops=6 * count * width * width,
+            bytes_accessed=2 * width * (4 * count + 3 * width),
             transcendentals=0,
         ),
-    )(rows, *([packed] * len(columns)), cosine, sine)
+    )(*blocks, packed, packed, cosine, sine)
 
 
 def split_heads(x):
@@ -148,17 +177,18 @@
     total_ref[...] = totals
 
 
-def attend(queries, keys, values, places, starts, key_places, prompt):
-    rows, width = places.shape[0], queries.shape[1]
-    length = keys.shape[0]
+def attend(projected, places, starts, key_places, prompt):
+    rows = places.shape[0]
+    length, width = projected.shape[0], projected.shape[1] // 3
     own = pl.BlockSpec((rows, LANES), lambda j: (0, j))
-    every = pl.BlockSpec((length, LANES), lambda j: (0, j))
+    keys = pl.BlockSpec((length, LANES), lambda j: (0, PAIRS + j))
+    values = pl.BlockSpec((length, LANES), lambda j: (0, 2 * PAIRS + j))
     column = pl.BlockSpec((rows, 1), lambda j: (0, 0))
     line = pl.BlockSpec((1, length), lambda j: (0, 0))
     return pl.pallas_call(
         functools.partial(attend_kernel, prompt),
         grid=(PAIRS,),
-        in_specs=[own, every, every, column, column, line],
+        in_specs=[own, keys, values, column, column, line],
         out_specs=[own, pl.BlockSpec((rows, LANES), lambda j: (0, 0))],
         out_shape=[
             jax.ShapeDtypeStruct((rows, width), f32),
@@ -171,7 +201,7 @@
             bytes_accessed=4 * length * width,
             transcendentals=rows * length * HEADS,
         ),
-    )(queries, keys, values, places, starts, key_places)
+    )(projected, projected, projected, places, starts, key_places)
 
 
 def pick_column(table, at):
@@ -225,12 +255,13 @@
 
 
 def query_back(
-    start, count, queries, grads, keys, values, totals, delta, places, starts, key_places, cosine, sine, prompt
+    start, count, projected, grads, totals, delta, places, starts, key_places, cosine, sine, prompt
 ):
     rows = places.shape[0]
-    length = keys.shape[0]
+    length = projected.shape[0]
     own = pl.BlockSpec((rows, LANES), lambda j: (0, j + start))
-    every = pl.BlockSpec((length, LANES), lambda j: (0, j + start))
+    keys = pl.BlockSpec((length, LANES), lambda j: (0, PAIRS + j + start))
+    values = pl.BlockSpec((length, LANES), lambda j: (0, 2 * PAIRS + j + start))
     same = pl.BlockSpec((rows, LANES), lambda j: (0, 0))
     column = pl.BlockSpec((rows, 1), lambda j: (0, 0))
     line = pl.BlockSpec((1, length), lambda j: (0, 0))
@@ -238,7 +269,7 @@
     return pl.pallas_call(
         functools.partial(query_kernel, prompt, start),
         grid=(count,),
-        in_specs=[own, own, every, every, same, same, column, column, line, same, same],
+        in_specs=[own, own, keys, values, same, same, column, column, line, same, same],
         out_specs=pl.BlockSpec((rows, LANES), lambda j: (0, j)),
         out_shape=jax.ShapeDtypeStruct((rows, width), bf16),
         scratch_shapes=[pltpu.VMEM((rows, length), f32)],
@@ -248,26 +279,25 @@
             bytes_accessed=4 * length * width,
             transcendentals=rows * length * HEADS,
         ),
-    )(queries, grads, keys, values, totals, delta, places, starts, key_places, cosine, sine)
-
-
-def key_kernel(
-    prompt,
-    k_ref,
-    v_ref,
-    q_ref,
-    g_ref,
-    stat_ref,
-    own_ref,
-    at_ref,
-    start_ref,
-    cos_ref,
-    sin_ref,
-    dk_ref,
-    dv_ref,
-    bias_ref,
-    lines_ref,
-):
+    )(
+        projected,
+        grads,
+        projected,
+        projected,
+        totals,
+        delta,
+        places,
+        starts,
+        key_places,
+        cosine,
+        sine,
+    )
+
+
+def key_kernel(prompt, count, k_ref, v_ref, q_ref, *refs):
+    grad_refs, stat_refs = refs[:count], refs[count : 2 * count]
+    own_ref, at_ref, start_ref, cos_ref, sin_ref = refs[2 * count : 2 * count + 5]
+    dk_ref, dv_ref, bias_ref, lines_ref = refs[2 * count + 5 :]
     pair = pl.program_id(0)
     rows = k_ref.shape[0]
 
@@ -276,7 +306,7 @@
         keys, places = own_ref[...], at_ref[...]
         seen = (keys <= places) & ((keys < prompt) | (keys >= start_ref[...]))
         bias_ref[...] = jnp.where(seen, 0.0, masked_score)
-        flat = stat_ref[...].astype(f32).T
+        flat = stack_rows(stat_refs).astype(f32).T
         for head in range(HEADS):
             lines_ref[head] = flat[head : head + 1] + flat[16 + head : 17 + head]
             lines_ref[16 + head] = flat[32 + head : 33 + head] + flat[48 + head : 49 + head]
@@ -284,7 +314,7 @@
     scale = HEAD_DIM ** (-0.5)
     own_keys = split_heads(k_ref[...] * scale)
     own_values = split_heads(v_ref[...])
-    queries, grads = q_ref[...], g_ref[...]
+    queries, grads = q_ref[...], stack_rows(grad_refs)
     lane = lax.broadcasted_iota(jnp.int32, (rows, LANES), 1)
     key_outs, value_outs = [], []
     for side in range(2):
@@ -303,20 +333,24 @@
     dv_ref[...] = jnp.where(left, value_outs[0], value_outs[1]).astype(bf16)
 
 
-def key_back(own_keys, own_values, queries, sent, own_places, places, starts, cosine, sine, prompt):
+def key_back(projected, sent, own_places, places, starts, cosine, sine, prompt):
     rows = own_places.shape[0]
-    length, width = queries.shape
-    own = pl.BlockSpec((rows, LANES), lambda j: (0, j))
+    length, width = projected.shape[0], projected.shape[1] // 3
+    out = pl.BlockSpec((rows, LANES), lambda j: (0, j))
+    keys = pl.BlockSpec((rows, LANES), lambda j: (0, PAIRS + j))
+    values = pl.BlockSpec((rows, LANES), lambda j: (0, 2 * PAIRS + j))
     every = pl.BlockSpec((length, LANES), lambda j: (0, j))
-    stats = pl.BlockSpec((length, LANES), lambda j: (0, PAIRS))
     same = pl.BlockSpec((rows, LANES), lambda j: (0, 0))
     column = pl.BlockSpec((rows, 1), lambda j: (0, 0))
     line = pl.BlockSpec((1, length), lambda j: (0, 0))
     return pl.pallas_call(
-        functools.partial(key_kernel, prompt),
+        functools.partial(key_kernel, prompt, len(sent)),
         grid=(PAIRS,),
-        in_specs=[own, own, every, every, stats, column, line, line, same, same],
-        out_specs=[own, own],
+        in_specs=[keys, values, every]
+        + [pl.BlockSpec((block.shape[0], LANES), lambda j: (0, j)) for block in sent]
+        + [pl.BlockSpec((block.shape[0], LANES), lambda j: (0, PAIRS)) for block in sent]
+        + [column, line, line, same, same],
+        out_specs=[out, out],
         out_shape=[jax.ShapeDtypeStruct((rows, width), bf16)] * 2,
         scratch_shapes=[
             pltpu.VMEM((rows, length), f32),
@@ -328,7 +362,7 @@
             bytes_accessed=4 * length * width,
             transcendentals=rows * length * HEADS,
         ),
-    )(own_keys, own_values, queries, sent, sent, own_places, places, starts, cosine, sine)
+    )(projected, projected, projected, *sent, *sent, own_places, places, starts, cosine, sine)
 
 
 def cross(x, flag_ref):
@@ -560,31 +594,32 @@
     return small_ref[...].astype(f32).T[at : at + 1]
 
 
-def norm_kernel(x_ref, small_ref, out_ref, line_ref):
-    @pl.when(pl.program_id(0) == 0)
-    def _():
-        line_ref[...] = line_of(small_ref, AT_ATTN)
-
-    x = x_ref[...].astype(f32)
-    out_ref[...] = (x * root_scale(x) * line_ref[...]).astype(bf16)
-
-
-def norm_rows(x, packed):
-    count, width = x.shape
-    tile = min(count, 512)
-    spec = pl.BlockSpec((tile, width), lambda i: (i, 0))
+def norm_kernel(*refs):
+    small_ref, out_ref = refs[-2:]
+    line = line_of(small_ref, AT_ATTN)
+    start = 0
+    for x_ref in refs[:-2]:
+        tall = x_ref.shape[0]
+        x = x_ref[...].astype(f32)
+        out_ref[start : start + tall] = (x * root_scale(x) * line).astype(bf16)
+        start += tall
+
+
+def norm_rows(blocks, packed):
+    width = blocks[0].shape[1]
+    count = sum(block.shape[0] for block in blocks)
     return pl.pallas_call(
         norm_kernel,
-        grid=(count // tile,),
-        in_specs=[spec, pl.BlockSpec((width, LANES), lambda i: (0, 3 * width // LANES))],
-        out_specs=spec,
+        grid=(1,),
+        in_specs=[once(block.shape, lambda i: (0, 0)) for block in blocks]
+        + [pl.BlockSpec((width, LANES), lambda i: (0, 4 * width // LANES))],
+        out_specs=once((count, width), lambda i: (0, 0)),
         out_shape=jax.ShapeDtypeStruct((count, width), bf16),
-        scratch_shapes=[pltpu.VMEM((1, width), f32)],
         compiler_params=kernel_params(1),
         cost_estimate=pl.CostEstimate(
             flops=8 * count * width, bytes_accessed=4 * count * width, transcendentals=0
         ),
-    )(x, packed)
+    )(*blocks, packed)
 
 
 def pair_partner(x):
@@ -771,12 +806,16 @@
     return dot_nn(turned, top) + dot_nn(turned, (x - top.astype(f32)).astype(bf16))
 
 
-def from_attention_kernel(final, q_ref, k_ref, v_ref, wq_ref, wk_ref, wv_ref, hidden_ref, small_ref, mid_grad_ref, *refs):
+def from_attention_kernel(final, *refs):
+    q_refs, (k_ref, v_ref, wq_ref, wk_ref, wv_ref) = refs[:3], refs[3:8]
+    hidden_ref, small_ref, mid_grad_ref = refs[8:11]
+    refs = refs[11:]
     if final:
         grad_ref, line_grad_ref = refs
     else:
         chance_ref, first_ref, second_ref, slot_pairs_ref, grad_ref, line_grad_ref, message_ref = refs
-    normed_grad = dot_nt(q_ref[...], wq_ref[...])
+    queries = jnp.concatenate([ref[...] for ref in q_refs], axis=1)
+    normed_grad = dot_nt(queries, wq_ref[...])
     normed_grad += dot_nt(k_ref[...], wk_ref[...])
     normed_grad += dot_nt(v_ref[...], wv_ref[...])
     part, gain_grad = rms_back_rows(
@@ -827,6 +866,81 @@
     return lax.optimization_barrier((x,) + things)[0]
 
 
+TABLE = {
+    "a_g0": ("", ""),
+    "a_u0": ("", "packed0"),
+    "a_d0": ("packed0", "proj0"),
+    "x_g0": ("", "packed0"),
+    "x_u0": ("packed0", "proj0"),
+    "x_d0": ("proj0", "ein0"),
+    "c_g0": ("packed0", ""),
+    "c_u0": ("proj0", ""),
+    "c_d0": ("", ""),
+    "k_1": ("proj0", ""),
+    "a_g1": ("proj0", "msg0"),
+    "a_u1": ("ein0", "eout0"),
+    "a_d1": ("ag1", "att1"),
+    "x_g1": ("eout0", "ag1"),
+    "x_u1": ("ag1", ""),
+    "x_d1": ("att1", ""),
+    "c_g1": ("msg1", ""),
+    "c_u1": ("msg1", ""),
+    "c_d1": ("msg1", ""),
+    "cj_g1": ("", ""),
+    "cj_u1": ("", ""),
+    "cj_d1": ("", ""),
+    "xj_g1": ("", "sall1"),
+    "xj_u1": ("", ""),
+    "xj_d1": ("", ""),
+    "p_o1": ("slot0", ""),
+    "xj_o1": ("", ""),
+    "r_g1": ("sall1", "key1"),
+    "p_q1": ("og0", ""),
+    "xj_q1": ("", "key0"),
+    "r_u1": ("og0", "ig0"),
+    "r_d1": ("sall0", "cols0"),
+    "cj_g0": ("", ""),
+    "cj_u0": ("", ""),
+    "cj_d0": ("", ""),
+    "xj_g0": ("", ""),
+    "xj_u0": ("", ""),
+    "xj_d0": ("", ""),
+    "p_o0": ("sall0", ""),
+    "xj_o0": ("", ""),
+    "rs": ("key0", "part"),
+    "r_u0": ("cols", "part0"),
+    "r_d0": ("part", ""),
+}
+
+
+class Plan:
+    def __init__(self, table):
+        self.table, self.make, self.found, self.passed = table, {}, {}, {"": True}
+
+    def add(self, name, build):
+        self.make[name] = build
+        if self.table[name][0] in self.passed:
+            self.get(name)
+
+    def get(self, name):
+        if name not in self.found:
+            self.found[name] = self.make[name](lambda x: x)
+        return self.found[name]
+
+    def point(self, at, value):
+        done = []
+        for name, (_, end) in self.table.items():
+            if end == at and name in self.make:
+                done += jax.tree.leaves(self.get(name))
+        if done:
+            value = after(value, *done)
+        self.passed[at] = True
+        for name, (start, _) in self.table.items():
+            if start == at and name in self.make and name not in self.found:
+                self.found[name] = self.make[name](lambda x: after(x, value))
+        return value
+
+
 def swap(x, axis):
     return lax.ppermute(x, axis, [(0, 1), (1, 0)])
 
@@ -846,13 +960,12 @@
         found.append(lax.ppermute(x, far, pairs))
     blocks, filled = [], []
     for step, block in enumerate(found):
-        beside = swap(block, near)
-        if step < len(fillers):
-            filled.append(fillers[step](beside if step == 0 else block))
-        pair = jnp.concatenate([block, beside], axis=0)
+        if 0 < step <= len(fillers):
+            filled.append(fillers[step - 1](block if step > 1 else blocks[0]))
+            block = after(block, filled[-1])
+        pair = jnp.concatenate([block, swap(block, near)], axis=0)
         blocks += [pair, swap(pair, core)]
-    rows = jnp.concatenate(blocks, axis=0)
-    return (rows, filled) if fillers else rows
+    return (blocks, filled) if fillers else blocks
 
 
 def gathered_order(axes):
@@ -901,26 +1014,21 @@
     fs_at = lax.axis_index(FS)
     sub_at = lax.axis_index(sub_axes)
 
-    ex_at = lax.axis_index(ex_axes)
 
     def deal_out(x):
         return lax.all_to_all(x, ex_axes, 0, 0, tiled=True)
 
     def dispatch(x):
-        blocks = [x[:SLOTS]]
-        for step in range(1, EXPERTS):
-            block = x[step * SLOTS : (step + 1) * SLOTS]
-            pairs = [(at, at ^ step) for at in range(EXPERTS)]
-            blocks.append(lax.ppermute(block, ex_axes, pairs))
-        return jnp.concatenate(blocks, axis=0)
+        return deal_out(x.reshape(EXPERTS, SLOTS, -1)).reshape(x.shape)
 
     def blank(count):
         return jnp.zeros((own_rows, count), bf16)
 
-    def fetch_packed(layer, *wait):
+    def fetch_packed(layer, tie):
         mine = jnp.concatenate(
             [
                 w_qkv[layer],
+                w_out[layer],
                 w_router[layer],
                 blank(AT_CONST - ROUTED),
                 w_const[layer],
@@ -933,28 +1041,38 @@
             ],
             axis=1,
         )
-        return lax.all_gather(after(mine, *wait), every_axis, axis=0, tiled=True)
+        return lax.all_gather(tie(mine), every_axis, axis=0, tiled=True)
 
     by_chunks = subs == 2
     flags = jnp.stack([sub_at, fs_at]).astype(jnp.int32)[None, :]
 
-    def move_in(member, *wait):
-        moved = deal_out(after(member, *wait))
-        return moved.reshape(-1, moved.shape[2]) if by_chunks else moved
-
-    def spread(moved, *wait):
-        moved = after(moved, *wait)
-        if not by_chunks:
-            whole = lax.all_gather(moved, sub_axes + (FS,), axis=1, tiled=True)
-            return (whole.reshape(-1, whole.shape[2]),)
-        across = swap(moved, FS)
-        return (moved, across)
-
-    def share(parts, *wait):
-        if not by_chunks:
-            return parts[0]
-        moved, across = after(parts[0], *wait), parts[1]
-        return (moved, across, swap(moved, sub_axes[0]), swap(across, sub_axes[0]))
+    plan = Plan(TABLE)
+
+    def add_weight(name, member):
+        plan.add(
+            "a_" + name,
+            lambda tie: deal_out(tie(member)).reshape(-1, member.shape[-1]),
+        )
+        plan.add("x_" + name, lambda tie: swap(tie(plan.get("a_" + name)), FS))
+        plan.add(
+            "c_" + name,
+            lambda tie: (
+                swap(tie(plan.get("a_" + name)), sub_axes[0]),
+                swap(plan.get("x_" + name), sub_axes[0]),
+            ),
+        )
+
+    def weights_of(layer):
+        found = []
+        for name, member in zip("gud", (w_gate, w_up, w_down)):
+            if by_chunks:
+                parts = [plan.get(part + name + str(layer)) for part in ("a_", "x_", "c_")]
+                found.append((parts[0], parts[1]) + parts[2])
+            else:
+                moved = deal_out(member[layer])
+                whole = lax.all_gather(moved, sub_axes + (FS,), axis=1, tiled=True)
+                found.append(whole.reshape(-1, whole.shape[2]))
+        return found
 
     if not by_chunks:
         to_chunks = jnp.eye(width, dtype=bf16)
@@ -967,18 +1085,7 @@
         to_chunks = (place[:, None] == source[None, :]).astype(bf16)
 
     tokens_all = gather_rows(tokens[0], axes)
-    def fetch_out(layer, *wait):
-        return lax.all_gather(after(w_out[layer], *wait), every_axis, axis=0, tiled=True)
-
-    all_packed = [fetch_packed(0)]
-    all_out = [fetch_out(0)]
-    gate_moved = move_in(w_gate[0])
-    up_moved = move_in(w_up[0], gate_moved)
-    gate_parts = spread(gate_moved)
-    down_moved = move_in(w_down[0], up_moved, *gate_parts, tokens_all)
-    up_parts = spread(up_moved)
-    all_experts = []
-
+    all_packed = [fetch_packed(0, lambda x: x)]
     block_order = gathered_order(axes)
     deal_pairs = deal.reshape(ctx_size, 2)
     own_blocks = jnp.sum(
@@ -1004,7 +1111,14 @@
     own_places, own_starts = all_places[:rows, None], all_starts[:rows, None]
     place_line, start_line = all_places[None, :], all_starts[None, :]
 
-    first_things = [tokens_all, *gate_parts, up_moved, cosine, sine]
+    if by_chunks:
+        for layer in range(LAYERS):
+            for name, member in zip("gud", (w_gate, w_up, w_down)):
+                member = member[layer]
+                if (name, layer) == ("u", 0):
+                    member = after(member, cosine, sine)
+                add_weight(name + str(layer), member)
+    first_things = [*tokens_all, cosine, sine]
 
     route_rows = routes[0]
     flat_routes = jnp.concatenate([route_rows[:, k] for k in range(TOP)])
@@ -1014,7 +1128,7 @@
     )
     slot = jnp.sum(earlier.astype(jnp.int32), axis=1)
     in_slot = (flat_routes < EXPERTS) & (slot < CAP)
-    target = jnp.where(in_slot, (flat_routes ^ ex_at) * SLOTS + slot, -1)
+    target = jnp.where(in_slot, flat_routes * SLOTS + slot, -1)
     slot_ids = jnp.arange(EXPERTS * SLOTS, dtype=jnp.int32)
     pair_slots = (target[:, None] == slot_ids[None, :]).astype(bf16)
     slot_pairs = (slot_ids[:, None] == target[None, :]).astype(bf16)
@@ -1045,6 +1159,70 @@
     def reduce_rows(part):
         part = part.reshape(-1, part.shape[2])
         return lax.psum_scatter(part, ex_axes, scatter_dimension=0, tiled=True)
+
+    def add_grads(layer, halves):
+        for at, name in enumerate("gud"):
+            name += str(layer)
+            kept, given = halves[2 * at], halves[2 * at + 1]
+            plan.add(
+                "cj_" + name,
+                lambda tie, kept=kept, given=given: join_cores(kept, tie(given)),
+            )
+            plan.add(
+                "xj_" + name,
+                lambda tie, name=name: join_groups(
+                    (plan.get("cj_" + name)[0], tie(plan.get("cj_" + name)[1]))
+                ),
+            )
+            if name == "u0":
+                plan.add(
+                    "r_u0",
+                    lambda tie: deal_out(
+                        tie(jnp.concatenate([plan.get("xj_g0"), plan.get("xj_u0")], axis=2))
+                    ),
+                )
+            if name not in ("g0", "u0", "d0"):
+                plan.add(
+                    "r_" + name, lambda tie, name=name: deal_out(tie(plan.get("xj_" + name)))
+                )
+
+    def add_out(layer, attended, mid_low):
+        name = "o" + str(layer)
+
+        def product(tie):
+            att_rel = dot_nn(attended.astype(bf16), to_chunks).astype(bf16)
+            return join_cores(*weight_product(att_rel, tie(mid_low)))
+
+        plan.add("p_" + name, product)
+        plan.add(
+            "xj_" + name,
+            lambda tie: join_groups((plan.get("p_" + name)[0], tie(plan.get("p_" + name)[1]))),
+        )
+        if layer == 0:
+            plan.add(
+                "r_d0",
+                lambda tie: deal_out(
+                    tie(jnp.concatenate([plan.get("xj_d0"), plan.get("xj_o0")], axis=1))
+                ),
+            )
+
+    def add_qkv(thin_part, normed, proj_grad):
+        def product(tie):
+            thin_low = dot_tn(to_chunks, thin_part.astype(bf16)).astype(bf16)
+            normed_rel = dot_nn(normed, to_chunks).astype(bf16)
+            return join_cores(*weight_product(normed_rel, tie(proj_grad), thin_low))
+
+        plan.add("p_q1", product)
+        plan.add(
+            "xj_q1",
+            lambda tie: join_groups((plan.get("p_q1")[0], tie(plan.get("p_q1")[1]))),
+        )
+        plan.add(
+            "rs",
+            lambda tie: reduce_rows(
+                jnp.concatenate([plan.get("xj_o1"), tie(plan.get("xj_q1"))], axis=2)
+            ),
+        )
 
     def scatter_whole(member):
         cut = member.astype(bf16).reshape(EXPERTS, subs * 2, -1, member.shape[1])
@@ -1073,35 +1251,28 @@
     previous = jnp.pad(prev_logits[0], ((0, 0), (0, LANES - ROUTED)))
     grad = grad_out[0]
     all_packed[0] = after(all_packed[0], *first_things, slot_tokens, previous)
+    all_packed[0] = plan.point("packed0", all_packed[0])
+    plan.add("k_1", lambda tie: fetch_packed(1, tie))
     saved_all = []
     for layer in range(LAYERS):
         final = layer == LAYERS - 1
         packed = all_packed[layer]
         if layer == 0:
+            blocks = tokens_all
             normed_all = norm_rows(tokens_all, packed)
-            normed = normed_all[:rows]
         else:
-            up_moved = move_in(w_up[layer], normed)
-            normed_all = gather_rows(normed, axes)
-            normed_all = after(normed_all, *gate_parts, up_moved)
-            down_moved = move_in(w_down[layer], normed_all)
-            up_parts = spread(up_moved, normed_all)
-        normed_used = normed
-        all_queries, keys, values = project(
-            normed_all, packed, (0, 1, 2), (True, True, False), cosine, sine
-        )
-        queries = all_queries
+            normed = plan.point("norm1", normed)
+            blocks = gather_rows(normed, axes)
+            blocks[-1] = plan.point("ag1", blocks[-1])
+            normed_all = None if by_chunks else jnp.concatenate(blocks, axis=0)
+        projected = project(blocks, packed, cosine, sine, layer == 0)
+        projected = plan.point("proj" + str(layer), projected)
+        attended, totals = attend(projected, own_places, own_starts, place_line, prompt)
+        attended = plan.point("att" + str(layer), attended)
         if layer == 0:
-            all_packed.append(fetch_packed(1, keys))
-            all_out.append(fetch_out(1, keys))
-        attended, totals = attend(
-            queries, keys, values, own_places, own_starts, place_line, prompt
-        )
-        if final:
-            attended = after(attended, down_moved, *up_parts)
-        down_parts = spread(down_moved)
-        small = Block(packed, LANES, 3 * width // LANES)
-        wout = all_out[layer]
+            all_packed.append(plan.get("k_1"))
+        small = Block(packed, LANES, 4 * width // LANES)
+        wout = Block(packed, width, 3)
         midway, logits, chances, mixing, slot_in = run_fused(
             functools.partial(to_expert_kernel, final),
             [attended, hidden, wout, small, previous, slot_tokens, to_chunks]
@@ -1115,12 +1286,10 @@
             ],
             6 * rows * width * width,
         )
-        if layer == 0:
-            slot_in = after(slot_in, down_moved, *up_parts)
+        slot_in = plan.point("msg" + str(layer), slot_in)
         expert_in = dispatch(slot_in)
-        weights = [share(parts, slot_in) for parts in (gate_parts, up_parts, down_parts)]
-        if not final:
-            next_gate = move_in(w_gate[layer + 1], expert_in)
+        expert_in = plan.point("ein" + str(layer), expert_in)
+        weights = weights_of(layer)
         gate_act = upward = halves = None
         if by_chunks and final:
             halves, expert_out = run_expert_back(
@@ -1135,38 +1304,29 @@
             expert_out = jnp.concatenate([in_grad, expert_out], axis=1)
         else:
             gate_act, upward, expert_out = expert_plain(expert_in, weights)
-        if not final:
-            expert_out = after(expert_out, next_gate)
-            gate_parts = spread(next_gate, expert_out)
+        if by_chunks and final:
+            add_grads(1, halves)
+        expert_out = plan.point("eout" + str(layer), expert_out)
         back = dispatch(expert_out)
         in_back = None
         if final:
             in_back, back = back[:, :width], back[:, width:]
-        if final:
-            (output_rows,) = run_fused(
-                functools.partial(from_expert_kernel, True),
-                [midway, chances, mixing, picks[0], picks[1], small, pair_slots, back],
-                [(full, bf16)],
-                2 * rows * width * EXPERTS * SLOTS,
-            )
-        else:
-            all_packed[layer + 1] = after(all_packed[layer + 1], expert_out)
+        if not final:
+            all_packed[1] = after(all_packed[1], expert_out)
             output, normed = run_fused(
                 functools.partial(from_expert_kernel, False),
                 [midway, chances, mixing, picks[0], picks[1], small, pair_slots, back]
-                + [Block(all_packed[layer + 1], LANES, 3 * width // LANES)],
+                + [Block(all_packed[layer + 1], LANES, 4 * width // LANES)],
                 [(full, f32), (full, bf16)],
                 2 * rows * width * EXPERTS * SLOTS,
             )
+        normed_own = None if layer == 0 else blocks[0][:rows]
         saved_all.append(
             (
                 hidden,
-                normed_used,
+                normed_own,
                 normed_all,
-                all_queries,
-                queries,
-                keys,
-                values,
+                projected,
                 attended,
                 totals,
                 midway,
@@ -1195,10 +1355,7 @@
             hidden,
             normed,
             normed_all,
-            all_queries,
-            queries,
-            keys,
-            values,
+            projected,
             attended,
             totals,
             midway,
@@ -1213,35 +1370,26 @@
             back,
         ) = saved_all[layer]
         packed = all_packed[layer]
-        small = Block(packed, LANES, 3 * width // LANES)
-        wout = all_out[layer]
+        small = Block(packed, LANES, 4 * width // LANES)
+        wout = Block(packed, width, 3)
         if not final:
+            slot_grad = plan.point("slot0", slot_grad)
+            out_grad = dispatch(slot_grad)
+            out_grad = plan.point("og0", out_grad)
             if by_chunks:
-                slot_grad = after(slot_grad, moved_grads[1][1])
-            out_grad = dispatch(slot_grad)
-            if by_chunks:
-                out_grad = after(out_grad, *qkv_joined)
-                moved_grads[1][2] = deal_out(after(folded[1][2], out_grad))
                 halves, in_grad = run_expert_back(
                     flags, (expert_in, out_grad), to_chunks, gate_act, upward, *weights
                 )
-                in_grad = after(in_grad, moved_grads[1][2])
             else:
                 halves, in_grad = expert_plain_back(
                     expert_in, out_grad, gate_act, upward, weights
                 )
+            if by_chunks:
+                add_grads(0, halves)
+            in_grad = plan.point("ig0", in_grad)
             in_back = dispatch(in_grad)
-            if by_chunks:
-                in_back = after(in_back, qkv_folded, out_folded[1])
-                owned = reduce_rows(
-                    jnp.concatenate([out_folded[1], after(qkv_folded, in_back)], axis=2)
-                )
-        if final:
-            folded = [None] * LAYERS
-        if by_chunks:
-            joined = [join_cores(halves[2 * at], halves[2 * at + 1]) for at in range(3)]
-            in_back = after(in_back, *joined[0])
-            folded[layer] = [join_groups(joined[at]) for at in range(3)]
+            in_back = plan.point("ib0", in_back)
+
         mid_grad, mid_low, sent, delta, logit_next, thin_w, line_grads = run_fused(
             to_attention_kernel,
             [grad, midway, chances, mixing, picks[0], picks[1], small, pair_slots]
@@ -1261,10 +1409,8 @@
             return query_back(
                 start,
                 2,
-                after(queries, dependence),
+                after(projected, dependence),
                 sent,
-                keys,
-                values,
                 totals,
                 delta,
                 own_places,
@@ -1275,23 +1421,25 @@
                 prompt,
             )
 
+        sent = plan.point("sent" + str(layer), sent)
+        if final:
+            (output_rows,) = run_fused(
+                functools.partial(from_expert_kernel, True),
+                [midway, chances, mixing, picks[0], picks[1], small, pair_slots]
+                + [after(back, sent)],
+                [(full, bf16)],
+                2 * rows * width * EXPERTS * SLOTS,
+            )
         sent_all, query_grads = gather_rows(
             sent, axes, [functools.partial(some_queries, start) for start in range(0, PAIRS, 2)]
         )
-        late_low = after(mid_low, sent)
         if by_chunks:
-            att_rel = dot_nn(attended.astype(bf16), to_chunks).astype(bf16)
-            out_joined = join_cores(*weight_product(att_rel, late_low))
+            add_out(layer, attended, mid_low)
         else:
-            out_w_grad = dot_tn(attended.astype(bf16), late_low).astype(bf16)
-        query_grad = jnp.concatenate(query_grads, axis=1)
-        if by_chunks:
-            sent_all = after(sent_all, folded[layer][0], query_grad)
-            moved_grads[layer][0] = deal_out(after(folded[layer][0], sent_all))
+            out_w_grad = dot_tn(attended.astype(bf16), mid_low).astype(bf16)
+        sent_all[-1] = plan.point("sall" + str(layer), sent_all[-1])
         key_grad, value_grad = key_back(
-            keys,
-            values,
-            all_queries,
+            projected,
             sent_all,
             own_places,
             place_line,
@@ -1300,16 +1448,14 @@
             own_sin,
             prompt,
         )
-        if by_chunks and final:
-            key_grad = after(key_grad, moved_grads[layer][0], folded[layer][1])
-            moved_grads[layer][1] = deal_out(after(folded[layer][1], key_grad))
-        proj_grad = jnp.concatenate([query_grad, key_grad, value_grad], axis=1)
+        key_grad = plan.point("key" + str(layer), key_grad)
+        proj_grad = jnp.concatenate([*query_grads, key_grad, value_grad], axis=1)
         before = []
         if layer > 0:
-            before = [saved_all[layer - 1][10], picks[0], picks[1], slot_pairs]
+            before = [saved_all[layer - 1][7], picks[0], picks[1], slot_pairs]
         grad, gain_grads, *slot_grad = run_fused(
             functools.partial(from_attention_kernel, layer == 0),
-            [query_grad, key_grad, value_grad]
+            [*query_grads, key_grad, value_grad]
             + [Block(packed, width, at) for at in range(3)]
             + [hidden, small, mid_grad]
             + before,
@@ -1322,32 +1468,28 @@
         wanted = jnp.array([AT_ATTN, AT_MOE, AT_CVEC, AT_CVEC + 1], dtype=jnp.int32)
         spread_out = (wanted[:, None] == lane[None, :]).astype(f32)
         thin_part = thin_w + jnp.dot(some.T, spread_out, precision=highest)
-        if by_chunks:
-            out_folded[layer] = join_groups(out_joined)
         if by_chunks and final:
-            thin_low = dot_tn(to_chunks, thin_part.astype(bf16)).astype(bf16)
-            normed_rel = dot_nn(normed, to_chunks).astype(bf16)
-            qkv_joined = join_cores(*weight_product(normed_rel, after(proj_grad, grad), thin_low))
-            qkv_folded = join_groups(qkv_joined)
+            add_qkv(thin_part, normed, proj_grad)
             continue
         share_of = 3 * width // ctx_size
         columns = proj_grad.reshape(rows, ctx_size, share_of).transpose(1, 0, 2)
-        if by_chunks:
-            columns = after(columns, moved_grads[0][0])
+        columns = plan.point("cols0", columns)
         columns = lax.all_to_all(columns, axes, 0, 0, tiled=True)
-        if by_chunks:
-            moved_grads[0][1] = deal_out(after(folded[0][1], columns))
+        columns = plan.point("cols", columns)
         columns = jnp.take(columns, block_order, axis=0).reshape(length, share_of)
         part = jnp.concatenate([dot_tn(columns, normed_all).T, thin_part], axis=1).astype(bf16)
         part = fold(part.reshape(ctx_size, 2, own_rows, share_of + LANES), FS, fs_at)
+        part = plan.point("part0", part)
+        part = lax.all_to_all(part, axes, 0, 0, tiled=True)
+        part = plan.point("part", part)
         if by_chunks:
-            part = after(part, moved_grads[0][1])
-        part = lax.all_to_all(part, axes, 0, 0, tiled=True)
-        if by_chunks:
-            last = jnp.concatenate([folded[0][2], out_folded[0]], axis=1)
-            last = deal_out(after(last, part))
-            tall = folded[0][2].shape[1]
-            moved_grads[0][2], last_out = last[:, :tall], last[:, tall:]
+            last = plan.get("r_d0")
+            tall = plan.get("xj_d0").shape[1]
+            both = plan.get("r_u0")
+            wide = both.shape[2] // 2
+            moved_grads[0] = [both[:, :, :wide], both[:, :, wide:], last[:, :tall]]
+            moved_grads[1] = [plan.get("r_" + name + "1") for name in "gud"]
+            last_out = last[:, tall:]
         part = part.astype(f32)
         qkv_owned = part[:, :, :share_of].transpose(1, 0, 2).reshape(own_rows, 3 * width)
         thin_owned = jnp.sum(part[:, :, share_of:], axis=0)
@@ -1360,7 +1502,7 @@
             ).astype(f32)
         results[layer] = (qkv_owned, out_owned, thin_owned)
     if by_chunks:
-        owned = owned.astype(f32)
+        owned = after(plan.get("rs"), last).astype(f32)
         results[1] = (owned[:, width : 4 * width], owned[:, :width], owned[:, 4 * width :])
 
     def stack(parts):

time: 831 us -> 769 us (0.925)
  starting transfers between devices: 206 us -> 154 us
  local copies, waits for them, and re-layouts: 114 us -> 82.5 us
  waiting for transfers between devices: 215 us -> 233 us
  Pallas kernels: 188 us -> 199 us
    all_to_all x12 -> x17, waiting for transfers between devices: 36.4 us -> 128 us  [deal_out(): return lax.all_to_all(x, ex_axes, 0, 0, tiled=True)]
    ppermute x42 -> x0, starting transfers between devices: 70.8 us -> none  [dispatch(): blocks.append(lax.ppermute(block, ex_axes, pairs))]
    ppermute x69, waiting for transfers between devices: 80.9 us -> 34.8 us  [swap(): return lax.ppermute(x, axis, [(0, 1), (1, 0)])]
    ppermute x42 -> x0, waiting for transfers between devices: 42.6 us -> none  [dispatch(): blocks.append(lax.ppermute(block, ex_axes, pairs))]
    optimization_barrier x0 -> x1, waiting for transfers between devices: none -> 27.1 us  [after(): return lax.optimization_barrier((x,) + things)[0]]
    all_to_all x12 -> x17, starting transfers between devices: 59.7 us -> 84.1 us  [deal_out(): return lax.all_to_all(x, ex_axes, 0, 0, tiled=True)]
    unnamed x273 -> x204, local copies, waits for them, and re-layouts: 50.9 us -> 29.4 us
    all_gather x4 -> x2, waiting for transfers between devices: 20.6 us -> 0.01 us  [fetch_packed(): return lax.all_gather(tie(mine), every_axis, axis=0, tiled=True)]
  transfers between devices with their start and end apart: 142 -> 103, of which waited for: 50 -> 36; matrix products, arithmetic and copies ran while one was open for 20% -> 16% of each run, Pallas kernels for 20% -> 23%
where the time goes in v3:
time: 769 us; the launch traced here: 756 us
  waiting for transfers between devices  233 us (30%)
  Pallas kernels  199 us (26%)
  starting transfers between devices  154 us (20%)
  local copies, waits for them, and re-layouts  82.5 us (11%)
  other arithmetic  62.5 us (8%)
  between operations  15.9 us (2%)
  matrix products  10.4 us (1%)
    all_to_all x17, waiting for transfers between devices, deal_out(): return lax.all_to_all(x, ex_axes, 0, 0, tiled=True)  128 us
    all_to_all x17, starting transfers between devices, deal_out(): return lax.all_to_all(x, ex_axes, 0, 0, tiled=True)  84.1 us
    ppermute x69, starting transfers between devices, swap(): return lax.ppermute(x, axis, [(0, 1), (1, 0)])  45.1 us
    pallas_call x2, Pallas kernels, run_expert_back(): pl.pallas_call(functools.partial(expert_back_kernel, both), grid=(EXPERTS...  34.9 us
    ppermute x69, waiting for transfers between devices, swap(): return lax.ppermute(x, axis, [(0, 1), (1, 0)])  34.8 us
    pallas_call x2, Pallas kernels, project(): pl.pallas_call(functools.partial(project_kernel, 2 * SPLIT, len(blocks),...  34.2 us
    pallas_call x8, Pallas kernels, run_fused(): pl.pallas_call(kernel, grid=(1,), in_specs=specs, out_specs=[pl.BlockSpec...  33.6 us
    ppermute x12, waiting for transfers between devices, gather_rows(): found.append(lax.ppermute(x, far, pairs))  31.4 us
  transfers between devices with their start and end apart: 103, of which 36 were waited for; matrix products, arithmetic and copies ran while one was open for 16% of the time, Pallas kernels for 23%

profile of v3, /device:TPU:0, one launch (start us, length us, event | category | flops | bytes accessed | tf_op | source)
XLA Modules:
  0.0 756.4 jit_solution(12278182953024089957)
XLA Ops:
  35.6 5.6 fusion.13
  42.5 25.3 %all-to-all-done.1 = bf16[8,24,2048]{2,1,0:T(8,128)(2,1)S(1)} async-done(((bf16[8,24,2048]{2,1,0:T(8,128)(2,1)}), bf16[8,24,2048]{2,1,0:T(8,128)(2,1)S(1)}, u32[]{:S(2)}, u32[]{:S(2)}) %all-to-all-start.1) | async-done | bytes 786464 | tf_op jit(solution)/shard_map/all_to_all | solution.py:1019
  85.6 5.6 collective-permute-done.3
  91.8 8.9 %all-to-all-done = bf16[8,24,2048]{2,1,0:T(8,128)(2,1)S(1)} async-done(((bf16[8,24,2048]{2,1,0:T(8,128)(2,1)}), bf16[8,24,2048]{2,1,0:T(8,128)(2,1)S(1)}, u32[]{:S(2)}, u32[]{:S(2)}) %all-to-all-start) | async-done | bytes 786464 | tf_op jit(solution)/shard_map/all_to_all | solution.py:1019
  100.7 5.3 all-to-all-start.2
  117.2 17.7 %shard_map.265.q_ref.k_ref.v_ref = bf16[2048,2304]{1,0:T(8,128)(2,1)} custom-call(bf16[256,768]{1,0:T(8,128)(2,1)} %copy-done.32, bf16[256,768]{1,0:T(8,128)(2,1)} %collective-permute-done.1.refs_1_, bf16[256,768]{1,0:T(8,128)(2,1)} %constant_dynamic-update-slice_fusion.refs_2_, bf16[256,768]{1,0:T(8,128)(2,1)} %collective-permute-done.4.refs_3_, ...), custom_call_target="tpu_custom_call" | custom-call | flops 7247757312 | bytes 16121856 | tf_op jit(solution)/shard_map/pallas_call | solution.py:119
  135.0 6.1 all-to-all-start.3
  146.5 10.2 %shard_map.266 = (f32[128,768]{1,0:T(8,128)}, f32[128,128]{1,0:T(8,128)}) custom-call(bf16[2048,2304]{1,0:T(8,128)(2,1)} %shard_map.265.q_ref.k_ref.v_ref, bf16[2048,2304]{1,0:T(8,128)(2,1)} %shard_map.265.q_ref.k_ref.v_ref, bf16[2048,2304]{1,0:T(8,128)(2,1)} %shard_map.265.q_ref.k_ref.v_ref, s32[128,1]{1,0:T(8,128)} %broadcast_in_dim.105.at_ref.refs_16_, ...), custom_call_target="tpu_custom_call" | custom-call | flops 1610612736 | bytes 6291456 | tf_op jit(solution)/shard_map/pallas_call | solution.py:188
  168.3 16.0 %all-to-all-done.4 = bf16[8,32,768]{2,1,0:T(8,128)(2,1)S(1)} async-done(((bf16[8,32,768]{2,1,0:T(8,128)(2,1)}), bf16[8,32,768]{2,1,0:T(8,128)(2,1)S(1)}, u32[]{:S(2)}, u32[]{:S(2)}) %all-to-all-start.4) | async-done | bytes 393248 | tf_op jit(solution)/shard_map/all_to_all | solution.py:1019
  197.5 11.2 %shard_map.268 = (f32[256,2048]{1,0:T(8,128)}, f32[256,2048]{1,0:T(8,128)}, bf16[256,768]{1,0:T(8,128)(2,1)}) custom-call(s32[1,2]{1,0:T(1,128)} %add_bitcast_fusion.flag_ref, bf16[256,768]{1,0:T(8,128)(2,1)} %bitcast.186, bf16[192,2048]{1,0:T(8,128)(2,1)} %bitcast.167, bf16[192,2048]{1,0:T(8,128)(2,1)} %collective-permute-done.11.refs_1_.refs_3_, ...), custom_call_target="tpu_custom_call" | custom-call | flops 2415919104 | bytes 13631488 | tf_op jit(solution)/shard_map/pallas_call | solution.py:422
  208.7 10.8 %all-to-all-done.5 = bf16[8,24,2048]{2,1,0:T(8,128)(2,1)} async-done(((bf16[8,24,2048]{2,1,0:T(8,128)(2,1)}), bf16[8,24,2048]{2,1,0:T(8,128)(2,1)}, u32[]{:S(2)}, u32[]{:S(2)}) %all-to-all-start.5) | async-done | bytes 786464 | tf_op jit(solution)/shard_map/all_to_all | solution.py:1019
  223.9 11.0 %all-to-all-done.6 = bf16[8,32,768]{2,1,0:T(8,128)(2,1)S(1)} async-done(((bf16[8,32,768]{2,1,0:T(8,128)(2,1)}), bf16[8,32,768]{2,1,0:T(8,128)(2,1)S(1)}, u32[]{:S(2)}, u32[]{:S(2)}) %all-to-all-start.6) | async-done | bytes 393248 | tf_op jit(solution)/shard_map/all_to_all | solution.py:1019
  257.9 4.5 collective-permute-done.25
  272.9 16.5 %shard_map.270.q_ref.k_ref.v_ref = bf16[2048,2304]{1,0:T(8,128)(2,1)} custom-call(bf16[256,768]{1,0:T(8,128)(2,1)} %copy-done.66, bf16[256,768]{1,0:T(8,128)(2,1)} %collective-permute-done.21.refs_1_, bf16[256,768]{1,0:T(8,128)(2,1)} %copy-done.64, bf16[256,768]{1,0:T(8,128)(2,1)} %copy-done.86, bf16[256,768]{1,0:T(8,128)(2,1)} %copy-done.63, ...), custom_call_target="tpu_custom_call" | custom-call | flops 7247757312 | bytes 16121856 | tf_op jit(solution)/shard_map/pallas_call | solution.py:119
  289.4 10.1 %shard_map.271 = (f32[128,768]{1,0:T(8,128)}, f32[128,128]{1,0:T(8,128)}) custom-call(bf16[2048,2304]{1,0:T(8,128)(2,1)} %shard_map.270.q_ref.k_ref.v_ref, bf16[2048,2304]{1,0:T(8,128)(2,1)} %shard_map.270.q_ref.k_ref.v_ref, bf16[2048,2304]{1,0:T(8,128)(2,1)} %shard_map.270.q_ref.k_ref.v_ref, s32[128,1]{1,0:T(8,128)} %broadcast_in_dim.105.at_ref.refs_16_, ...), custom_call_target="tpu_custom_call" | custom-call | flops 1610612736 | bytes 6291456 | tf_op jit(solution)/shard_map/pallas_call | solution.py:188
  304.8 6.1 all-to-all-start.8
  312.0 7.2 collective-permute-done.37.refs_9_
  320.2 10.9 %all-to-all-done.8 = bf16[8,32,1536]{2,1,0:T(8,128)(2,1)S(1)} async-done(((bf16[8,32,1536]{2,1,0:T(8,128)(2,1)}), bf16[8,32,1536]{2,1,0:T(8,128)(2,1)S(1)}, u32[]{:S(2)}, u32[]{:S(2)}) %all-to-all-start.8) | async-done | bytes 786464 | tf_op jit(solution)/shard_map/all_to_all | solution.py:1019
  332.0 18.7 %shard_map.273 = (bf16[384,2048]{1,0:T(8,128)(2,1)}, bf16[384,2048]{1,0:T(8,128)(2,1)}, bf16[384,2048]{1,0:T(8,128)(2,1)}, bf16[384,2048]{1,0:T(8,128)(2,1)}, bf...) custom-call(s32[1,2]{1,0:T(1,128)} %add_bitcast_fusion.flag_ref, ...), custom_call_target="tpu_custom_call" | custom-call | flops 7247757312 | bytes 23068672 | tf_op jit(solution)/shard_map/pallas_call | solution.py:519
  356.2 4.8 shard_map.289
  360.9 4.7 copy.251
  368.7 6.3 all-to-all-done.9
  376.5 5.0 shard_map.274
  400.3 4.6 shard_map.276.refs_0_
  405.3 4.6 shard_map.277.refs_1_
  409.9 4.6 shard_map.278.refs_2_
  416.3 5.9 collective-permute-done.49
  425.4 7.7 %all-to-all-start.10 = ((bf16[8,24,2048]{2,1,0:T(8,128)(2,1)}), bf16[8,24,2048]{2,1,0:T(8,128)(2,1)S(1)}, u32[]{:S(2)}, u32[]{:S(2)}) async-start(bf16[8,24,2048]{2,1,0:T(8,128)(2,1)} %bitcast.61), calls=%async_computation.10 | async-start | bytes 1572864 | tf_op jit(solution)/shard_map/all_to_all | solution.py:1019
  442.0 11.4 %shard_map.279 = (bf16[128,768]{1,0:T(8,128)(2,1)}, bf16[128,768]{1,0:T(8,128)(2,1)}) custom-call(bf16[2048,2304]{1,0:T(8,128)(2,1)} %shard_map.270.q_ref.k_ref.v_ref, bf16[2048,2304]{1,0:T(8,128)(2,1)} %shard_map.270.q_ref.k_ref.v_ref, bf16[2048,2304]{1,0:T(8,128)(2,1)} %shard_map.270.q_ref.k_ref.v_ref, ...), custom_call_target="tpu_custom_call" | custom-call | flops 3221225472 | bytes 6291456 | tf_op jit(solution)/shard_map/pallas_call | solution.py:346
  453.7 5.4 shard_map.280
  459.1 5.9 all-to-all-start.11
  477.1 5.0 all-to-all-start.12
  485.5 16.3 %shard_map.281 = (bf16[384,2048]{1,0:T(8,128)(2,1)}, bf16[384,2048]{1,0:T(8,128)(2,1)}, bf16[384,2048]{1,0:T(8,128)(2,1)}, bf16[384,2048]{1,0:T(8,128)(2,1)}, bf...) custom-call(s32[1,2]{1,0:T(1,128)} %add_bitcast_fusion.flag_ref, ...), custom_call_target="tpu_custom_call" | custom-call | flops 4831838208 | bytes 23068672 | tf_op jit(solution)/shard_map/pallas_call | solution.py:519
  507.5 6.3 all-to-all-start.13
  525.9 5.1 shard_map.282
  540.0 13.6 %collective-permute-done.57 = bf16[128,896]{1,0:T(8,128)(2,1)S(1)} collective-permute-done((bf16[128,896]{1,0:T(8,128)(2,1)S(1)}, bf16[128,896]{1,0:T(8,128)(2,1)S(1)}, u32[]{:S(2)}, u32[]{:S(2)}) %collective-permute-start.57) | collective-permute-done | bytes 229408 | tf_op jit(solution)/shard_map/ppermute | solution.py:960
  553.6 4.6 shard_map.285.refs_2_
  558.9 4.6 shard_map.283.refs_0_
  565.0 4.6 shard_map.284.refs_1_
  577.6 7.5 all-to-all-start.14
  590.0 11.4 %shard_map.286 = (bf16[128,768]{1,0:T(8,128)(2,1)}, bf16[128,768]{1,0:T(8,128)(2,1)}) custom-call(bf16[2048,2304]{1,0:T(8,128)(2,1)} %shard_map.265.q_ref.k_ref.v_ref, bf16[2048,2304]{1,0:T(8,128)(2,1)} %shard_map.265.q_ref.k_ref.v_ref, bf16[2048,2304]{1,0:T(8,128)(2,1)} %shard_map.265.q_ref.k_ref.v_ref, ...), custom_call_target="tpu_custom_call" | custom-call | flops 3221225472 | bytes 6291456 | tf_op jit(solution)/shard_map/pallas_call | solution.py:346
  605.5 5.3 all-to-all-start.15
  614.9 11.5 %all-to-all-done.15 = bf16[16,128,144]{1,2,0:T(8,128)(2,1)} async-done(((bf16[16,128,144]{1,2,0:T(8,128)(2,1)}), bf16[16,128,144]{1,2,0:T(8,128)(2,1)}, u32[]{:S(2)}, u32[]{:S(2)}) %all-to-all-start.15) | async-done | bytes 589856 | tf_op jit(solution)/shard_map/all_to_all | solution.py:1477
  639.8 4.7 shard_map.288
  660.0 5.7 collective-permute-done.70
  666.6 10.8 %all-to-all-done.16 = bf16[8,24,4096]{2,1,0:T(8,128)(2,1)S(1)} async-done(((bf16[8,24,4096]{2,1,0:T(8,128)(2,1)}), bf16[8,24,4096]{2,1,0:T(8,128)(2,1)S(1)}, u32[]{:S(2)}, u32[]{:S(2)}) %all-to-all-start.16) | async-done | bytes 1572896 | tf_op jit(solution)/shard_map/all_to_all | solution.py:1019
  685.3 27.1 %reduce-scatter.4.cloned.1.call-done = bf16[24,3200]{1,0:T(8,128)(2,1)} async-done(((bf16[192,3200]{1,0:T(8,128)(2,1)}), bf16[24,3200]{1,0:T(8,128)(2,1)}) %reduce-scatter.4.cloned.1.call-update) | async-done | bytes 153616 | tf_op jit(solution)/shard_map/optimization_barrier | solution.py:866
  724.6 16.7 %all-to-all-done.18 = bf16[8,88,768]{2,1,0:T(8,128)(2,1)S(1)} async-done(((bf16[8,88,768]{2,1,0:T(8,128)(2,1)}), bf16[8,88,768]{2,1,0:T(8,128)(2,1)S(1)}, u32[]{:S(2)}, u32[]{:S(2)}) %all-to-all-start.18) | async-done | bytes 1081376 | tf_op jit(solution)/shard_map/all_to_all | solution.py:1019
  (561 shorter events, 301.1 us)
Async XLA Ops:
  7.2 103.0 %all-gather.3.cloned.1.call-start = ((), (), s32[]{:S(2)}) async-start(), calls=%async_computation.20 | async-start | bytes 5068800 | tf_op jit(solution)/shard_map/all_gather | solution.py:1044
  17.2 57.3 %collective-permute-start = (bf16[128,768]{1,0:T(8,128)(2,1)}, bf16[128,768]{1,0:T(8,128)(2,1)}, u32[]{:S(2)}, u32[]{:S(2)}) collective-permute-start(bf16[128,768]{1,0:T(8,128)(2,1)} %bitcast.196), channel_id=1, source_target_pairs={{0,4},{4,0},{1,5},{5,1},{2,6},{6,2},{3,7},{7,3},{8,12},{12,8},{9,1... | collective-permute-start | bytes 589832 | tf_op jit(solution)/shard_map/ppermute | solution.py:945
  20.3 55.4 %collective-permute-start.2 = (bf16[128,768]{1,0:T(8,128)(2,1)}, bf16[128,768]{1,0:T(8,128)(2,1)}, u32[]{:S(2)}, u32[]{:S(2)}) collective-permute-start(bf16[128,768]{1,0:T(8,128)(2,1)} %bitcast.197), channel_id=1, source_target_pairs={{0,8},{8,16},{16,24},{24,0},{1,9},{9,17},{17,25},{25,1},{2,10},{10... | collective-permute-start | bytes 589832 | tf_op jit(solution)/shard_map/ppermute | solution.py:960
  21.8 55.8 %collective-permute-start.5 = (bf16[128,768]{1,0:T(8,128)(2,1)}, bf16[128,768]{1,0:T(8,128)(2,1)}, u32[]{:S(2)}, u32[]{:S(2)}) collective-permute-start(bf16[128,768]{1,0:T(8,128)(2,1)} %bitcast.198), channel_id=1, source_target_pairs={{0,16},{8,24},{16,0},{24,8},{1,17},{9,25},{17,1},{25,9},{2,18},{10... | collective-permute-start | bytes 589832 | tf_op jit(solution)/shard_map/ppermute | solution.py:960
  24.4 53.3 %collective-permute-start.8 = (bf16[128,768]{1,0:T(8,128)(2,1)}, bf16[128,768]{1,0:T(8,128)(2,1)}, u32[]{:S(2)}, u32[]{:S(2)}) collective-permute-start(bf16[128,768]{1,0:T(8,128)(2,1)} %bitcast.199), channel_id=1, source_target_pairs={{0,24},{8,0},{16,8},{24,16},{1,25},{9,1},{17,9},{25,17},{2,26},{10... | collective-permute-start | bytes 589832 | tf_op jit(solution)/shard_map/ppermute | solution.py:960
  28.5 39.3 %all-to-all-start.1 = ((bf16[8,24,2048]{2,1,0:T(8,128)(2,1)}), bf16[8,24,2048]{2,1,0:T(8,128)(2,1)S(1)}, u32[]{:S(2)}, u32[]{:S(2)}) async-start(bf16[8,24,2048]{2,1,0:T(8,128)(2,1)} %get-tuple-element.317), calls=%async_computation.1 | async-start | bytes 1572864 | tf_op jit(solution)/shard_map/all_to_all | solution.py:1019
  67.8 32.9 %all-to-all-start = ((bf16[8,24,2048]{2,1,0:T(8,128)(2,1)}), bf16[8,24,2048]{2,1,0:T(8,128)(2,1)S(1)}, u32[]{:S(2)}, u32[]{:S(2)}) async-start(bf16[8,24,2048]{2,1,0:T(8,128)(2,1)} %get-tuple-element.123), calls=%async_computation | async-start | bytes 1572864 | tf_op jit(solution)/shard_map/all_to_all | solution.py:1019
  75.5 34.2 %collective-permute-start.1 = (bf16[256,768]{1,0:T(8,128)(2,1)S(1)}, bf16[256,768]{1,0:T(8,128)(2,1)}, u32[]{:S(2)}, u32[]{:S(2)}) collective-permute-start(bf16[256,768]{1,0:T(8,128)(2,1)S(1)} %pad_maximum_fusion.4.refs_0_), channel_id=1, source_target_pairs={{0,2},{2,0},{1,3},{3,1},{4,6},{6,4},{5,7},{7,5},{8,10},{10,8},{9,1... | collective-permute-start | bytes 1179656 | tf_op jit(solution)/shard_map/ppermute | solution.py:945
  77.6 28.5 %collective-permute-start.6 = (bf16[128,768]{1,0:T(8,128)(2,1)}, bf16[128,768]{1,0:T(8,128)(2,1)}, u32[]{:S(2)}, u32[]{:S(2)}) collective-permute-start(bf16[128,768]{1,0:T(8,128)(2,1)} %collective-permute-done.5), channel_id=1, source_target_pairs={{0,4},{4,0},{1,5},{5,1},{2,6},{6,2},{3,7},{7,3},{8,12},{12,8},{9,1... | collective-permute-start | bytes 589832 | tf_op jit(solution)/shard_map/ppermute | solution.py:945
  77.7 30.0 %collective-permute-start.9 = (bf16[128,768]{1,0:T(8,128)(2,1)}, bf16[128,768]{1,0:T(8,128)(2,1)S(1)}, u32[]{:S(2)}, u32[]{:S(2)}) collective-permute-start(bf16[128,768]{1,0:T(8,128)(2,1)} %collective-permute-done.8), channel_id=1, source_target_pairs={{0,4},{4,0},{1,5},{5,1},{2,6},{6,2},{3,7},{7,3},{8,12},{12,8},{9,1... | collective-permute-start | bytes 589832 | tf_op jit(solution)/shard_map/ppermute | solution.py:945
  83.8 26.3 %collective-permute-start.11 = (bf16[192,2048]{1,0:T(8,128)(2,1)S(1)}, bf16[192,2048]{1,0:T(8,128)(2,1)}, u32[]{:S(2)}, u32[]{:S(2)}) collective-permute-start(bf16[192,2048]{1,0:T(8,128)(2,1)S(1)} %bitcast.165), channel_id=1, source_target_pairs={{0,1},{1,0},{2,3},{3,2},{4,5},{5,4},{6,7},{7,6},{8,9},{9,8},{10,11... | collective-permute-start | bytes 2359304 | tf_op jit(solution)/shard_map/ppermute | solution.py:945
  100.7 34.2 %all-to-all-start.2 = ((bf16[8,64,768]{2,1,0:T(8,128)(2,1)}), bf16[8,64,768]{2,1,0:T(8,128)(2,1)S(1)}, u32[]{:S(2)}, u32[]{:S(2)}) async-start(bf16[8,64,768]{2,1,0:T(8,128)(2,1)} %get-tuple-element.313), calls=%async_computation.2 | async-start | bytes 1572864 | tf_op jit(solution)/shard_map/all_to_all | solution.py:1019
  106.0 117.8 %all-gather.5.cloned.1.call-start = ((), (), s32[]{:S(2)}) async-start(), calls=%async_computation.21 | async-start | bytes 5068800 | tf_op jit(solution)/shard_map/all_gather | solution.py:1044
  110.1 24.8 %collective-permute-start.12 = (bf16[192,2048]{1,0:T(8,128)(2,1)S(1)}, bf16[192,2048]{1,0:T(8,128)(2,1)}, u32[]{:S(2)}, u32[]{:S(2)}) collective-permute-start(bf16[192,2048]{1,0:T(8,128)(2,1)S(1)} %bitcast.169), channel_id=1, source_target_pairs={{0,1},{1,0},{2,3},{3,2},{4,5},{5,4},{6,7},{7,6},{8,9},{9,8},{10,11... | collective-permute-start | bytes 2359304 | tf_op jit(solution)/shard_map/ppermute | solution.py:945
  135.0 29.7 %all-to-all-start.3 = ((bf16[8,24,2048]{2,1,0:T(8,128)(2,1)}), bf16[8,24,2048]{2,1,0:T(8,128)(2,1)}, u32[]{:S(2)}, u32[]{:S(2)}) async-start(bf16[8,24,2048]{2,1,0:T(8,128)(2,1)} %get-tuple-element.132), calls=%async_computation.3 | async-start | bytes 1572864 | tf_op jit(solution)/shard_map/all_to_all | solution.py:1019
  146.2 22.1 %collective-permute-start.13 = (bf16[512,768]{1,0:T(8,128)(2,1)S(1)}, bf16[512,768]{1,0:T(8,128)(2,1)S(1)}, u32[]{:S(2)}, u32[]{:S(2)}) collective-permute-start(bf16[512,768]{1,0:T(8,128)(2,1)S(1)} %bitcast.173), channel_id=1, source_target_pairs={{0,1},{1,0},{2,3},{3,2},{4,5},{5,4},{6,7},{7,6},{8,9},{9,8},{10,11... | collective-permute-start | bytes 2359304 | tf_op jit(solution)/shard_map/ppermute | solution.py:945
  184.3 35.2 %all-to-all-start.5 = ((bf16[8,24,2048]{2,1,0:T(8,128)(2,1)}), bf16[8,24,2048]{2,1,0:T(8,128)(2,1)}, u32[]{:S(2)}, u32[]{:S(2)}) async-start(bf16[8,24,2048]{2,1,0:T(8,128)(2,1)} %get-tuple-element.138), calls=%async_computation.5 | async-start | bytes 1572864 | tf_op jit(solution)/shard_map/all_to_all | solution.py:1019
  239.5 24.6 %collective-permute-start.31 = (bf16[192,2048]{1,0:T(8,128)(2,1)}, bf16[192,2048]{1,0:T(8,128)(2,1)S(1)}, u32[]{:S(2)}, u32[]{:S(2)}) collective-permute-start(bf16[192,2048]{1,0:T(8,128)(2,1)} %bitcast.39.refs_0_), channel_id=1, source_target_pairs={{0,1},{1,0},{2,3},{3,2},{4,5},{5,4},{6,7},{7,6},{8,9},{9,8},{10,11... | collective-permute-start | bytes 2359304 | tf_op jit(solution)/shard_map/ppermute | solution.py:945
  265.8 33.7 %all-to-all-start.7 = ((bf16[8,64,768]{2,1,0:T(8,128)(2,1)}), bf16[8,64,768]{2,1,0:T(8,128)(2,1)S(1)}, u32[]{:S(2)}, u32[]{:S(2)}) async-start(bf16[8,64,768]{2,1,0:T(8,128)(2,1)} %get-tuple-element.146), calls=%async_computation.7 | async-start | bytes 1572864 | tf_op jit(solution)/shard_map/all_to_all | solution.py:1019
  270.1 41.5 %collective-permute-start.33 = (bf16[192,2048]{1,0:T(8,128)(2,1)}, bf16[192,2048]{1,0:T(8,128)(2,1)}, u32[]{:S(2)}, u32[]{:S(2)}) collective-permute-start(bf16[192,2048]{1,0:T(8,128)(2,1)} %copy-done.82), channel_id=1, source_target_pairs={{0,2},{2,0},{1,3},{3,1},{4,6},{6,4},{5,7},{7,5},{8,10},{10,8},{9,1... | collective-permute-start | bytes 2359304 | tf_op jit(solution)/shard_map/ppermute | solution.py:945
  270.2 40.7 %collective-permute-start.34 = (bf16[192,2048]{1,0:T(8,128)(2,1)}, bf16[192,2048]{1,0:T(8,128)(2,1)}, u32[]{:S(2)}, u32[]{:S(2)}) collective-permute-start(bf16[192,2048]{1,0:T(8,128)(2,1)} %bitcast.43.refs_4_), channel_id=1, source_target_pairs={{0,1},{1,0},{2,3},{3,2},{4,5},{5,4},{6,7},{7,6},{8,9},{9,8},{10,11... | collective-permute-start | bytes 2359304 | tf_op jit(solution)/shard_map/ppermute | solution.py:945
  304.8 26.3 %all-to-all-start.8 = ((bf16[8,32,1536]{2,1,0:T(8,128)(2,1)}), bf16[8,32,1536]{2,1,0:T(8,128)(2,1)S(1)}, u32[]{:S(2)}, u32[]{:S(2)}) async-start(bf16[8,32,1536]{2,1,0:T(8,128)(2,1)} %bitcast.194), calls=%async_computation.8 | async-start | bytes 1572864 | tf_op jit(solution)/shard_map/all_to_all | solution.py:1019
  350.7 24.3 %all-to-all-start.9 = ((bf16[8,32,1536]{2,1,0:T(8,128)(2,1)}), bf16[8,32,1536]{2,1,0:T(8,128)(2,1)S(1)}, u32[]{:S(2)}, u32[]{:S(2)}) async-start(bf16[8,32,1536]{2,1,0:T(8,128)(2,1)} %bitcast.195), calls=%async_computation.9 | async-start | bytes 1572864 | tf_op jit(solution)/shard_map/all_to_all | solution.py:1019
  355.5 33.8 %collective-permute-start.51 = (bf16[384,2048]{1,0:T(8,128)(2,1)}, bf16[384,2048]{1,0:T(8,128)(2,1)S(1)}, u32[]{:S(2)}, u32[]{:S(2)}) collective-permute-start(bf16[384,2048]{1,0:T(8,128)(2,1)} %get-tuple-element.171), channel_id=1, source_target_pairs={{0,2},{2,0},{1,3},{3,1},{4,6},{6,4},{5,7},{7,5},{8,10},{10,8},{9,1... | collective-permute-start | bytes 4718600 | tf_op jit(solution)/shard_map/ppermute | solution.py:945
  368.2 65.6 %collective-permute-start.53 = (bf16[384,2048]{1,0:T(8,128)(2,1)}, bf16[384,2048]{1,0:T(8,128)(2,1)}, u32[]{:S(2)}, u32[]{:S(2)}) collective-permute-start(bf16[384,2048]{1,0:T(8,128)(2,1)} %get-tuple-element.184), channel_id=1, source_target_pairs={{0,2},{2,0},{1,3},{3,1},{4,6},{6,4},{5,7},{7,5},{8,10},{10,8},{9,1... | collective-permute-start | bytes 4718600 | tf_op jit(solution)/shard_map/ppermute | solution.py:945
  390.6 31.9 %collective-permute-start.52 = (bf16[192,2048]{1,0:T(8,128)(2,1)S(1)}, bf16[192,2048]{1,0:T(8,128)(2,1)S(1)}, u32[]{:S(2)}, u32[]{:S(2)}) collective-permute-start(bf16[192,2048]{1,0:T(8,128)(2,1)S(1)} %slice.330), channel_id=1, source_target_pairs={{0,1},{1,0},{2,3},{3,2},{4,5},{5,4},{6,7},{7,6},{8,9},{9,8},{10,11... | collective-permute-start | bytes 2359304 | tf_op jit(solution)/shard_map/ppermute | solution.py:945
  396.2 86.0 %collective-permute-start.68 = (bf16[8,128,768]{2,1,0:T(8,128)(2,1)}, bf16[8,128,768]{2,1,0:T(8,128)(2,1)}, u32[]{:S(2)}, u32[]{:S(2)}) collective-permute-start(bf16[8,128,768]{2,1,0:T(8,128)(2,1)} %get-tuple-element.208), channel_id=1, source_target_pairs={{0,2},{2,0},{1,3},{3,1},{4,6},{6,4},{5,7},{7,5},{8,10},{10,8},{9,1... | collective-permute-start | bytes 4718600 | tf_op jit(solution)/shard_map/ppermute | solution.py:945
  404.9 28.2 %collective-permute-start.45 = (bf16[128,896]{1,0:T(8,128)(2,1)S(1)}, bf16[128,896]{1,0:T(8,128)(2,1)S(1)}, u32[]{:S(2)}, u32[]{:S(2)}) collective-permute-start(bf16[128,896]{1,0:T(8,128)(2,1)S(1)} %collective-permute-done.44), channel_id=1, source_target_pairs={{0,4},{4,0},{1,5},{5,1},{2,6},{6,2},{3,7},{7,3},{8,12},{12,8},{9,1... | collective-permute-start | bytes 688136 | tf_op jit(solution)/shard_map/ppermute | solution.py:945
  425.2 77.9 %collective-permute-start.75 = (bf16[384,768]{1,0:T(8,128)(2,1)}, bf16[384,768]{1,0:T(8,128)(2,1)}, u32[]{:S(2)}, u32[]{:S(2)}) collective-permute-start(bf16[384,768]{1,0:T(8,128)(2,1)} %get-tuple-element.222), channel_id=1, source_target_pairs={{0,2},{2,0},{1,3},{3,1},{4,6},{6,4},{5,7},{7,5},{8,10},{10,8},{9,1... | collective-permute-start | bytes 1769480 | tf_op jit(solution)/shard_map/ppermute | solution.py:945
  425.4 28.3 %all-to-all-start.10 = ((bf16[8,24,2048]{2,1,0:T(8,128)(2,1)}), bf16[8,24,2048]{2,1,0:T(8,128)(2,1)S(1)}, u32[]{:S(2)}, u32[]{:S(2)}) async-start(bf16[8,24,2048]{2,1,0:T(8,128)(2,1)} %bitcast.61), calls=%async_computation.10 | async-start | bytes 1572864 | tf_op jit(solution)/shard_map/all_to_all | solution.py:1019
  439.4 34.4 %collective-permute-start.54 = (bf16[192,2048]{1,0:T(8,128)(2,1)}, bf16[192,2048]{1,0:T(8,128)(2,1)}, u32[]{:S(2)}, u32[]{:S(2)}) collective-permute-start(bf16[192,2048]{1,0:T(8,128)(2,1)} %slice.332), channel_id=1, source_target_pairs={{0,1},{1,0},{2,3},{3,2},{4,5},{5,4},{6,7},{7,6},{8,9},{9,8},{10,11... | collective-permute-start | bytes 2359304 | tf_op jit(solution)/shard_map/ppermute | solution.py:945
  473.8 40.0 %collective-permute-start.66 = (bf16[384,2432]{1,0:T(8,128)(2,1)}, bf16[384,2432]{1,0:T(8,128)(2,1)S(1)}, u32[]{:S(2)}, u32[]{:S(2)}) collective-permute-start(bf16[384,2432]{1,0:T(8,128)(2,1)} %get-tuple-element.202), channel_id=1, source_target_pairs={{0,2},{2,0},{1,3},{3,1},{4,6},{6,4},{5,7},{7,5},{8,10},{10,8},{9,1... | collective-permute-start | bytes 5603336 | tf_op jit(solution)/shard_map/ppermute | solution.py:945
  477.1 30.4 %all-to-all-start.12 = ((bf16[8,24,2048]{2,1,0:T(8,128)(2,1)}), bf16[8,24,2048]{2,1,0:T(8,128)(2,1)S(1)}, u32[]{:S(2)}, u32[]{:S(2)}) async-start(bf16[8,24,2048]{2,1,0:T(8,128)(2,1)} %bitcast.64), calls=%async_computation.12 | async-start | bytes 1572864 | tf_op jit(solution)/shard_map/all_to_all | solution.py:1019
  505.2 125.6 %collective-permute-start.76 = (bf16[192,768]{1,0:T(8,128)(2,1)}, bf16[192,768]{1,0:T(8,128)(2,1)}, u32[]{:S(2)}, u32[]{:S(2)}) collective-permute-start(bf16[192,768]{1,0:T(8,128)(2,1)} %slice.342), channel_id=1, source_target_pairs={{0,1},{1,0},{2,3},{3,2},{4,5},{5,4},{6,7},{7,6},{8,9},{9,8},{10,11... | collective-permute-start | bytes 884744 | tf_op jit(solution)/shard_map/ppermute | solution.py:945
  506.2 26.3 %collective-permute-start.71 = (bf16[384,2048]{1,0:T(8,128)(2,1)}, bf16[384,2048]{1,0:T(8,128)(2,1)}, u32[]{:S(2)}, u32[]{:S(2)}) collective-permute-start(bf16[384,2048]{1,0:T(8,128)(2,1)} %get-tuple-element.215), channel_id=1, source_target_pairs={{0,2},{2,0},{1,3},{3,1},{4,6},{6,4},{5,7},{7,5},{8,10},{10,8},{9,1... | collective-permute-start | bytes 4718600 | tf_op jit(solution)/shard_map/ppermute | solution.py:945
  518.5 66.6 %collective-permute-start.67 = (bf16[192,2432]{1,0:T(8,128)(2,1)}, bf16[192,2432]{1,0:T(8,128)(2,1)}, u32[]{:S(2)}, u32[]{:S(2)}) collective-permute-start(bf16[192,2432]{1,0:T(8,128)(2,1)} %slice.334), channel_id=1, source_target_pairs={{0,1},{1,0},{2,3},{3,2},{4,5},{5,4},{6,7},{7,6},{8,9},{9,8},{10,11... | collective-permute-start | bytes 2801672 | tf_op jit(solution)/shard_map/ppermute | solution.py:945
  536.5 27.0 %collective-permute-start.56 = (bf16[128,896]{1,0:T(8,128)(2,1)S(1)}, bf16[128,896]{1,0:T(8,128)(2,1)S(1)}, u32[]{:S(2)}, u32[]{:S(2)}) collective-permute-start(bf16[128,896]{1,0:T(8,128)(2,1)S(1)} %copy-done.4), channel_id=1, source_target_pairs={{0,16},{8,24},{16,0},{24,8},{1,17},{9,25},{17,1},{25,9},{2,18},{10... | collective-permute-start | bytes 688136 | tf_op jit(solution)/shard_map/ppermute | solution.py:960
  539.1 24.5 %collective-permute-start.59 = (bf16[128,896]{1,0:T(8,128)(2,1)S(1)}, bf16[128,896]{1,0:T(8,128)(2,1)S(1)}, u32[]{:S(2)}, u32[]{:S(2)}) collective-permute-start(bf16[128,896]{1,0:T(8,128)(2,1)S(1)} %copy-done.4), channel_id=1, source_target_pairs={{0,8},{8,16},{16,24},{24,0},{1,9},{9,17},{17,25},{25,1},{2,10},{10... | collective-permute-start | bytes 688136 | tf_op jit(solution)/shard_map/ppermute | solution.py:960
  572.6 38.3 %collective-permute-start.74 = (bf16[192,2048]{1,0:T(8,128)(2,1)}, bf16[192,2048]{1,0:T(8,128)(2,1)}, u32[]{:S(2)}, u32[]{:S(2)}) collective-permute-start(bf16[192,2048]{1,0:T(8,128)(2,1)} %slice.340), channel_id=1, source_target_pairs={{0,1},{1,0},{2,3},{3,2},{4,5},{5,4},{6,7},{7,6},{8,9},{9,8},{10,11... | collective-permute-start | bytes 2359304 | tf_op jit(solution)/shard_map/ppermute | solution.py:945
  577.6 27.9 %all-to-all-start.14 = ((bf16[8,64,768]{2,1,0:T(8,128)(2,1)}), bf16[8,64,768]{2,1,0:T(8,128)(2,1)}, u32[]{:S(2)}, u32[]{:S(2)}) async-start(bf16[8,64,768]{2,1,0:T(8,128)(2,1)} %add_convert_fusion.11), calls=%async_computation.14 | async-start | bytes 1572864 | tf_op jit(solution)/shard_map/all_to_all | solution.py:1019
  587.6 45.4 %collective-permute-start.77 = (bf16[8,128,768]{2,1,0:T(8,128)(2,1)}, bf16[8,128,768]{2,1,0:T(8,128)(2,1)}, u32[]{:S(2)}, u32[]{:S(2)}) collective-permute-start(bf16[8,128,768]{2,1,0:T(8,128)(2,1)} %get-tuple-element.226), channel_id=1, source_target_pairs={{0,2},{2,0},{1,3},{3,1},{4,6},{6,4},{5,7},{7,5},{8,10},{10,8},{9,1... | collective-permute-start | bytes 4718600 | tf_op jit(solution)/shard_map/ppermute | solution.py:945
  588.2 24.1 %collective-permute-start.72 = (bf16[192,2048]{1,0:T(8,128)(2,1)}, bf16[192,2048]{1,0:T(8,128)(2,1)}, u32[]{:S(2)}, u32[]{:S(2)}) collective-permute-start(bf16[192,2048]{1,0:T(8,128)(2,1)} %slice.338), channel_id=1, source_target_pairs={{0,1},{1,0},{2,3},{3,2},{4,5},{5,4},{6,7},{7,6},{8,9},{9,8},{10,11... | collective-permute-start | bytes 2359304 | tf_op jit(solution)/shard_map/ppermute | solution.py:945
  626.4 51.0 %all-to-all-start.16 = ((bf16[8,24,4096]{2,1,0:T(8,128)(2,1)}), bf16[8,24,4096]{2,1,0:T(8,128)(2,1)S(1)}, u32[]{:S(2)}, u32[]{:S(2)}) async-start(bf16[8,24,4096]{2,1,0:T(8,128)(2,1)} %pad_maximum_fusion), calls=%async_computation.16 | async-start | bytes 3145728 | tf_op jit(solution)/shard_map/all_to_all | solution.py:1019
  630.8 81.7 %reduce-scatter.4.cloned.1.call-start = ((), (), s32[]{:S(2)}) async-start(), calls=%async_computation.22 | async-start | bytes 1382400
  636.2 45.6 %collective-permute-start.78 = (bf16[8,64,768]{2,1,0:T(8,128)(2,1)}, bf16[8,64,768]{2,1,0:T(8,128)(2,1)}, u32[]{:S(2)}, u32[]{:S(2)}) collective-permute-start(bf16[8,64,768]{2,1,0:T(8,128)(2,1)} %slice.345), channel_id=1, source_target_pairs={{0,1},{1,0},{2,3},{3,2},{4,5},{5,4},{6,7},{7,6},{8,9},{9,8},{10,11... | collective-permute-start | bytes 2359304 | tf_op jit(solution)/shard_map/ppermute | solution.py:945
  659.0 24.3 %collective-permute-start.80 = (bf16[192,768]{1,0:T(8,128)(2,1)}, bf16[192,768]{1,0:T(8,128)(2,1)}, u32[]{:S(2)}, u32[]{:S(2)}) collective-permute-start(bf16[192,768]{1,0:T(8,128)(2,1)} %slice.347), channel_id=1, source_target_pairs={{0,1},{1,0},{2,3},{3,2},{4,5},{5,4},{6,7},{7,6},{8,9},{9,8},{10,11... | collective-permute-start | bytes 884744 | tf_op jit(solution)/shard_map/ppermute | solution.py:945
  677.4 35.1 %all-to-all-start.17 = ((bf16[16,24,272]{2,1,0:T(8,128)(2,1)}), bf16[16,24,272]{2,1,0:T(8,128)(2,1)S(1)}, u32[]{:S(2)}, u32[]{:S(2)}) async-start(bf16[16,24,272]{2,1,0:T(8,128)(2,1)} %fusion.14), calls=%async_computation.17 | async-start | bytes 589824 | tf_op jit(solution)/shard_map/all_to_all | solution.py:1483
  712.5 28.8 %all-to-all-start.18 = ((bf16[8,88,768]{2,1,0:T(8,128)(2,1)}), bf16[8,88,768]{2,1,0:T(8,128)(2,1)S(1)}, u32[]{:S(2)}, u32[]{:S(2)}) async-start(bf16[8,88,768]{2,1,0:T(8,128)(2,1)} %pad_maximum_fusion.2), calls=%async_computation.18 | async-start | bytes 2162688 | tf_op jit(solution)/shard_map/all_to_all | solution.py:1019
  (143 other events, 1499.3 us)
Sparse Core Ops, SparseCore 0:
  17.3 90.4 all-gather.2
  135.1 84.6 all-gather.4
  635.6 76.8 reduce-scatter.3

commit v4 on v3

--- a/solution.py
+++ b/solution.py
@@ -907,7 +907,7 @@
     "xj_d0": ("", ""),
     "p_o0": ("sall0", ""),
     "xj_o0": ("", ""),
-    "rs": ("key0", "part"),
+    "rs": ("key0", ""),
     "r_u0": ("cols", "part0"),
     "r_d0": ("part", ""),
 }
@@ -961,7 +961,8 @@
     blocks, filled = [], []
     for step, block in enumerate(found):
         if 0 < step <= len(fillers):
-            filled.append(fillers[step - 1](block if step > 1 else blocks[0]))
+            beside = [block] if step > 1 else [blocks[0]]
+            filled.append(fillers[step - 1](*beside, *filled[-1:]))
             block = after(block, filled[-1])
         pair = jnp.concatenate([block, swap(block, near)], axis=0)
         blocks += [pair, swap(pair, core)]
@@ -1405,11 +1406,11 @@
             ],
             6 * rows * width * width,
         )
-        def some_queries(start, dependence):
+        def some_queries(start, *things):
             return query_back(
                 start,
                 2,
-                after(projected, dependence),
+                after(projected, *things),
                 sent,
                 totals,
                 delta,

time: 769 us -> 759 us (0.987)
  waiting for transfers between devices: 233 us -> 212 us
    all_to_all x17, waiting for transfers between devices: 128 us -> 102 us  [deal_out(): return lax.all_to_all(x, ex_axes, 0, 0, tiled=True)]
    ppermute x12, waiting for transfers between devices: 31.4 us -> 11.4 us  [gather_rows(): found.append(lax.ppermute(x, far, pairs))]
    ppermute x69, waiting for transfers between devices: 34.8 us -> 44.7 us  [swap(): return lax.ppermute(x, axis, [(0, 1), (1, 0)])]
    all_to_all x1, waiting for transfers between devices: 0.01 us -> 9.9 us  [shards(): part = lax.all_to_all(part, axes, 0, 0, tiled=True)]
    unnamed x204 -> x206, local copies, waits for them, and re-layouts: 29.4 us -> 33.1 us
  transfers between devices with their start and end apart: 103 -> 103, of which waited for: 36 -> 35; matrix products, arithmetic and copies ran while one was open for 16% -> 17% of each run, Pallas kernels for 23% -> 24%
where the time goes in v4:
time: 759 us; the launch traced here: 747 us
  waiting for transfers between devices  212 us (28%)
  Pallas kernels  199 us (26%)
  starting transfers between devices  156 us (21%)
  local copies, waits for them, and re-layouts  88.3 us (12%)
  other arithmetic  65.8 us (9%)
  between operations  15.9 us (2%)
  matrix products  10.5 us (1%)
    all_to_all x17, waiting for transfers between devices, deal_out(): return lax.all_to_all(x, ex_axes, 0, 0, tiled=True)  102 us
    all_to_all x17, starting transfers between devices, deal_out(): return lax.all_to_all(x, ex_axes, 0, 0, tiled=True)  78.8 us
    ppermute x69, starting transfers between devices, swap(): return lax.ppermute(x, axis, [(0, 1), (1, 0)])  47.5 us
    ppermute x69, waiting for transfers between devices, swap(): return lax.ppermute(x, axis, [(0, 1), (1, 0)])  44.7 us
    pallas_call x2, Pallas kernels, run_expert_back(): pl.pallas_call(functools.partial(expert_back_kernel, both), grid=(EXPERTS...  34.9 us
    pallas_call x2, Pallas kernels, project(): pl.pallas_call(functools.partial(project_kernel, 2 * SPLIT, len(blocks),...  34.2 us
    pallas_call x8, Pallas kernels, run_fused(): pl.pallas_call(kernel, grid=(1,), in_specs=specs, out_specs=[pl.BlockSpec...  33.6 us
    unnamed x206, local copies, waits for them, and re-layouts  33.1 us
  transfers between devices with their start and end apart: 103, of which 35 were waited for; matrix products, arithmetic and copies ran while one was open for 17% of the time, Pallas kernels for 24%

profile of v4, /device:TPU:0, one launch (start us, length us, event | category | flops | bytes accessed | tf_op | source)
XLA Modules:
  0.0 746.6 jit_solution(978737875751309574)
XLA Ops:
  35.6 5.6 fusion.13
  42.5 25.3 %all-to-all-done.1 = bf16[8,24,2048]{2,1,0:T(8,128)(2,1)S(1)} async-done(((bf16[8,24,2048]{2,1,0:T(8,128)(2,1)}), bf16[8,24,2048]{2,1,0:T(8,128)(2,1)S(1)}, u32[]{:S(2)}, u32[]{:S(2)}) %all-to-all-start.1) | async-done | bytes 786464 | tf_op jit(solution)/shard_map/all_to_all | solution.py:1020
  85.5 5.6 collective-permute-done.3
  91.8 8.9 %all-to-all-done = bf16[8,24,2048]{2,1,0:T(8,128)(2,1)S(1)} async-done(((bf16[8,24,2048]{2,1,0:T(8,128)(2,1)}), bf16[8,24,2048]{2,1,0:T(8,128)(2,1)S(1)}, u32[]{:S(2)}, u32[]{:S(2)}) %all-to-all-start) | async-done | bytes 786464 | tf_op jit(solution)/shard_map/all_to_all | solution.py:1020
  100.8 5.3 all-to-all-start.2
  117.2 17.7 %shard_map.265.q_ref.k_ref.v_ref = bf16[2048,2304]{1,0:T(8,128)(2,1)} custom-call(bf16[256,768]{1,0:T(8,128)(2,1)} %copy-done.31, bf16[256,768]{1,0:T(8,128)(2,1)} %collective-permute-done.1.refs_1_, bf16[256,768]{1,0:T(8,128)(2,1)} %constant_dynamic-update-slice_fusion.refs_2_, bf16[256,768]{1,0:T(8,128)(2,1)} %collective-permute-done.4.refs_3_, ...), custom_call_target="tpu_custom_call" | custom-call | flops 7247757312 | bytes 16121856 | tf_op jit(solution)/shard_map/pallas_call | solution.py:119
  135.0 6.1 all-to-all-start.3
  146.6 10.1 %shard_map.266 = (f32[128,768]{1,0:T(8,128)}, f32[128,128]{1,0:T(8,128)}) custom-call(bf16[2048,2304]{1,0:T(8,128)(2,1)} %shard_map.265.q_ref.k_ref.v_ref, bf16[2048,2304]{1,0:T(8,128)(2,1)} %shard_map.265.q_ref.k_ref.v_ref, bf16[2048,2304]{1,0:T(8,128)(2,1)} %shard_map.265.q_ref.k_ref.v_ref, s32[128,1]{1,0:T(8,128)} %broadcast_in_dim.105.at_ref.refs_16_, ...), custom_call_target="tpu_custom_call" | custom-call | flops 1610612736 | bytes 6291456 | tf_op jit(solution)/shard_map/pallas_call | solution.py:188
  168.4 16.0 %all-to-all-done.4 = bf16[8,32,768]{2,1,0:T(8,128)(2,1)S(1)} async-done(((bf16[8,32,768]{2,1,0:T(8,128)(2,1)}), bf16[8,32,768]{2,1,0:T(8,128)(2,1)S(1)}, u32[]{:S(2)}, u32[]{:S(2)}) %all-to-all-start.4) | async-done | bytes 393248 | tf_op jit(solution)/shard_map/all_to_all | solution.py:1020
  184.4 4.5 all-to-all-start.5
  197.6 11.2 %shard_map.268 = (f32[256,2048]{1,0:T(8,128)}, f32[256,2048]{1,0:T(8,128)}, bf16[256,768]{1,0:T(8,128)(2,1)}) custom-call(s32[1,2]{1,0:T(1,128)} %add_bitcast_fusion.flag_ref, bf16[256,768]{1,0:T(8,128)(2,1)} %bitcast.186, bf16[192,2048]{1,0:T(8,128)(2,1)} %bitcast.167, bf16[192,2048]{1,0:T(8,128)(2,1)} %collective-permute-done.11.refs_1_.refs_3_, ...), custom_call_target="tpu_custom_call" | custom-call | flops 2415919104 | bytes 13631488 | tf_op jit(solution)/shard_map/pallas_call | solution.py:422
  208.8 10.8 %all-to-all-done.5 = bf16[8,24,2048]{2,1,0:T(8,128)(2,1)} async-done(((bf16[8,24,2048]{2,1,0:T(8,128)(2,1)}), bf16[8,24,2048]{2,1,0:T(8,128)(2,1)}, u32[]{:S(2)}, u32[]{:S(2)}) %all-to-all-start.5) | async-done | bytes 786464 | tf_op jit(solution)/shard_map/all_to_all | solution.py:1020
  223.9 11.0 %all-to-all-done.6 = bf16[8,32,768]{2,1,0:T(8,128)(2,1)S(1)} async-done(((bf16[8,32,768]{2,1,0:T(8,128)(2,1)}), bf16[8,32,768]{2,1,0:T(8,128)(2,1)S(1)}, u32[]{:S(2)}, u32[]{:S(2)}) %all-to-all-start.6) | async-done | bytes 393248 | tf_op jit(solution)/shard_map/all_to_all | solution.py:1020
  257.9 4.5 collective-permute-done.25
  273.0 16.4 %shard_map.270.q_ref.k_ref.v_ref = bf16[2048,2304]{1,0:T(8,128)(2,1)} custom-call(bf16[256,768]{1,0:T(8,128)(2,1)} %copy-done.67, bf16[256,768]{1,0:T(8,128)(2,1)} %collective-permute-done.21.refs_1_, bf16[256,768]{1,0:T(8,128)(2,1)} %copy-done.65, bf16[256,768]{1,0:T(8,128)(2,1)} %copy-done.87, bf16[256,768]{1,0:T(8,128)(2,1)} %copy-done.64, ...), custom_call_target="tpu_custom_call" | custom-call | flops 7247757312 | bytes 16121856 | tf_op jit(solution)/shard_map/pallas_call | solution.py:119
  289.4 10.1 %shard_map.271 = (f32[128,768]{1,0:T(8,128)}, f32[128,128]{1,0:T(8,128)}) custom-call(bf16[2048,2304]{1,0:T(8,128)(2,1)} %shard_map.270.q_ref.k_ref.v_ref, bf16[2048,2304]{1,0:T(8,128)(2,1)} %shard_map.270.q_ref.k_ref.v_ref, bf16[2048,2304]{1,0:T(8,128)(2,1)} %shard_map.270.q_ref.k_ref.v_ref, s32[128,1]{1,0:T(8,128)} %broadcast_in_dim.105.at_ref.refs_16_, ...), custom_call_target="tpu_custom_call" | custom-call | flops 1610612736 | bytes 6291456 | tf_op jit(solution)/shard_map/pallas_call | solution.py:188
  304.9 6.1 all-to-all-start.8
  312.0 7.2 collective-permute-done.37.refs_9_
  320.2 10.9 %all-to-all-done.8 = bf16[8,32,1536]{2,1,0:T(8,128)(2,1)S(1)} async-done(((bf16[8,32,1536]{2,1,0:T(8,128)(2,1)}), bf16[8,32,1536]{2,1,0:T(8,128)(2,1)S(1)}, u32[]{:S(2)}, u32[]{:S(2)}) %all-to-all-start.8) | async-done | bytes 786464 | tf_op jit(solution)/shard_map/all_to_all | solution.py:1020
  332.0 18.7 %shard_map.273 = (bf16[384,2048]{1,0:T(8,128)(2,1)}, bf16[384,2048]{1,0:T(8,128)(2,1)}, bf16[384,2048]{1,0:T(8,128)(2,1)}, bf16[384,2048]{1,0:T(8,128)(2,1)}, bf...) custom-call(s32[1,2]{1,0:T(1,128)} %add_bitcast_fusion.flag_ref, ...), custom_call_target="tpu_custom_call" | custom-call | flops 7247757312 | bytes 23068672 | tf_op jit(solution)/shard_map/pallas_call | solution.py:519
  356.2 4.8 shard_map.289
  361.0 4.7 copy.251
  368.7 6.3 all-to-all-done.9
  376.6 5.1 shard_map.274
  392.5 4.6 shard_map.276.refs_0_
  397.2 4.6 shard_map.277.refs_1_
  405.3 4.6 shard_map.278.refs_2_
  410.0 7.6 %collective-permute-done.49 = bf16[128,896]{1,0:T(8,128)(2,1)S(1)} collective-permute-done((bf16[128,896]{1,0:T(8,128)(2,1)S(1)}, bf16[128,896]{1,0:T(8,128)(2,1)S(1)}, u32[]{:S(2)}, u32[]{:S(2)}) %collective-permute-start.49) | collective-permute-done | bytes 229408 | tf_op jit(solution)/shard_map/ppermute | solution.py:945
  434.1 11.4 %shard_map.279 = (bf16[128,768]{1,0:T(8,128)(2,1)}, bf16[128,768]{1,0:T(8,128)(2,1)}) custom-call(bf16[2048,2304]{1,0:T(8,128)(2,1)} %shard_map.270.q_ref.k_ref.v_ref, bf16[2048,2304]{1,0:T(8,128)(2,1)} %shard_map.270.q_ref.k_ref.v_ref, bf16[2048,2304]{1,0:T(8,128)(2,1)} %shard_map.270.q_ref.k_ref.v_ref, ...), custom_call_target="tpu_custom_call" | custom-call | flops 3221225472 | bytes 6291456 | tf_op jit(solution)/shard_map/pallas_call | solution.py:346
  445.8 5.4 shard_map.280
  451.2 5.8 all-to-all-start.11
  469.1 5.0 all-to-all-start.12
  477.6 16.3 %shard_map.281 = (bf16[384,2048]{1,0:T(8,128)(2,1)}, bf16[384,2048]{1,0:T(8,128)(2,1)}, bf16[384,2048]{1,0:T(8,128)(2,1)}, bf16[384,2048]{1,0:T(8,128)(2,1)}, bf...) custom-call(s32[1,2]{1,0:T(1,128)} %add_bitcast_fusion.flag_ref, ...), custom_call_target="tpu_custom_call" | custom-call | flops 4831838208 | bytes 23068672 | tf_op jit(solution)/shard_map/pallas_call | solution.py:519
  499.6 6.2 all-to-all-start.13
  511.6 6.3 all-to-all-done.13
  518.7 5.1 shard_map.282
  533.4 4.6 shard_map.283.refs_0_
  543.2 4.6 shard_map.284.refs_1_
  547.8 4.7 shard_map.285.refs_2_
  574.6 5.0 all-to-all-start.14
  584.5 11.4 %shard_map.286 = (bf16[128,768]{1,0:T(8,128)(2,1)}, bf16[128,768]{1,0:T(8,128)(2,1)}) custom-call(bf16[2048,2304]{1,0:T(8,128)(2,1)} %shard_map.265.q_ref.k_ref.v_ref, bf16[2048,2304]{1,0:T(8,128)(2,1)} %shard_map.265.q_ref.k_ref.v_ref, bf16[2048,2304]{1,0:T(8,128)(2,1)} %shard_map.265.q_ref.k_ref.v_ref, ...), custom_call_target="tpu_custom_call" | custom-call | flops 3221225472 | bytes 6291456 | tf_op jit(solution)/shard_map/pallas_call | solution.py:346
  600.4 4.7 all-to-all-start.15
  609.2 11.5 %all-to-all-done.15 = bf16[16,128,144]{1,2,0:T(8,128)(2,1)} async-done(((bf16[16,128,144]{1,2,0:T(8,128)(2,1)}), bf16[16,128,144]{1,2,0:T(8,128)(2,1)}, u32[]{:S(2)}, u32[]{:S(2)}) %all-to-all-start.15) | async-done | bytes 589856 | tf_op jit(solution)/shard_map/all_to_all | solution.py:1478
  635.0 4.7 shard_map.288
  654.6 7.9 %collective-permute-done.70 = bf16[16,24,272]{2,1,0:T(8,128)(2,1)} collective-permute-done((bf16[16,24,272]{2,1,0:T(8,128)(2,1)}, bf16[16,24,272]{2,1,0:T(8,128)(2,1)}, u32[]{:S(2)}, u32[]{:S(2)}) %collective-permute-start.70) | collective-permute-done | bytes 208928 | tf_op jit(solution)/shard_map/ppermute | solution.py:945
  664.4 5.8 all-to-all-start.17
  673.7 9.9 %all-to-all-done.17 = bf16[16,24,272]{2,1,0:T(8,128)(2,1)S(1)} async-done(((bf16[16,24,272]{2,1,0:T(8,128)(2,1)}), bf16[16,24,272]{2,1,0:T(8,128)(2,1)S(1)}, u32[]{:S(2)}, u32[]{:S(2)}) %all-to-all-start.17) | async-done | bytes 208928 | tf_op jit(solution)/shard_map/all_to_all | solution.py:1484
  696.6 31.9 %reduce-scatter.4.cloned.1.call-done = bf16[24,3200]{1,0:T(8,128)(2,1)} async-done(((bf16[192,3200]{1,0:T(8,128)(2,1)}), bf16[24,3200]{1,0:T(8,128)(2,1)}) %reduce-scatter.4.cloned.1.call-update) | async-done | bytes 153616 | tf_op jit(solution)/shard_map/optimization_barrier | solution.py:866
  (563 shorter events, 308.0 us)
Async XLA Ops:
  7.2 103.0 %all-gather.3.cloned.1.call-start = ((), (), s32[]{:S(2)}) async-start(), calls=%async_computation.20 | async-start | bytes 5068800 | tf_op jit(solution)/shard_map/all_gather | solution.py:1045
  17.2 57.3 %collective-permute-start = (bf16[128,768]{1,0:T(8,128)(2,1)}, bf16[128,768]{1,0:T(8,128)(2,1)}, u32[]{:S(2)}, u32[]{:S(2)}) collective-permute-start(bf16[128,768]{1,0:T(8,128)(2,1)} %bitcast.197), channel_id=1, source_target_pairs={{0,4},{4,0},{1,5},{5,1},{2,6},{6,2},{3,7},{7,3},{8,12},{12,8},{9,1... | collective-permute-start | bytes 589832 | tf_op jit(solution)/shard_map/ppermute | solution.py:945
  20.3 55.4 %collective-permute-start.2 = (bf16[128,768]{1,0:T(8,128)(2,1)}, bf16[128,768]{1,0:T(8,128)(2,1)}, u32[]{:S(2)}, u32[]{:S(2)}) collective-permute-start(bf16[128,768]{1,0:T(8,128)(2,1)} %bitcast.198), channel_id=1, source_target_pairs={{0,8},{8,16},{16,24},{24,0},{1,9},{9,17},{17,25},{25,1},{2,10},{10... | collective-permute-start | bytes 589832 | tf_op jit(solution)/shard_map/ppermute | solution.py:960
  21.8 55.7 %collective-permute-start.5 = (bf16[128,768]{1,0:T(8,128)(2,1)}, bf16[128,768]{1,0:T(8,128)(2,1)}, u32[]{:S(2)}, u32[]{:S(2)}) collective-permute-start(bf16[128,768]{1,0:T(8,128)(2,1)} %bitcast.199), channel_id=1, source_target_pairs={{0,16},{8,24},{16,0},{24,8},{1,17},{9,25},{17,1},{25,9},{2,18},{10... | collective-permute-start | bytes 589832 | tf_op jit(solution)/shard_map/ppermute | solution.py:960
  24.4 53.3 %collective-permute-start.8 = (bf16[128,768]{1,0:T(8,128)(2,1)}, bf16[128,768]{1,0:T(8,128)(2,1)}, u32[]{:S(2)}, u32[]{:S(2)}) collective-permute-start(bf16[128,768]{1,0:T(8,128)(2,1)} %bitcast.200), channel_id=1, source_target_pairs={{0,24},{8,0},{16,8},{24,16},{1,25},{9,1},{17,9},{25,17},{2,26},{10... | collective-permute-start | bytes 589832 | tf_op jit(solution)/shard_map/ppermute | solution.py:960
  28.5 39.3 %all-to-all-start.1 = ((bf16[8,24,2048]{2,1,0:T(8,128)(2,1)}), bf16[8,24,2048]{2,1,0:T(8,128)(2,1)S(1)}, u32[]{:S(2)}, u32[]{:S(2)}) async-start(bf16[8,24,2048]{2,1,0:T(8,128)(2,1)} %get-tuple-element.315), calls=%async_computation.1 | async-start | bytes 1572864 | tf_op jit(solution)/shard_map/all_to_all | solution.py:1020
  67.8 32.9 %all-to-all-start = ((bf16[8,24,2048]{2,1,0:T(8,128)(2,1)}), bf16[8,24,2048]{2,1,0:T(8,128)(2,1)S(1)}, u32[]{:S(2)}, u32[]{:S(2)}) async-start(bf16[8,24,2048]{2,1,0:T(8,128)(2,1)} %get-tuple-element.122), calls=%async_computation | async-start | bytes 1572864 | tf_op jit(solution)/shard_map/all_to_all | solution.py:1020
  75.5 34.3 %collective-permute-start.1 = (bf16[256,768]{1,0:T(8,128)(2,1)S(1)}, bf16[256,768]{1,0:T(8,128)(2,1)}, u32[]{:S(2)}, u32[]{:S(2)}) collective-permute-start(bf16[256,768]{1,0:T(8,128)(2,1)S(1)} %pad_maximum_fusion.4.refs_0_), channel_id=1, source_target_pairs={{0,2},{2,0},{1,3},{3,1},{4,6},{6,4},{5,7},{7,5},{8,10},{10,8},{9,1... | collective-permute-start | bytes 1179656 | tf_op jit(solution)/shard_map/ppermute | solution.py:945
  77.6 28.5 %collective-permute-start.6 = (bf16[128,768]{1,0:T(8,128)(2,1)}, bf16[128,768]{1,0:T(8,128)(2,1)}, u32[]{:S(2)}, u32[]{:S(2)}) collective-permute-start(bf16[128,768]{1,0:T(8,128)(2,1)} %collective-permute-done.5), channel_id=1, source_target_pairs={{0,4},{4,0},{1,5},{5,1},{2,6},{6,2},{3,7},{7,3},{8,12},{12,8},{9,1... | collective-permute-start | bytes 589832 | tf_op jit(solution)/shard_map/ppermute | solution.py:945
  77.7 30.0 %collective-permute-start.9 = (bf16[128,768]{1,0:T(8,128)(2,1)}, bf16[128,768]{1,0:T(8,128)(2,1)S(1)}, u32[]{:S(2)}, u32[]{:S(2)}) collective-permute-start(bf16[128,768]{1,0:T(8,128)(2,1)} %collective-permute-done.8), channel_id=1, source_target_pairs={{0,4},{4,0},{1,5},{5,1},{2,6},{6,2},{3,7},{7,3},{8,12},{12,8},{9,1... | collective-permute-start | bytes 589832 | tf_op jit(solution)/shard_map/ppermute | solution.py:945
  83.8 26.4 %collective-permute-start.11 = (bf16[192,2048]{1,0:T(8,128)(2,1)S(1)}, bf16[192,2048]{1,0:T(8,128)(2,1)}, u32[]{:S(2)}, u32[]{:S(2)}) collective-permute-start(bf16[192,2048]{1,0:T(8,128)(2,1)S(1)} %bitcast.165), channel_id=1, source_target_pairs={{0,1},{1,0},{2,3},{3,2},{4,5},{5,4},{6,7},{7,6},{8,9},{9,8},{10,11... | collective-permute-start | bytes 2359304 | tf_op jit(solution)/shard_map/ppermute | solution.py:945
  100.8 34.2 %all-to-all-start.2 = ((bf16[8,64,768]{2,1,0:T(8,128)(2,1)}), bf16[8,64,768]{2,1,0:T(8,128)(2,1)S(1)}, u32[]{:S(2)}, u32[]{:S(2)}) async-start(bf16[8,64,768]{2,1,0:T(8,128)(2,1)} %get-tuple-element.311), calls=%async_computation.2 | async-start | bytes 1572864 | tf_op jit(solution)/shard_map/all_to_all | solution.py:1020
  106.1 117.8 %all-gather.5.cloned.1.call-start = ((), (), s32[]{:S(2)}) async-start(), calls=%async_computation.21 | async-start | bytes 5068800 | tf_op jit(solution)/shard_map/all_gather | solution.py:1045
  110.2 24.8 %collective-permute-start.12 = (bf16[192,2048]{1,0:T(8,128)(2,1)S(1)}, bf16[192,2048]{1,0:T(8,128)(2,1)}, u32[]{:S(2)}, u32[]{:S(2)}) collective-permute-start(bf16[192,2048]{1,0:T(8,128)(2,1)S(1)} %bitcast.169), channel_id=1, source_target_pairs={{0,1},{1,0},{2,3},{3,2},{4,5},{5,4},{6,7},{7,6},{8,9},{9,8},{10,11... | collective-permute-start | bytes 2359304 | tf_op jit(solution)/shard_map/ppermute | solution.py:945
  135.0 29.7 %all-to-all-start.3 = ((bf16[8,24,2048]{2,1,0:T(8,128)(2,1)}), bf16[8,24,2048]{2,1,0:T(8,128)(2,1)}, u32[]{:S(2)}, u32[]{:S(2)}) async-start(bf16[8,24,2048]{2,1,0:T(8,128)(2,1)} %get-tuple-element.131), calls=%async_computation.3 | async-start | bytes 1572864 | tf_op jit(solution)/shard_map/all_to_all | solution.py:1020
  146.2 22.1 %collective-permute-start.13 = (bf16[512,768]{1,0:T(8,128)(2,1)S(1)}, bf16[512,768]{1,0:T(8,128)(2,1)S(1)}, u32[]{:S(2)}, u32[]{:S(2)}) collective-permute-start(bf16[512,768]{1,0:T(8,128)(2,1)S(1)} %bitcast.173), channel_id=1, source_target_pairs={{0,1},{1,0},{2,3},{3,2},{4,5},{5,4},{6,7},{7,6},{8,9},{9,8},{10,11... | collective-permute-start | bytes 2359304 | tf_op jit(solution)/shard_map/ppermute | solution.py:945
  184.4 35.2 %all-to-all-start.5 = ((bf16[8,24,2048]{2,1,0:T(8,128)(2,1)}), bf16[8,24,2048]{2,1,0:T(8,128)(2,1)}, u32[]{:S(2)}, u32[]{:S(2)}) async-start(bf16[8,24,2048]{2,1,0:T(8,128)(2,1)} %get-tuple-element.137), calls=%async_computation.5 | async-start | bytes 1572864 | tf_op jit(solution)/shard_map/all_to_all | solution.py:1020
  239.6 24.6 %collective-permute-start.31 = (bf16[192,2048]{1,0:T(8,128)(2,1)}, bf16[192,2048]{1,0:T(8,128)(2,1)S(1)}, u32[]{:S(2)}, u32[]{:S(2)}) collective-permute-start(bf16[192,2048]{1,0:T(8,128)(2,1)} %bitcast.39.refs_0_), channel_id=1, source_target_pairs={{0,1},{1,0},{2,3},{3,2},{4,5},{5,4},{6,7},{7,6},{8,9},{9,8},{10,11... | collective-permute-start | bytes 2359304 | tf_op jit(solution)/shard_map/ppermute | solution.py:945
  265.9 33.6 %all-to-all-start.7 = ((bf16[8,64,768]{2,1,0:T(8,128)(2,1)}), bf16[8,64,768]{2,1,0:T(8,128)(2,1)S(1)}, u32[]{:S(2)}, u32[]{:S(2)}) async-start(bf16[8,64,768]{2,1,0:T(8,128)(2,1)} %get-tuple-element.145), calls=%async_computation.7 | async-start | bytes 1572864 | tf_op jit(solution)/shard_map/all_to_all | solution.py:1020
  270.2 41.4 %collective-permute-start.33 = (bf16[192,2048]{1,0:T(8,128)(2,1)}, bf16[192,2048]{1,0:T(8,128)(2,1)}, u32[]{:S(2)}, u32[]{:S(2)}) collective-permute-start(bf16[192,2048]{1,0:T(8,128)(2,1)} %copy-done.83), channel_id=1, source_target_pairs={{0,2},{2,0},{1,3},{3,1},{4,6},{6,4},{5,7},{7,5},{8,10},{10,8},{9,1... | collective-permute-start | bytes 2359304 | tf_op jit(solution)/shard_map/ppermute | solution.py:945
  270.2 40.7 %collective-permute-start.34 = (bf16[192,2048]{1,0:T(8,128)(2,1)}, bf16[192,2048]{1,0:T(8,128)(2,1)}, u32[]{:S(2)}, u32[]{:S(2)}) collective-permute-start(bf16[192,2048]{1,0:T(8,128)(2,1)} %bitcast.43.refs_4_), channel_id=1, source_target_pairs={{0,1},{1,0},{2,3},{3,2},{4,5},{5,4},{6,7},{7,6},{8,9},{9,8},{10,11... | collective-permute-start | bytes 2359304 | tf_op jit(solution)/shard_map/ppermute | solution.py:945
  304.9 26.2 %all-to-all-start.8 = ((bf16[8,32,1536]{2,1,0:T(8,128)(2,1)}), bf16[8,32,1536]{2,1,0:T(8,128)(2,1)S(1)}, u32[]{:S(2)}, u32[]{:S(2)}) async-start(bf16[8,32,1536]{2,1,0:T(8,128)(2,1)} %bitcast.195), calls=%async_computation.8 | async-start | bytes 1572864 | tf_op jit(solution)/shard_map/all_to_all | solution.py:1020
  350.7 24.4 %all-to-all-start.9 = ((bf16[8,32,1536]{2,1,0:T(8,128)(2,1)}), bf16[8,32,1536]{2,1,0:T(8,128)(2,1)S(1)}, u32[]{:S(2)}, u32[]{:S(2)}) async-start(bf16[8,32,1536]{2,1,0:T(8,128)(2,1)} %bitcast.196), calls=%async_computation.9 | async-start | bytes 1572864 | tf_op jit(solution)/shard_map/all_to_all | solution.py:1020
  355.5 33.9 %collective-permute-start.51 = (bf16[384,2048]{1,0:T(8,128)(2,1)}, bf16[384,2048]{1,0:T(8,128)(2,1)S(1)}, u32[]{:S(2)}, u32[]{:S(2)}) collective-permute-start(bf16[384,2048]{1,0:T(8,128)(2,1)} %get-tuple-element.170), channel_id=1, source_target_pairs={{0,2},{2,0},{1,3},{3,1},{4,6},{6,4},{5,7},{7,5},{8,10},{10,8},{9,1... | collective-permute-start | bytes 4718600 | tf_op jit(solution)/shard_map/ppermute | solution.py:945
  368.2 57.7 %collective-permute-start.53 = (bf16[384,2048]{1,0:T(8,128)(2,1)}, bf16[384,2048]{1,0:T(8,128)(2,1)}, u32[]{:S(2)}, u32[]{:S(2)}) collective-permute-start(bf16[384,2048]{1,0:T(8,128)(2,1)} %get-tuple-element.183), channel_id=1, source_target_pairs={{0,2},{2,0},{1,3},{3,1},{4,6},{6,4},{5,7},{7,5},{8,10},{10,8},{9,1... | collective-permute-start | bytes 4718600 | tf_op jit(solution)/shard_map/ppermute | solution.py:945
  390.7 27.6 %collective-permute-start.52 = (bf16[192,2048]{1,0:T(8,128)(2,1)S(1)}, bf16[192,2048]{1,0:T(8,128)(2,1)S(1)}, u32[]{:S(2)}, u32[]{:S(2)}) collective-permute-start(bf16[192,2048]{1,0:T(8,128)(2,1)S(1)} %slice.330), channel_id=1, source_target_pairs={{0,1},{1,0},{2,3},{3,2},{4,5},{5,4},{6,7},{7,6},{8,9},{9,8},{10,11... | collective-permute-start | bytes 2359304 | tf_op jit(solution)/shard_map/ppermute | solution.py:945
  397.1 77.0 %collective-permute-start.68 = (bf16[8,128,768]{2,1,0:T(8,128)(2,1)}, bf16[8,128,768]{2,1,0:T(8,128)(2,1)}, u32[]{:S(2)}, u32[]{:S(2)}) collective-permute-start(bf16[8,128,768]{2,1,0:T(8,128)(2,1)} %get-tuple-element.207), channel_id=1, source_target_pairs={{0,2},{2,0},{1,3},{3,1},{4,6},{6,4},{5,7},{7,5},{8,10},{10,8},{9,1... | collective-permute-start | bytes 4718600 | tf_op jit(solution)/shard_map/ppermute | solution.py:945
  401.9 23.3 %collective-permute-start.45 = (bf16[128,896]{1,0:T(8,128)(2,1)S(1)}, bf16[128,896]{1,0:T(8,128)(2,1)S(1)}, u32[]{:S(2)}, u32[]{:S(2)}) collective-permute-start(bf16[128,896]{1,0:T(8,128)(2,1)S(1)} %collective-permute-done.44), channel_id=1, source_target_pairs={{0,4},{4,0},{1,5},{5,1},{2,6},{6,2},{3,7},{7,3},{8,12},{12,8},{9,1... | collective-permute-start | bytes 688136 | tf_op jit(solution)/shard_map/ppermute | solution.py:945
  420.9 74.3 %collective-permute-start.75 = (bf16[384,768]{1,0:T(8,128)(2,1)}, bf16[384,768]{1,0:T(8,128)(2,1)}, u32[]{:S(2)}, u32[]{:S(2)}) collective-permute-start(bf16[384,768]{1,0:T(8,128)(2,1)} %get-tuple-element.221), channel_id=1, source_target_pairs={{0,2},{2,0},{1,3},{3,1},{4,6},{6,4},{5,7},{7,5},{8,10},{10,8},{9,1... | collective-permute-start | bytes 1769480 | tf_op jit(solution)/shard_map/ppermute | solution.py:945
  421.1 24.7 %all-to-all-start.10 = ((bf16[8,24,2048]{2,1,0:T(8,128)(2,1)}), bf16[8,24,2048]{2,1,0:T(8,128)(2,1)S(1)}, u32[]{:S(2)}, u32[]{:S(2)}) async-start(bf16[8,24,2048]{2,1,0:T(8,128)(2,1)} %bitcast.61), calls=%async_computation.10 | async-start | bytes 1572864 | tf_op jit(solution)/shard_map/all_to_all | solution.py:1020
  431.5 34.3 %collective-permute-start.54 = (bf16[192,2048]{1,0:T(8,128)(2,1)}, bf16[192,2048]{1,0:T(8,128)(2,1)}, u32[]{:S(2)}, u32[]{:S(2)}) collective-permute-start(bf16[192,2048]{1,0:T(8,128)(2,1)} %slice.332), channel_id=1, source_target_pairs={{0,1},{1,0},{2,3},{3,2},{4,5},{5,4},{6,7},{7,6},{8,9},{9,8},{10,11... | collective-permute-start | bytes 2359304 | tf_op jit(solution)/shard_map/ppermute | solution.py:945
  465.8 40.0 %collective-permute-start.66 = (bf16[384,2432]{1,0:T(8,128)(2,1)}, bf16[384,2432]{1,0:T(8,128)(2,1)S(1)}, u32[]{:S(2)}, u32[]{:S(2)}) collective-permute-start(bf16[384,2432]{1,0:T(8,128)(2,1)} %get-tuple-element.201), channel_id=1, source_target_pairs={{0,2},{2,0},{1,3},{3,1},{4,6},{6,4},{5,7},{7,5},{8,10},{10,8},{9,1... | collective-permute-start | bytes 5603336 | tf_op jit(solution)/shard_map/ppermute | solution.py:945
  469.1 30.4 %all-to-all-start.12 = ((bf16[8,24,2048]{2,1,0:T(8,128)(2,1)}), bf16[8,24,2048]{2,1,0:T(8,128)(2,1)S(1)}, u32[]{:S(2)}, u32[]{:S(2)}) async-start(bf16[8,24,2048]{2,1,0:T(8,128)(2,1)} %bitcast.64), calls=%async_computation.12 | async-start | bytes 1572864 | tf_op jit(solution)/shard_map/all_to_all | solution.py:1020
  476.5 21.8 %collective-permute-start.69 = (bf16[8,64,768]{2,1,0:T(8,128)(2,1)S(1)}, bf16[8,64,768]{2,1,0:T(8,128)(2,1)S(1)}, u32[]{:S(2)}, u32[]{:S(2)}) collective-permute-start(bf16[8,64,768]{2,1,0:T(8,128)(2,1)S(1)} %slice.336), channel_id=1, source_target_pairs={{0,1},{1,0},{2,3},{3,2},{4,5},{5,4},{6,7},{7,6},{8,9},{9,8},{10,11... | collective-permute-start | bytes 2359304 | tf_op jit(solution)/shard_map/ppermute | solution.py:945
  493.9 31.4 %collective-permute-start.73 = (bf16[384,2048]{1,0:T(8,128)(2,1)}, bf16[384,2048]{1,0:T(8,128)(2,1)}, u32[]{:S(2)}, u32[]{:S(2)}) collective-permute-start(bf16[384,2048]{1,0:T(8,128)(2,1)} %get-tuple-element.216), channel_id=1, source_target_pairs={{0,2},{2,0},{1,3},{3,1},{4,6},{6,4},{5,7},{7,5},{8,10},{10,8},{9,1... | collective-permute-start | bytes 4718600 | tf_op jit(solution)/shard_map/ppermute | solution.py:945
  497.3 127.8 %collective-permute-start.76 = (bf16[192,768]{1,0:T(8,128)(2,1)}, bf16[192,768]{1,0:T(8,128)(2,1)}, u32[]{:S(2)}, u32[]{:S(2)}) collective-permute-start(bf16[192,768]{1,0:T(8,128)(2,1)} %slice.343), channel_id=1, source_target_pairs={{0,1},{1,0},{2,3},{3,2},{4,5},{5,4},{6,7},{7,6},{8,9},{9,8},{10,11... | collective-permute-start | bytes 884744 | tf_op jit(solution)/shard_map/ppermute | solution.py:945
  499.4 54.6 %collective-permute-start.71 = (bf16[384,2048]{1,0:T(8,128)(2,1)}, bf16[384,2048]{1,0:T(8,128)(2,1)}, u32[]{:S(2)}, u32[]{:S(2)}) collective-permute-start(bf16[384,2048]{1,0:T(8,128)(2,1)} %get-tuple-element.214), channel_id=1, source_target_pairs={{0,2},{2,0},{1,3},{3,1},{4,6},{6,4},{5,7},{7,5},{8,10},{10,8},{9,1... | collective-permute-start | bytes 4718600 | tf_op jit(solution)/shard_map/ppermute | solution.py:945
  510.6 69.0 %collective-permute-start.67 = (bf16[192,2432]{1,0:T(8,128)(2,1)}, bf16[192,2432]{1,0:T(8,128)(2,1)}, u32[]{:S(2)}, u32[]{:S(2)}) collective-permute-start(bf16[192,2432]{1,0:T(8,128)(2,1)} %slice.334), channel_id=1, source_target_pairs={{0,1},{1,0},{2,3},{3,2},{4,5},{5,4},{6,7},{7,6},{8,9},{9,8},{10,11... | collective-permute-start | bytes 2801672 | tf_op jit(solution)/shard_map/ppermute | solution.py:945
  569.3 35.8 %collective-permute-start.74 = (bf16[192,2048]{1,0:T(8,128)(2,1)}, bf16[192,2048]{1,0:T(8,128)(2,1)}, u32[]{:S(2)}, u32[]{:S(2)}) collective-permute-start(bf16[192,2048]{1,0:T(8,128)(2,1)} %slice.340), channel_id=1, source_target_pairs={{0,1},{1,0},{2,3},{3,2},{4,5},{5,4},{6,7},{7,6},{8,9},{9,8},{10,11... | collective-permute-start | bytes 2359304 | tf_op jit(solution)/shard_map/ppermute | solution.py:945
  574.6 25.8 %all-to-all-start.14 = ((bf16[8,64,768]{2,1,0:T(8,128)(2,1)}), bf16[8,64,768]{2,1,0:T(8,128)(2,1)}, u32[]{:S(2)}, u32[]{:S(2)}) async-start(bf16[8,64,768]{2,1,0:T(8,128)(2,1)} %add_convert_fusion.11), calls=%async_computation.14 | async-start | bytes 1572864 | tf_op jit(solution)/shard_map/all_to_all | solution.py:1020
  582.1 44.8 %collective-permute-start.77 = (bf16[8,128,768]{2,1,0:T(8,128)(2,1)}, bf16[8,128,768]{2,1,0:T(8,128)(2,1)}, u32[]{:S(2)}, u32[]{:S(2)}) collective-permute-start(bf16[8,128,768]{2,1,0:T(8,128)(2,1)} %get-tuple-element.224), channel_id=1, source_target_pairs={{0,2},{2,0},{1,3},{3,1},{4,6},{6,4},{5,7},{7,5},{8,10},{10,8},{9,1... | collective-permute-start | bytes 4718600 | tf_op jit(solution)/shard_map/ppermute | solution.py:945
  582.7 23.9 %collective-permute-start.72 = (bf16[192,2048]{1,0:T(8,128)(2,1)}, bf16[192,2048]{1,0:T(8,128)(2,1)}, u32[]{:S(2)}, u32[]{:S(2)}) collective-permute-start(bf16[192,2048]{1,0:T(8,128)(2,1)} %slice.338), channel_id=1, source_target_pairs={{0,1},{1,0},{2,3},{3,2},{4,5},{5,4},{6,7},{7,6},{8,9},{9,8},{10,11... | collective-permute-start | bytes 2359304 | tf_op jit(solution)/shard_map/ppermute | solution.py:945
  583.7 47.4 %collective-permute-start.79 = (bf16[384,768]{1,0:T(8,128)(2,1)}, bf16[384,768]{1,0:T(8,128)(2,1)}, u32[]{:S(2)}, u32[]{:S(2)}) collective-permute-start(bf16[384,768]{1,0:T(8,128)(2,1)} %get-tuple-element.227), channel_id=1, source_target_pairs={{0,2},{2,0},{1,3},{3,1},{4,6},{6,4},{5,7},{7,5},{8,10},{10,8},{9,1... | collective-permute-start | bytes 1769480 | tf_op jit(solution)/shard_map/ppermute | solution.py:945
  620.7 43.7 %all-to-all-start.16 = ((bf16[8,24,4096]{2,1,0:T(8,128)(2,1)}), bf16[8,24,4096]{2,1,0:T(8,128)(2,1)S(1)}, u32[]{:S(2)}, u32[]{:S(2)}) async-start(bf16[8,24,4096]{2,1,0:T(8,128)(2,1)} %pad_maximum_fusion), calls=%async_computation.16 | async-start | bytes 3145728 | tf_op jit(solution)/shard_map/all_to_all | solution.py:1020
  625.1 103.5 %reduce-scatter.4.cloned.1.call-start = ((), (), s32[]{:S(2)}) async-start(), calls=%async_computation.22 | async-start | bytes 1382400
  630.1 40.1 %collective-permute-start.78 = (bf16[8,64,768]{2,1,0:T(8,128)(2,1)}, bf16[8,64,768]{2,1,0:T(8,128)(2,1)}, u32[]{:S(2)}, u32[]{:S(2)}) collective-permute-start(bf16[8,64,768]{2,1,0:T(8,128)(2,1)} %slice.345), channel_id=1, source_target_pairs={{0,1},{1,0},{2,3},{3,2},{4,5},{5,4},{6,7},{7,6},{8,9},{9,8},{10,11... | collective-permute-start | bytes 2359304 | tf_op jit(solution)/shard_map/ppermute | solution.py:945
  633.9 37.7 %collective-permute-start.80 = (bf16[192,768]{1,0:T(8,128)(2,1)}, bf16[192,768]{1,0:T(8,128)(2,1)}, u32[]{:S(2)}, u32[]{:S(2)}) collective-permute-start(bf16[192,768]{1,0:T(8,128)(2,1)} %slice.347), channel_id=1, source_target_pairs={{0,1},{1,0},{2,3},{3,2},{4,5},{5,4},{6,7},{7,6},{8,9},{9,8},{10,11... | collective-permute-start | bytes 884744 | tf_op jit(solution)/shard_map/ppermute | solution.py:945
  683.6 44.9 %all-to-all-start.18 = ((bf16[8,88,768]{2,1,0:T(8,128)(2,1)}), bf16[8,88,768]{2,1,0:T(8,128)(2,1)S(1)}, u32[]{:S(2)}, u32[]{:S(2)}) async-start(bf16[8,88,768]{2,1,0:T(8,128)(2,1)} %pad_maximum_fusion.2), calls=%async_computation.18 | async-start | bytes 2162688 | tf_op jit(solution)/shard_map/all_to_all | solution.py:1020
  (144 other events, 1456.6 us)
Sparse Core Ops, SparseCore 0:
  17.4 90.4 all-gather.2
  135.1 84.6 all-gather.4
  654.7 73.7 reduce-scatter.3

commit v5 on v4

--- a/solution.py
+++ b/solution.py
@@ -889,7 +889,7 @@
     "cj_g1": ("", ""),
     "cj_u1": ("", ""),
     "cj_d1": ("", ""),
-    "xj_g1": ("", "sall1"),
+    "xj_g1": ("", ""),
     "xj_u1": ("", ""),
     "xj_d1": ("", ""),
     "p_o1": ("slot0", ""),

time: 759 us -> 759 us (level)
  no operation moved by 1% of the time
where the time goes in v5:
time: 759 us; the launch traced here: 747 us
  waiting for transfers between devices  212 us (28%)
  Pallas kernels  199 us (26%)
  starting transfers between devices  156 us (21%)
  local copies, waits for them, and re-layouts  88.3 us (12%)
  other arithmetic  65.8 us (9%)
  between operations  15.9 us (2%)
  matrix products  10.5 us (1%)
    all_to_all x17, waiting for transfers between devices, deal_out(): return lax.all_to_all(x, ex_axes, 0, 0, tiled=True)  102 us
    all_to_all x17, starting transfers between devices, deal_out(): return lax.all_to_all(x, ex_axes, 0, 0, tiled=True)  78.8 us
    ppermute x69, starting transfers between devices, swap(): return lax.ppermute(x, axis, [(0, 1), (1, 0)])  47.5 us
    ppermute x69, waiting for transfers between devices, swap(): return lax.ppermute(x, axis, [(0, 1), (1, 0)])  44.7 us
    pallas_call x2, Pallas kernels, run_expert_back(): pl.pallas_call(functools.partial(expert_back_kernel, both), grid=(EXPERTS...  34.9 us
    pallas_call x2, Pallas kernels, project(): pl.pallas_call(functools.partial(project_kernel, 2 * SPLIT, len(blocks),...  34.2 us
    pallas_call x8, Pallas kernels, run_fused(): pl.pallas_call(kernel, grid=(1,), in_specs=specs, out_specs=[pl.BlockSpec...  33.6 us
    unnamed x206, local copies, waits for them, and re-layouts  33.1 us
  transfers between devices with their start and end apart: 103, of which 35 were waited for; matrix products, arithmetic and copies ran while one was open for 17% of the time, Pallas kernels for 24%

profile of v5, /device:TPU:0, one launch (start us, length us, event | category | flops | bytes accessed | tf_op | source)
XLA Modules:
  0.0 746.6 jit_solution(978737875751309574)
XLA Ops:
  35.6 5.6 fusion.13
  42.5 25.3 %all-to-all-done.1 = bf16[8,24,2048]{2,1,0:T(8,128)(2,1)S(1)} async-done(((bf16[8,24,2048]{2,1,0:T(8,128)(2,1)}), bf16[8,24,2048]{2,1,0:T(8,128)(2,1)S(1)}, u32[]{:S(2)}, u32[]{:S(2)}) %all-to-all-start.1) | async-done | bytes 786464 | tf_op jit(solution)/shard_map/all_to_all | solution.py:1020
  85.5 5.6 collective-permute-done.3
  91.8 8.9 %all-to-all-done = bf16[8,24,2048]{2,1,0:T(8,128)(2,1)S(1)} async-done(((bf16[8,24,2048]{2,1,0:T(8,128)(2,1)}), bf16[8,24,2048]{2,1,0:T(8,128)(2,1)S(1)}, u32[]{:S(2)}, u32[]{:S(2)}) %all-to-all-start) | async-done | bytes 786464 | tf_op jit(solution)/shard_map/all_to_all | solution.py:1020
  100.8 5.3 all-to-all-start.2
  117.2 17.7 %shard_map.265.q_ref.k_ref.v_ref = bf16[2048,2304]{1,0:T(8,128)(2,1)} custom-call(bf16[256,768]{1,0:T(8,128)(2,1)} %copy-done.31, bf16[256,768]{1,0:T(8,128)(2,1)} %collective-permute-done.1.refs_1_, bf16[256,768]{1,0:T(8,128)(2,1)} %constant_dynamic-update-slice_fusion.refs_2_, bf16[256,768]{1,0:T(8,128)(2,1)} %collective-permute-done.4.refs_3_, ...), custom_call_target="tpu_custom_call" | custom-call | flops 7247757312 | bytes 16121856 | tf_op jit(solution)/shard_map/pallas_call | solution.py:119
  135.0 6.1 all-to-all-start.3
  146.6 10.1 %shard_map.266 = (f32[128,768]{1,0:T(8,128)}, f32[128,128]{1,0:T(8,128)}) custom-call(bf16[2048,2304]{1,0:T(8,128)(2,1)} %shard_map.265.q_ref.k_ref.v_ref, bf16[2048,2304]{1,0:T(8,128)(2,1)} %shard_map.265.q_ref.k_ref.v_ref, bf16[2048,2304]{1,0:T(8,128)(2,1)} %shard_map.265.q_ref.k_ref.v_ref, s32[128,1]{1,0:T(8,128)} %broadcast_in_dim.105.at_ref.refs_16_, ...), custom_call_target="tpu_custom_call" | custom-call | flops 1610612736 | bytes 6291456 | tf_op jit(solution)/shard_map/pallas_call | solution.py:188
  168.4 16.0 %all-to-all-done.4 = bf16[8,32,768]{2,1,0:T(8,128)(2,1)S(1)} async-done(((bf16[8,32,768]{2,1,0:T(8,128)(2,1)}), bf16[8,32,768]{2,1,0:T(8,128)(2,1)S(1)}, u32[]{:S(2)}, u32[]{:S(2)}) %all-to-all-start.4) | async-done | bytes 393248 | tf_op jit(solution)/shard_map/all_to_all | solution.py:1020
  184.4 4.5 all-to-all-start.5
  197.6 11.2 %shard_map.268 = (f32[256,2048]{1,0:T(8,128)}, f32[256,2048]{1,0:T(8,128)}, bf16[256,768]{1,0:T(8,128)(2,1)}) custom-call(s32[1,2]{1,0:T(1,128)} %add_bitcast_fusion.flag_ref, bf16[256,768]{1,0:T(8,128)(2,1)} %bitcast.186, bf16[192,2048]{1,0:T(8,128)(2,1)} %bitcast.167, bf16[192,2048]{1,0:T(8,128)(2,1)} %collective-permute-done.11.refs_1_.refs_3_, ...), custom_call_target="tpu_custom_call" | custom-call | flops 2415919104 | bytes 13631488 | tf_op jit(solution)/shard_map/pallas_call | solution.py:422
  208.8 10.8 %all-to-all-done.5 = bf16[8,24,2048]{2,1,0:T(8,128)(2,1)} async-done(((bf16[8,24,2048]{2,1,0:T(8,128)(2,1)}), bf16[8,24,2048]{2,1,0:T(8,128)(2,1)}, u32[]{:S(2)}, u32[]{:S(2)}) %all-to-all-start.5) | async-done | bytes 786464 | tf_op jit(solution)/shard_map/all_to_all | solution.py:1020
  223.9 11.0 %all-to-all-done.6 = bf16[8,32,768]{2,1,0:T(8,128)(2,1)S(1)} async-done(((bf16[8,32,768]{2,1,0:T(8,128)(2,1)}), bf16[8,32,768]{2,1,0:T(8,128)(2,1)S(1)}, u32[]{:S(2)}, u32[]{:S(2)}) %all-to-all-start.6) | async-done | bytes 393248 | tf_op jit(solution)/shard_map/all_to_all | solution.py:1020
  257.9 4.5 collective-permute-done.25
  273.0 16.4 %shard_map.270.q_ref.k_ref.v_ref = bf16[2048,2304]{1,0:T(8,128)(2,1)} custom-call(bf16[256,768]{1,0:T(8,128)(2,1)} %copy-done.67, bf16[256,768]{1,0:T(8,128)(2,1)} %collective-permute-done.21.refs_1_, bf16[256,768]{1,0:T(8,128)(2,1)} %copy-done.65, bf16[256,768]{1,0:T(8,128)(2,1)} %copy-done.87, bf16[256,768]{1,0:T(8,128)(2,1)} %copy-done.64, ...), custom_call_target="tpu_custom_call" | custom-call | flops 7247757312 | bytes 16121856 | tf_op jit(solution)/shard_map/pallas_call | solution.py:119
  289.4 10.1 %shard_map.271 = (f32[128,768]{1,0:T(8,128)}, f32[128,128]{1,0:T(8,128)}) custom-call(bf16[2048,2304]{1,0:T(8,128)(2,1)} %shard_map.270.q_ref.k_ref.v_ref, bf16[2048,2304]{1,0:T(8,128)(2,1)} %shard_map.270.q_ref.k_ref.v_ref, bf16[2048,2304]{1,0:T(8,128)(2,1)} %shard_map.270.q_ref.k_ref.v_ref, s32[128,1]{1,0:T(8,128)} %broadcast_in_dim.105.at_ref.refs_16_, ...), custom_call_target="tpu_custom_call" | custom-call | flops 1610612736 | bytes 6291456 | tf_op jit(solution)/shard_map/pallas_call | solution.py:188
  304.9 6.1 all-to-all-start.8
  312.0 7.2 collective-permute-done.37.refs_9_
  320.2 10.9 %all-to-all-done.8 = bf16[8,32,1536]{2,1,0:T(8,128)(2,1)S(1)} async-done(((bf16[8,32,1536]{2,1,0:T(8,128)(2,1)}), bf16[8,32,1536]{2,1,0:T(8,128)(2,1)S(1)}, u32[]{:S(2)}, u32[]{:S(2)}) %all-to-all-start.8) | async-done | bytes 786464 | tf_op jit(solution)/shard_map/all_to_all | solution.py:1020
  332.0 18.7 %shard_map.273 = (bf16[384,2048]{1,0:T(8,128)(2,1)}, bf16[384,2048]{1,0:T(8,128)(2,1)}, bf16[384,2048]{1,0:T(8,128)(2,1)}, bf16[384,2048]{1,0:T(8,128)(2,1)}, bf...) custom-call(s32[1,2]{1,0:T(1,128)} %add_bitcast_fusion.flag_ref, ...), custom_call_target="tpu_custom_call" | custom-call | flops 7247757312 | bytes 23068672 | tf_op jit(solution)/shard_map/pallas_call | solution.py:519
  356.2 4.8 shard_map.289
  361.0 4.7 copy.251
  368.7 6.3 all-to-all-done.9
  376.6 5.1 shard_map.274
  392.5 4.6 shard_map.276.refs_0_
  397.2 4.6 shard_map.277.refs_1_
  405.3 4.6 shard_map.278.refs_2_
  410.0 7.6 %collective-permute-done.49 = bf16[128,896]{1,0:T(8,128)(2,1)S(1)} collective-permute-done((bf16[128,896]{1,0:T(8,128)(2,1)S(1)}, bf16[128,896]{1,0:T(8,128)(2,1)S(1)}, u32[]{:S(2)}, u32[]{:S(2)}) %collective-permute-start.49) | collective-permute-done | bytes 229408 | tf_op jit(solution)/shard_map/ppermute | solution.py:945
  434.1 11.4 %shard_map.279 = (bf16[128,768]{1,0:T(8,128)(2,1)}, bf16[128,768]{1,0:T(8,128)(2,1)}) custom-call(bf16[2048,2304]{1,0:T(8,128)(2,1)} %shard_map.270.q_ref.k_ref.v_ref, bf16[2048,2304]{1,0:T(8,128)(2,1)} %shard_map.270.q_ref.k_ref.v_ref, bf16[2048,2304]{1,0:T(8,128)(2,1)} %shard_map.270.q_ref.k_ref.v_ref, ...), custom_call_target="tpu_custom_call" | custom-call | flops 3221225472 | bytes 6291456 | tf_op jit(solution)/shard_map/pallas_call | solution.py:346
  445.8 5.4 shard_map.280
  451.2 5.8 all-to-all-start.11
  469.1 5.0 all-to-all-start.12
  477.6 16.3 %shard_map.281 = (bf16[384,2048]{1,0:T(8,128)(2,1)}, bf16[384,2048]{1,0:T(8,128)(2,1)}, bf16[384,2048]{1,0:T(8,128)(2,1)}, bf16[384,2048]{1,0:T(8,128)(2,1)}, bf...) custom-call(s32[1,2]{1,0:T(1,128)} %add_bitcast_fusion.flag_ref, ...), custom_call_target="tpu_custom_call" | custom-call | flops 4831838208 | bytes 23068672 | tf_op jit(solution)/shard_map/pallas_call | solution.py:519
  499.6 6.2 all-to-all-start.13
  511.6 6.3 all-to-all-done.13
  518.7 5.1 shard_map.282
  533.4 4.6 shard_map.283.refs_0_
  543.2 4.6 shard_map.284.refs_1_
  547.8 4.7 shard_map.285.refs_2_
  574.6 5.0 all-to-all-start.14
  584.5 11.4 %shard_map.286 = (bf16[128,768]{1,0:T(8,128)(2,1)}, bf16[128,768]{1,0:T(8,128)(2,1)}) custom-call(bf16[2048,2304]{1,0:T(8,128)(2,1)} %shard_map.265.q_ref.k_ref.v_ref, bf16[2048,2304]{1,0:T(8,128)(2,1)} %shard_map.265.q_ref.k_ref.v_ref, bf16[2048,2304]{1,0:T(8,128)(2,1)} %shard_map.265.q_ref.k_ref.v_ref, ...), custom_call_target="tpu_custom_call" | custom-call | flops 3221225472 | bytes 6291456 | tf_op jit(solution)/shard_map/pallas_call | solution.py:346
  600.4 4.7 all-to-all-start.15
  609.2 11.5 %all-to-all-done.15 = bf16[16,128,144]{1,2,0:T(8,128)(2,1)} async-done(((bf16[16,128,144]{1,2,0:T(8,128)(2,1)}), bf16[16,128,144]{1,2,0:T(8,128)(2,1)}, u32[]{:S(2)}, u32[]{:S(2)}) %all-to-all-start.15) | async-done | bytes 589856 | tf_op jit(solution)/shard_map/all_to_all | solution.py:1478
  635.0 4.7 shard_map.288
  654.6 7.9 %collective-permute-done.70 = bf16[16,24,272]{2,1,0:T(8,128)(2,1)} collective-permute-done((bf16[16,24,272]{2,1,0:T(8,128)(2,1)}, bf16[16,24,272]{2,1,0:T(8,128)(2,1)}, u32[]{:S(2)}, u32[]{:S(2)}) %collective-permute-start.70) | collective-permute-done | bytes 208928 | tf_op jit(solution)/shard_map/ppermute | solution.py:945
  664.4 5.8 all-to-all-start.17
  673.7 9.9 %all-to-all-done.17 = bf16[16,24,272]{2,1,0:T(8,128)(2,1)S(1)} async-done(((bf16[16,24,272]{2,1,0:T(8,128)(2,1)}), bf16[16,24,272]{2,1,0:T(8,128)(2,1)S(1)}, u32[]{:S(2)}, u32[]{:S(2)}) %all-to-all-start.17) | async-done | bytes 208928 | tf_op jit(solution)/shard_map/all_to_all | solution.py:1484
  696.6 31.9 %reduce-scatter.4.cloned.1.call-done = bf16[24,3200]{1,0:T(8,128)(2,1)} async-done(((bf16[192,3200]{1,0:T(8,128)(2,1)}), bf16[24,3200]{1,0:T(8,128)(2,1)}) %reduce-scatter.4.cloned.1.call-update) | async-done | bytes 153616 | tf_op jit(solution)/shard_map/optimization_barrier | solution.py:866
  (563 shorter events, 308.0 us)
Async XLA Ops:
  7.2 103.0 %all-gather.3.cloned.1.call-start = ((), (), s32[]{:S(2)}) async-start(), calls=%async_computation.20 | async-start | bytes 5068800 | tf_op jit(solution)/shard_map/all_gather | solution.py:1045
  17.2 57.3 %collective-permute-start = (bf16[128,768]{1,0:T(8,128)(2,1)}, bf16[128,768]{1,0:T(8,128)(2,1)}, u32[]{:S(2)}, u32[]{:S(2)}) collective-permute-start(bf16[128,768]{1,0:T(8,128)(2,1)} %bitcast.197), channel_id=1, source_target_pairs={{0,4},{4,0},{1,5},{5,1},{2,6},{6,2},{3,7},{7,3},{8,12},{12,8},{9,1... | collective-permute-start | bytes 589832 | tf_op jit(solution)/shard_map/ppermute | solution.py:945
  20.3 55.4 %collective-permute-start.2 = (bf16[128,768]{1,0:T(8,128)(2,1)}, bf16[128,768]{1,0:T(8,128)(2,1)}, u32[]{:S(2)}, u32[]{:S(2)}) collective-permute-start(bf16[128,768]{1,0:T(8,128)(2,1)} %bitcast.198), channel_id=1, source_target_pairs={{0,8},{8,16},{16,24},{24,0},{1,9},{9,17},{17,25},{25,1},{2,10},{10... | collective-permute-start | bytes 589832 | tf_op jit(solution)/shard_map/ppermute | solution.py:960
  21.8 55.7 %collective-permute-start.5 = (bf16[128,768]{1,0:T(8,128)(2,1)}, bf16[128,768]{1,0:T(8,128)(2,1)}, u32[]{:S(2)}, u32[]{:S(2)}) collective-permute-start(bf16[128,768]{1,0:T(8,128)(2,1)} %bitcast.199), channel_id=1, source_target_pairs={{0,16},{8,24},{16,0},{24,8},{1,17},{9,25},{17,1},{25,9},{2,18},{10... | collective-permute-start | bytes 589832 | tf_op jit(solution)/shard_map/ppermute | solution.py:960
  24.4 53.3 %collective-permute-start.8 = (bf16[128,768]{1,0:T(8,128)(2,1)}, bf16[128,768]{1,0:T(8,128)(2,1)}, u32[]{:S(2)}, u32[]{:S(2)}) collective-permute-start(bf16[128,768]{1,0:T(8,128)(2,1)} %bitcast.200), channel_id=1, source_target_pairs={{0,24},{8,0},{16,8},{24,16},{1,25},{9,1},{17,9},{25,17},{2,26},{10... | collective-permute-start | bytes 589832 | tf_op jit(solution)/shard_map/ppermute | solution.py:960
  28.5 39.3 %all-to-all-start.1 = ((bf16[8,24,2048]{2,1,0:T(8,128)(2,1)}), bf16[8,24,2048]{2,1,0:T(8,128)(2,1)S(1)}, u32[]{:S(2)}, u32[]{:S(2)}) async-start(bf16[8,24,2048]{2,1,0:T(8,128)(2,1)} %get-tuple-element.313), calls=%async_computation.1 | async-start | bytes 1572864 | tf_op jit(solution)/shard_map/all_to_all | solution.py:1020
  67.8 32.9 %all-to-all-start = ((bf16[8,24,2048]{2,1,0:T(8,128)(2,1)}), bf16[8,24,2048]{2,1,0:T(8,128)(2,1)S(1)}, u32[]{:S(2)}, u32[]{:S(2)}) async-start(bf16[8,24,2048]{2,1,0:T(8,128)(2,1)} %get-tuple-element.121), calls=%async_computation | async-start | bytes 1572864 | tf_op jit(solution)/shard_map/all_to_all | solution.py:1020
  75.5 34.3 %collective-permute-start.1 = (bf16[256,768]{1,0:T(8,128)(2,1)S(1)}, bf16[256,768]{1,0:T(8,128)(2,1)}, u32[]{:S(2)}, u32[]{:S(2)}) collective-permute-start(bf16[256,768]{1,0:T(8,128)(2,1)S(1)} %pad_maximum_fusion.4.refs_0_), channel_id=1, source_target_pairs={{0,2},{2,0},{1,3},{3,1},{4,6},{6,4},{5,7},{7,5},{8,10},{10,8},{9,1... | collective-permute-start | bytes 1179656 | tf_op jit(solution)/shard_map/ppermute | solution.py:945
  77.6 28.5 %collective-permute-start.6 = (bf16[128,768]{1,0:T(8,128)(2,1)}, bf16[128,768]{1,0:T(8,128)(2,1)}, u32[]{:S(2)}, u32[]{:S(2)}) collective-permute-start(bf16[128,768]{1,0:T(8,128)(2,1)} %collective-permute-done.5), channel_id=1, source_target_pairs={{0,4},{4,0},{1,5},{5,1},{2,6},{6,2},{3,7},{7,3},{8,12},{12,8},{9,1... | collective-permute-start | bytes 589832 | tf_op jit(solution)/shard_map/ppermute | solution.py:945
  77.7 30.0 %collective-permute-start.9 = (bf16[128,768]{1,0:T(8,128)(2,1)}, bf16[128,768]{1,0:T(8,128)(2,1)S(1)}, u32[]{:S(2)}, u32[]{:S(2)}) collective-permute-start(bf16[128,768]{1,0:T(8,128)(2,1)} %collective-permute-done.8), channel_id=1, source_target_pairs={{0,4},{4,0},{1,5},{5,1},{2,6},{6,2},{3,7},{7,3},{8,12},{12,8},{9,1... | collective-permute-start | bytes 589832 | tf_op jit(solution)/shard_map/ppermute | solution.py:945
  83.8 26.4 %collective-permute-start.11 = (bf16[192,2048]{1,0:T(8,128)(2,1)S(1)}, bf16[192,2048]{1,0:T(8,128)(2,1)}, u32[]{:S(2)}, u32[]{:S(2)}) collective-permute-start(bf16[192,2048]{1,0:T(8,128)(2,1)S(1)} %bitcast.165), channel_id=1, source_target_pairs={{0,1},{1,0},{2,3},{3,2},{4,5},{5,4},{6,7},{7,6},{8,9},{9,8},{10,11... | collective-permute-start | bytes 2359304 | tf_op jit(solution)/shard_map/ppermute | solution.py:945
  100.8 34.2 %all-to-all-start.2 = ((bf16[8,64,768]{2,1,0:T(8,128)(2,1)}), bf16[8,64,768]{2,1,0:T(8,128)(2,1)S(1)}, u32[]{:S(2)}, u32[]{:S(2)}) async-start(bf16[8,64,768]{2,1,0:T(8,128)(2,1)} %get-tuple-element.309), calls=%async_computation.2 | async-start | bytes 1572864 | tf_op jit(solution)/shard_map/all_to_all | solution.py:1020
  106.1 117.8 %all-gather.5.cloned.1.call-start = ((), (), s32[]{:S(2)}) async-start(), calls=%async_computation.21 | async-start | bytes 5068800 | tf_op jit(solution)/shard_map/all_gather | solution.py:1045
  110.2 24.8 %collective-permute-start.12 = (bf16[192,2048]{1,0:T(8,128)(2,1)S(1)}, bf16[192,2048]{1,0:T(8,128)(2,1)}, u32[]{:S(2)}, u32[]{:S(2)}) collective-permute-start(bf16[192,2048]{1,0:T(8,128)(2,1)S(1)} %bitcast.169), channel_id=1, source_target_pairs={{0,1},{1,0},{2,3},{3,2},{4,5},{5,4},{6,7},{7,6},{8,9},{9,8},{10,11... | collective-permute-start | bytes 2359304 | tf_op jit(solution)/shard_map/ppermute | solution.py:945
  135.0 29.7 %all-to-all-start.3 = ((bf16[8,24,2048]{2,1,0:T(8,128)(2,1)}), bf16[8,24,2048]{2,1,0:T(8,128)(2,1)}, u32[]{:S(2)}, u32[]{:S(2)}) async-start(bf16[8,24,2048]{2,1,0:T(8,128)(2,1)} %get-tuple-element.130), calls=%async_computation.3 | async-start | bytes 1572864 | tf_op jit(solution)/shard_map/all_to_all | solution.py:1020
  146.2 22.1 %collective-permute-start.13 = (bf16[512,768]{1,0:T(8,128)(2,1)S(1)}, bf16[512,768]{1,0:T(8,128)(2,1)S(1)}, u32[]{:S(2)}, u32[]{:S(2)}) collective-permute-start(bf16[512,768]{1,0:T(8,128)(2,1)S(1)} %bitcast.173), channel_id=1, source_target_pairs={{0,1},{1,0},{2,3},{3,2},{4,5},{5,4},{6,7},{7,6},{8,9},{9,8},{10,11... | collective-permute-start | bytes 2359304 | tf_op jit(solution)/shard_map/ppermute | solution.py:945
  184.4 35.2 %all-to-all-start.5 = ((bf16[8,24,2048]{2,1,0:T(8,128)(2,1)}), bf16[8,24,2048]{2,1,0:T(8,128)(2,1)}, u32[]{:S(2)}, u32[]{:S(2)}) async-start(bf16[8,24,2048]{2,1,0:T(8,128)(2,1)} %get-tuple-element.136), calls=%async_computation.5 | async-start | bytes 1572864 | tf_op jit(solution)/shard_map/all_to_all | solution.py:1020
  239.6 24.6 %collective-permute-start.31 = (bf16[192,2048]{1,0:T(8,128)(2,1)}, bf16[192,2048]{1,0:T(8,128)(2,1)S(1)}, u32[]{:S(2)}, u32[]{:S(2)}) collective-permute-start(bf16[192,2048]{1,0:T(8,128)(2,1)} %bitcast.39.refs_0_), channel_id=1, source_target_pairs={{0,1},{1,0},{2,3},{3,2},{4,5},{5,4},{6,7},{7,6},{8,9},{9,8},{10,11... | collective-permute-start | bytes 2359304 | tf_op jit(solution)/shard_map/ppermute | solution.py:945
  265.9 33.6 %all-to-all-start.7 = ((bf16[8,64,768]{2,1,0:T(8,128)(2,1)}), bf16[8,64,768]{2,1,0:T(8,128)(2,1)S(1)}, u32[]{:S(2)}, u32[]{:S(2)}) async-start(bf16[8,64,768]{2,1,0:T(8,128)(2,1)} %get-tuple-element.144), calls=%async_computation.7 | async-start | bytes 1572864 | tf_op jit(solution)/shard_map/all_to_all | solution.py:1020
  270.2 41.4 %collective-permute-start.33 = (bf16[192,2048]{1,0:T(8,128)(2,1)}, bf16[192,2048]{1,0:T(8,128)(2,1)}, u32[]{:S(2)}, u32[]{:S(2)}) collective-permute-start(bf16[192,2048]{1,0:T(8,128)(2,1)} %copy-done.83), channel_id=1, source_target_pairs={{0,2},{2,0},{1,3},{3,1},{4,6},{6,4},{5,7},{7,5},{8,10},{10,8},{9,1... | collective-permute-start | bytes 2359304 | tf_op jit(solution)/shard_map/ppermute | solution.py:945
  270.2 40.7 %collective-permute-start.34 = (bf16[192,2048]{1,0:T(8,128)(2,1)}, bf16[192,2048]{1,0:T(8,128)(2,1)}, u32[]{:S(2)}, u32[]{:S(2)}) collective-permute-start(bf16[192,2048]{1,0:T(8,128)(2,1)} %bitcast.43.refs_4_), channel_id=1, source_target_pairs={{0,1},{1,0},{2,3},{3,2},{4,5},{5,4},{6,7},{7,6},{8,9},{9,8},{10,11... | collective-permute-start | bytes 2359304 | tf_op jit(solution)/shard_map/ppermute | solution.py:945
  304.9 26.2 %all-to-all-start.8 = ((bf16[8,32,1536]{2,1,0:T(8,128)(2,1)}), bf16[8,32,1536]{2,1,0:T(8,128)(2,1)S(1)}, u32[]{:S(2)}, u32[]{:S(2)}) async-start(bf16[8,32,1536]{2,1,0:T(8,128)(2,1)} %bitcast.195), calls=%async_computation.8 | async-start | bytes 1572864 | tf_op jit(solution)/shard_map/all_to_all | solution.py:1020
  350.7 24.4 %all-to-all-start.9 = ((bf16[8,32,1536]{2,1,0:T(8,128)(2,1)}), bf16[8,32,1536]{2,1,0:T(8,128)(2,1)S(1)}, u32[]{:S(2)}, u32[]{:S(2)}) async-start(bf16[8,32,1536]{2,1,0:T(8,128)(2,1)} %bitcast.196), calls=%async_computation.9 | async-start | bytes 1572864 | tf_op jit(solution)/shard_map/all_to_all | solution.py:1020
  355.5 33.9 %collective-permute-start.51 = (bf16[384,2048]{1,0:T(8,128)(2,1)}, bf16[384,2048]{1,0:T(8,128)(2,1)S(1)}, u32[]{:S(2)}, u32[]{:S(2)}) collective-permute-start(bf16[384,2048]{1,0:T(8,128)(2,1)} %get-tuple-element.170), channel_id=1, source_target_pairs={{0,2},{2,0},{1,3},{3,1},{4,6},{6,4},{5,7},{7,5},{8,10},{10,8},{9,1... | collective-permute-start | bytes 4718600 | tf_op jit(solution)/shard_map/ppermute | solution.py:945
  368.2 57.7 %collective-permute-start.53 = (bf16[384,2048]{1,0:T(8,128)(2,1)}, bf16[384,2048]{1,0:T(8,128)(2,1)}, u32[]{:S(2)}, u32[]{:S(2)}) collective-permute-start(bf16[384,2048]{1,0:T(8,128)(2,1)} %get-tuple-element.181), channel_id=1, source_target_pairs={{0,2},{2,0},{1,3},{3,1},{4,6},{6,4},{5,7},{7,5},{8,10},{10,8},{9,1... | collective-permute-start | bytes 4718600 | tf_op jit(solution)/shard_map/ppermute | solution.py:945
  390.7 27.6 %collective-permute-start.52 = (bf16[192,2048]{1,0:T(8,128)(2,1)S(1)}, bf16[192,2048]{1,0:T(8,128)(2,1)S(1)}, u32[]{:S(2)}, u32[]{:S(2)}) collective-permute-start(bf16[192,2048]{1,0:T(8,128)(2,1)S(1)} %slice.330), channel_id=1, source_target_pairs={{0,1},{1,0},{2,3},{3,2},{4,5},{5,4},{6,7},{7,6},{8,9},{9,8},{10,11... | collective-permute-start | bytes 2359304 | tf_op jit(solution)/shard_map/ppermute | solution.py:945
  397.1 77.0 %collective-permute-start.68 = (bf16[8,128,768]{2,1,0:T(8,128)(2,1)}, bf16[8,128,768]{2,1,0:T(8,128)(2,1)}, u32[]{:S(2)}, u32[]{:S(2)}) collective-permute-start(bf16[8,128,768]{2,1,0:T(8,128)(2,1)} %get-tuple-element.205), channel_id=1, source_target_pairs={{0,2},{2,0},{1,3},{3,1},{4,6},{6,4},{5,7},{7,5},{8,10},{10,8},{9,1... | collective-permute-start | bytes 4718600 | tf_op jit(solution)/shard_map/ppermute | solution.py:945
  401.9 23.3 %collective-permute-start.45 = (bf16[128,896]{1,0:T(8,128)(2,1)S(1)}, bf16[128,896]{1,0:T(8,128)(2,1)S(1)}, u32[]{:S(2)}, u32[]{:S(2)}) collective-permute-start(bf16[128,896]{1,0:T(8,128)(2,1)S(1)} %collective-permute-done.44), channel_id=1, source_target_pairs={{0,4},{4,0},{1,5},{5,1},{2,6},{6,2},{3,7},{7,3},{8,12},{12,8},{9,1... | collective-permute-start | bytes 688136 | tf_op jit(solution)/shard_map/ppermute | solution.py:945
  420.9 74.3 %collective-permute-start.75 = (bf16[384,768]{1,0:T(8,128)(2,1)}, bf16[384,768]{1,0:T(8,128)(2,1)}, u32[]{:S(2)}, u32[]{:S(2)}) collective-permute-start(bf16[384,768]{1,0:T(8,128)(2,1)} %get-tuple-element.219), channel_id=1, source_target_pairs={{0,2},{2,0},{1,3},{3,1},{4,6},{6,4},{5,7},{7,5},{8,10},{10,8},{9,1... | collective-permute-start | bytes 1769480 | tf_op jit(solution)/shard_map/ppermute | solution.py:945
  421.1 24.7 %all-to-all-start.10 = ((bf16[8,24,2048]{2,1,0:T(8,128)(2,1)}), bf16[8,24,2048]{2,1,0:T(8,128)(2,1)S(1)}, u32[]{:S(2)}, u32[]{:S(2)}) async-start(bf16[8,24,2048]{2,1,0:T(8,128)(2,1)} %bitcast.61), calls=%async_computation.10 | async-start | bytes 1572864 | tf_op jit(solution)/shard_map/all_to_all | solution.py:1020
  431.5 34.3 %collective-permute-start.54 = (bf16[192,2048]{1,0:T(8,128)(2,1)}, bf16[192,2048]{1,0:T(8,128)(2,1)}, u32[]{:S(2)}, u32[]{:S(2)}) collective-permute-start(bf16[192,2048]{1,0:T(8,128)(2,1)} %slice.332), channel_id=1, source_target_pairs={{0,1},{1,0},{2,3},{3,2},{4,5},{5,4},{6,7},{7,6},{8,9},{9,8},{10,11... | collective-permute-start | bytes 2359304 | tf_op jit(solution)/shard_map/ppermute | solution.py:945
  465.8 40.0 %collective-permute-start.66 = (bf16[384,2432]{1,0:T(8,128)(2,1)}, bf16[384,2432]{1,0:T(8,128)(2,1)S(1)}, u32[]{:S(2)}, u32[]{:S(2)}) collective-permute-start(bf16[384,2432]{1,0:T(8,128)(2,1)} %get-tuple-element.199), channel_id=1, source_target_pairs={{0,2},{2,0},{1,3},{3,1},{4,6},{6,4},{5,7},{7,5},{8,10},{10,8},{9,1... | collective-permute-start | bytes 5603336 | tf_op jit(solution)/shard_map/ppermute | solution.py:945
  469.1 30.4 %all-to-all-start.12 = ((bf16[8,24,2048]{2,1,0:T(8,128)(2,1)}), bf16[8,24,2048]{2,1,0:T(8,128)(2,1)S(1)}, u32[]{:S(2)}, u32[]{:S(2)}) async-start(bf16[8,24,2048]{2,1,0:T(8,128)(2,1)} %bitcast.64), calls=%async_computation.12 | async-start | bytes 1572864 | tf_op jit(solution)/shard_map/all_to_all | solution.py:1020
  476.5 21.8 %collective-permute-start.69 = (bf16[8,64,768]{2,1,0:T(8,128)(2,1)S(1)}, bf16[8,64,768]{2,1,0:T(8,128)(2,1)S(1)}, u32[]{:S(2)}, u32[]{:S(2)}) collective-permute-start(bf16[8,64,768]{2,1,0:T(8,128)(2,1)S(1)} %slice.336), channel_id=1, source_target_pairs={{0,1},{1,0},{2,3},{3,2},{4,5},{5,4},{6,7},{7,6},{8,9},{9,8},{10,11... | collective-permute-start | bytes 2359304 | tf_op jit(solution)/shard_map/ppermute | solution.py:945
  493.9 31.4 %collective-permute-start.73 = (bf16[384,2048]{1,0:T(8,128)(2,1)}, bf16[384,2048]{1,0:T(8,128)(2,1)}, u32[]{:S(2)}, u32[]{:S(2)}) collective-permute-start(bf16[384,2048]{1,0:T(8,128)(2,1)} %get-tuple-element.214), channel_id=1, source_target_pairs={{0,2},{2,0},{1,3},{3,1},{4,6},{6,4},{5,7},{7,5},{8,10},{10,8},{9,1... | collective-permute-start | bytes 4718600 | tf_op jit(solution)/shard_map/ppermute | solution.py:945
  497.3 127.8 %collective-permute-start.76 = (bf16[192,768]{1,0:T(8,128)(2,1)}, bf16[192,768]{1,0:T(8,128)(2,1)}, u32[]{:S(2)}, u32[]{:S(2)}) collective-permute-start(bf16[192,768]{1,0:T(8,128)(2,1)} %slice.343), channel_id=1, source_target_pairs={{0,1},{1,0},{2,3},{3,2},{4,5},{5,4},{6,7},{7,6},{8,9},{9,8},{10,11... | collective-permute-start | bytes 884744 | tf_op jit(solution)/shard_map/ppermute | solution.py:945
  499.4 54.6 %collective-permute-start.71 = (bf16[384,2048]{1,0:T(8,128)(2,1)}, bf16[384,2048]{1,0:T(8,128)(2,1)}, u32[]{:S(2)}, u32[]{:S(2)}) collective-permute-start(bf16[384,2048]{1,0:T(8,128)(2,1)} %get-tuple-element.212), channel_id=1, source_target_pairs={{0,2},{2,0},{1,3},{3,1},{4,6},{6,4},{5,7},{7,5},{8,10},{10,8},{9,1... | collective-permute-start | bytes 4718600 | tf_op jit(solution)/shard_map/ppermute | solution.py:945
  510.6 69.0 %collective-permute-start.67 = (bf16[192,2432]{1,0:T(8,128)(2,1)}, bf16[192,2432]{1,0:T(8,128)(2,1)}, u32[]{:S(2)}, u32[]{:S(2)}) collective-permute-start(bf16[192,2432]{1,0:T(8,128)(2,1)} %slice.334), channel_id=1, source_target_pairs={{0,1},{1,0},{2,3},{3,2},{4,5},{5,4},{6,7},{7,6},{8,9},{9,8},{10,11... | collective-permute-start | bytes 2801672 | tf_op jit(solution)/shard_map/ppermute | solution.py:945
  569.3 35.8 %collective-permute-start.74 = (bf16[192,2048]{1,0:T(8,128)(2,1)}, bf16[192,2048]{1,0:T(8,128)(2,1)}, u32[]{:S(2)}, u32[]{:S(2)}) collective-permute-start(bf16[192,2048]{1,0:T(8,128)(2,1)} %slice.340), channel_id=1, source_target_pairs={{0,1},{1,0},{2,3},{3,2},{4,5},{5,4},{6,7},{7,6},{8,9},{9,8},{10,11... | collective-permute-start | bytes 2359304 | tf_op jit(solution)/shard_map/ppermute | solution.py:945
  574.6 25.8 %all-to-all-start.14 = ((bf16[8,64,768]{2,1,0:T(8,128)(2,1)}), bf16[8,64,768]{2,1,0:T(8,128)(2,1)}, u32[]{:S(2)}, u32[]{:S(2)}) async-start(bf16[8,64,768]{2,1,0:T(8,128)(2,1)} %add_convert_fusion.11), calls=%async_computation.14 | async-start | bytes 1572864 | tf_op jit(solution)/shard_map/all_to_all | solution.py:1020
  582.1 44.8 %collective-permute-start.77 = (bf16[8,128,768]{2,1,0:T(8,128)(2,1)}, bf16[8,128,768]{2,1,0:T(8,128)(2,1)}, u32[]{:S(2)}, u32[]{:S(2)}) collective-permute-start(bf16[8,128,768]{2,1,0:T(8,128)(2,1)} %get-tuple-element.222), channel_id=1, source_target_pairs={{0,2},{2,0},{1,3},{3,1},{4,6},{6,4},{5,7},{7,5},{8,10},{10,8},{9,1... | collective-permute-start | bytes 4718600 | tf_op jit(solution)/shard_map/ppermute | solution.py:945
  582.7 23.9 %collective-permute-start.72 = (bf16[192,2048]{1,0:T(8,128)(2,1)}, bf16[192,2048]{1,0:T(8,128)(2,1)}, u32[]{:S(2)}, u32[]{:S(2)}) collective-permute-start(bf16[192,2048]{1,0:T(8,128)(2,1)} %slice.338), channel_id=1, source_target_pairs={{0,1},{1,0},{2,3},{3,2},{4,5},{5,4},{6,7},{7,6},{8,9},{9,8},{10,11... | collective-permute-start | bytes 2359304 | tf_op jit(solution)/shard_map/ppermute | solution.py:945
  583.7 47.4 %collective-permute-start.79 = (bf16[384,768]{1,0:T(8,128)(2,1)}, bf16[384,768]{1,0:T(8,128)(2,1)}, u32[]{:S(2)}, u32[]{:S(2)}) collective-permute-start(bf16[384,768]{1,0:T(8,128)(2,1)} %get-tuple-element.225), channel_id=1, source_target_pairs={{0,2},{2,0},{1,3},{3,1},{4,6},{6,4},{5,7},{7,5},{8,10},{10,8},{9,1... | collective-permute-start | bytes 1769480 | tf_op jit(solution)/shard_map/ppermute | solution.py:945
  620.7 43.7 %all-to-all-start.16 = ((bf16[8,24,4096]{2,1,0:T(8,128)(2,1)}), bf16[8,24,4096]{2,1,0:T(8,128)(2,1)S(1)}, u32[]{:S(2)}, u32[]{:S(2)}) async-start(bf16[8,24,4096]{2,1,0:T(8,128)(2,1)} %pad_maximum_fusion), calls=%async_computation.16 | async-start | bytes 3145728 | tf_op jit(solution)/shard_map/all_to_all | solution.py:1020
  625.1 103.5 %reduce-scatter.4.cloned.1.call-start = ((), (), s32[]{:S(2)}) async-start(), calls=%async_computation.22 | async-start | bytes 1382400
  630.1 40.1 %collective-permute-start.78 = (bf16[8,64,768]{2,1,0:T(8,128)(2,1)}, bf16[8,64,768]{2,1,0:T(8,128)(2,1)}, u32[]{:S(2)}, u32[]{:S(2)}) collective-permute-start(bf16[8,64,768]{2,1,0:T(8,128)(2,1)} %slice.345), channel_id=1, source_target_pairs={{0,1},{1,0},{2,3},{3,2},{4,5},{5,4},{6,7},{7,6},{8,9},{9,8},{10,11... | collective-permute-start | bytes 2359304 | tf_op jit(solution)/shard_map/ppermute | solution.py:945
  633.9 37.7 %collective-permute-start.80 = (bf16[192,768]{1,0:T(8,128)(2,1)}, bf16[192,768]{1,0:T(8,128)(2,1)}, u32[]{:S(2)}, u32[]{:S(2)}) collective-permute-start(bf16[192,768]{1,0:T(8,128)(2,1)} %slice.347), channel_id=1, source_target_pairs={{0,1},{1,0},{2,3},{3,2},{4,5},{5,4},{6,7},{7,6},{8,9},{9,8},{10,11... | collective-permute-start | bytes 884744 | tf_op jit(solution)/shard_map/ppermute | solution.py:945
  683.6 44.9 %all-to-all-start.18 = ((bf16[8,88,768]{2,1,0:T(8,128)(2,1)}), bf16[8,88,768]{2,1,0:T(8,128)(2,1)S(1)}, u32[]{:S(2)}, u32[]{:S(2)}) async-start(bf16[8,88,768]{2,1,0:T(8,128)(2,1)} %pad_maximum_fusion.2), calls=%async_computation.18 | async-start | bytes 2162688 | tf_op jit(solution)/shard_map/all_to_all | solution.py:1020
  (144 other events, 1456.6 us)
Sparse Core Ops, SparseCore 0:
  17.4 90.4 all-gather.2
  135.1 84.6 all-gather.4
  654.7 73.7 reduce-scatter.3
